TPU v7x, 32 devices: a whole 2x2x4 slice. The times are simulated.
32 devices in a mesh: dp: 8 (over z, y), expert: 4 (over x, core).
Axes of the slice: x: 2, y: 2, z: 4, core: 2. Of those that a mesh axis runs over, the one named last changes fastest.
Arguments:
- hidden_in: bfloat16 [32768, 768], P(('dp', 'expert')), may hold values from -6 to 6
- gate_prior: float32 [32768, 8], P(('dp', 'expert')), may hold values from -6 to 6
- routes: int32 [32768, 2], P(('dp', 'expert')), may hold values from 0 to 7, all different within a row
- priority: int32 [32, 1024], P(('dp', 'expert')), may hold values from 0 to 1023, each once within a row
- segments: int32 [32, 1024], P(('dp', 'expert')), may hold values from 0 to 5, never falling along the last dimension, each value on 1 to 768 neighbouring positions
- cotangent: bfloat16 [32768, 768], P(('dp', 'expert')), may hold values from -6 to 6
- attend_in: float32 [768, 2304], P(('dp', 'expert')), may hold values from -0.21875 to 0.21875
- first_attend_in: float32 [768, 2304], P(('dp', 'expert')), may hold values from -0.0029296875 to 0.0029296875
- second_attend_in: float32 [768, 2304], P(('dp', 'expert')), may hold values from 1e-08 to 1e-07
- attend_out: float32 [768, 768], P(('dp', 'expert')), may hold values from -1.25 to 1.25
- first_attend_out: float32 [768, 768], P(('dp', 'expert')), may hold values from -0.0029296875 to 0.0029296875
- second_attend_out: float32 [768, 768], P(('dp', 'expert')), may hold values from 1e-08 to 1e-07
- router: float32 [768, 8], P(('dp', 'expert')), may hold values from -0.109375 to 0.109375
- first_router: float32 [768, 8], P(('dp', 'expert')), may hold values from -0.0029296875 to 0.0029296875
- second_router: float32 [768, 8], P(('dp', 'expert')), may hold values from 1e-08 to 1e-07
- gate_mix: float32 [8, 8], replicated, may hold values from -1 to 1
- first_gate_mix: float32 [8, 8], replicated, may hold values from -0.0029296875 to 0.0029296875
- second_gate_mix: float32 [8, 8], replicated, may hold values from 1e-08 to 1e-07
- constants: float32 [768, 6], P(('dp', 'expert')), may hold values from -0.4375 to 0.4375
- first_constants: float32 [768, 6], P(('dp', 'expert')), may hold values from -0.0029296875 to 0.0029296875
- second_constants: float32 [768, 6], P(('dp', 'expert')), may hold values from 1e-08 to 1e-07
- norm_gains: float32 [2, 768], P(None, ('dp', 'expert')), may hold values from 0.5 to 1.5
- first_norm_gains: float32 [2, 768], P(None, ('dp', 'expert')), may hold values from -0.0029296875 to 0.0029296875
- second_norm_gains: float32 [2, 768], P(None, ('dp', 'expert')), may hold values from 1e-08 to 1e-05
- expert_in: float32 [4, 768, 4096], P('expert', 'dp'), may hold values from -0.21875 to 0.21875
- first_expert_in: float32 [4, 768, 4096], P('expert', 'dp'), may hold values from -0.0029296875 to 0.0029296875
- second_expert_in: float32 [4, 768, 4096], P('expert', 'dp'), may hold values from 1e-08 to 1e-07
- expert_out: float32 [4, 2048, 768], P('expert', 'dp'), may hold values from -0.5 to 0.5
- first_expert_out: float32 [4, 2048, 768], P('expert', 'dp'), may hold values from -0.0029296875 to 0.0029296875
- second_expert_out: float32 [4, 2048, 768], P('expert', 'dp'), may hold values from 1e-11 to 1e-08
Outputs:
- activations: bfloat16 [32768, 768], P(('dp', 'expert'))
- input_grad: float32 [32768, 768], P(('dp', 'expert'))
- grad_norm: float32 [], replicated
- grad_attend_in: float32 [768, 2304], P(('dp', 'expert'))
- new_attend_in: float32 [768, 2304], P(('dp', 'expert'))
- new_first_attend_in: float32 [768, 2304], P(('dp', 'expert'))
- new_second_attend_in: float32 [768, 2304], P(('dp', 'expert'))
- copy_attend_in: bfloat16 [768, 2304], P(('dp', 'expert'))
- grad_attend_out: float32 [768, 768], P(('dp', 'expert'))
- new_attend_out: float32 [768, 768], P(('dp', 'expert'))
- new_first_attend_out: float32 [768, 768], P(('dp', 'expert'))
- new_second_attend_out: float32 [768, 768], P(('dp', 'expert'))
- copy_attend_out: bfloat16 [768, 768], P(('dp', 'expert'))
- grad_router: float32 [768, 8], P(('dp', 'expert'))
- new_router: float32 [768, 8], P(('dp', 'expert'))
- new_first_router: float32 [768, 8], P(('dp', 'expert'))
- new_second_router: float32 [768, 8], P(('dp', 'expert'))
- copy_router: bfloat16 [768, 8], P(('dp', 'expert'))
- grad_gate_mix: float32 [8, 8], replicated
- new_gate_mix: float32 [8, 8], replicated
- new_first_gate_mix: float32 [8, 8], replicated
- new_second_gate_mix: float32 [8, 8], replicated
- copy_gate_mix: bfloat16 [8, 8], replicated
- grad_constants: float32 [768, 6], P(('dp', 'expert'))
- new_constants: float32 [768, 6], P(('dp', 'expert'))
- new_first_constants: float32 [768, 6], P(('dp', 'expert'))
- new_second_constants: float32 [768, 6], P(('dp', 'expert'))
- copy_constants: bfloat16 [768, 6], P(('dp', 'expert'))
- grad_norm_gains: float32 [2, 768], P(None, ('dp', 'expert'))
- new_norm_gains: float32 [2, 768], P(None, ('dp', 'expert'))
- new_first_norm_gains: float32 [2, 768], P(None, ('dp', 'expert'))
- new_second_norm_gains: float32 [2, 768], P(None, ('dp', 'expert'))
- copy_norm_gains: bfloat16 [2, 768], P(None, ('dp', 'expert'))
- grad_expert_in: float32 [4, 768, 4096], P('expert', 'dp')
- new_expert_in: float32 [4, 768, 4096], P('expert', 'dp')
- new_first_expert_in: float32 [4, 768, 4096], P('expert', 'dp')
- new_second_expert_in: float32 [4, 768, 4096], P('expert', 'dp')
- copy_expert_in: bfloat16 [4, 768, 4096], P('expert', 'dp')
- grad_expert_out: float32 [4, 2048, 768], P('expert', 'dp')
- new_expert_out: float32 [4, 2048, 768], P('expert', 'dp')
- new_first_expert_out: float32 [4, 2048, 768], P('expert', 'dp')
- new_second_expert_out: float32 [4, 2048, 768], P('expert', 'dp')
- copy_expert_out: bfloat16 [4, 2048, 768], P('expert', 'dp')
Inputs may be any that keep to these rules, and one draw needn't show every extreme that they name: `routes`: each row names 2 different kinds; kinds below 4 are feed-forward experts, 4 the zero expert, 5 the copy expert, the rest constant experts. `priority`: each row is a permutation. `segments`: numbers never fall along a sequence; a document has 1 to 768 tokens.
All inputs are finite; a program needn't handle non-finite values.
Results may differ from a plain program's by a relative error of at most 0.013.
The roundings to bfloat16 on the way count: a program that leaves them out, or rounds other values in their place, can miss the bound.
Values may be sent and summed in bfloat16 or wider, within the bound.
No kernel may reach another device: no remote copies, remote signals or barrier semaphores. Data moves between devices by JAX's collectives and lax.ppermute only.
A program may use at most 320 MiB of HBM per device.

v0:
```python
import functools

import jax
import jax.numpy as jnp
from jax import lax
from jax.experimental import pallas as pl
from jax.experimental.pallas import tpu as pltpu
from jax.sharding import PartitionSpec as P

D = 768
FF = 2048
HEAD_DIM = 64
PAIR = 2 * HEAD_DIM
BLOCK = 256
LANES = 128
TOKENS = {'route': 512, 'mix': 512, 'middle': 512, 'input': 512}
BOTH = ("dp", "expert")

norm_epsilon = 1e-05
adam_epsilon = 1e-08
learn_rates = (0.01, 0.04, 0.01, 0.03, 0.01, 0.1, 0.01, 0.01)
decay_rate = 0.1
beta_moment = 0.5
step_number = 4.0
clip_limit = 1.0
score_scale = 0.125
masked_score = -1e30
highest = lax.Precision.HIGHEST
F32 = jnp.float32
BF16 = jnp.bfloat16

NN = (((1,), (0,)), ((), ()))
NT = (((1,), (1,)), ((), ()))
TN = (((0,), (0,)), ((), ()))

CHOSEN, COEF, SCALE, REST, BETA, GATE_GRAD, PROBS = 0, 2, 3, 4, 8, 16, 32
PIECES = 3
HINT = 64


def dot(left, right, form=NN):
    return lax.dot_general(left, right, form, preferred_element_type=F32)


def iota(shape, dim):
    return lax.broadcasted_iota(jnp.int32, shape, dim)


def row_scale(values):
    return lax.rsqrt(jnp.mean(values * values, axis=-1, keepdims=True) + norm_epsilon)


def params(mebibytes=56):
    return pltpu.CompilerParams(vmem_limit_bytes=mebibytes << 20)


def whole(shape):
    return pl.BlockSpec(shape, lambda *step: (0,) * len(shape))


def cost(flops, moved, transcendentals=0):
    share = HINT
    return pl.CostEstimate(
        flops=flops // share, bytes_accessed=moved // share, transcendentals=transcendentals // share
    )


def project_kernel(hidden_ref, gain_ref, weight_ref, normed_ref, packed_ref):
    @pl.when(pl.program_id(0) == 0)
    def _():
        values = hidden_ref[...].astype(F32)
        normed_ref[...] = (values * row_scale(values) * gain_ref[...]).astype(BF16)

    packed_ref[...] = dot(normed_ref[...], weight_ref[...]).astype(BF16)


def project(hidden, gain, weights):
    tokens = hidden.shape[0]
    return pl.pallas_call(
        project_kernel,
        grid=(3,),
        in_specs=[
            whole((tokens, D)),
            whole((1, D)),
            pl.BlockSpec((D, D), lambda step: (0, step)),
        ],
        out_specs=[whole((tokens, D)), pl.BlockSpec((tokens, D), lambda step: (0, step))],
        out_shape=[
            jax.ShapeDtypeStruct((tokens, D), BF16),
            jax.ShapeDtypeStruct((tokens, 3 * D), BF16),
        ],
        compiler_params=params(),
        cost_estimate=cost(6 * tokens * D * D, 10 * tokens * D + 6 * D * D),
        name="project",
    )(hidden, gain, weights)


def fill_bias(seg_column_ref, seg_row_ref, bias_ref, block):
    length = bias_ref.shape[0]
    for low in range(0, length, block):
        high = low + block
        columns = low + iota((high, block), 1)
        allowed = jnp.logical_and(
            seg_column_ref[:high, :] == seg_row_ref[:, low:high], iota((high, block), 0) <= columns
        )
        bias_ref[:high, low:high] = jnp.where(allowed, 0.0, masked_score)


def attend_forward_kernel(
    query_ref, key_ref, value_ref, seg_column_ref, seg_row_ref, out_ref, logsum_ref, bias_ref
):
    length, block = query_ref.shape[0], BLOCK

    @pl.when(pl.program_id(0) == 0)
    def _():
        fill_bias(seg_column_ref, seg_row_ref, bias_ref, block)

    for low in range(0, length, block):
        high = low + block
        for head in range(2):
            lanes = slice(head * HEAD_DIM, (head + 1) * HEAD_DIM)
            queries = query_ref[low:high, lanes] * score_scale
            scores = dot(key_ref[:high, lanes], queries, NT) + bias_ref[:high, low:high]
            maximum = jnp.max(scores, axis=0, keepdims=True)
            powers = jnp.exp(scores - maximum)
            totals = jnp.sum(powers, axis=0, keepdims=True)
            weights = (powers * (1.0 / totals)).astype(BF16)
            out_ref[low:high, lanes] = dot(weights, value_ref[:high, lanes], TN).astype(BF16)
            logsum_ref[0, head : head + 1, low:high] = maximum + jnp.log(totals)


def attend_forward(packed, seg_column, seg_row):
    length = packed.shape[0]
    pairs = D // PAIR
    return pl.pallas_call(
        attend_forward_kernel,
        grid=(pairs,),
        in_specs=[
            pl.BlockSpec((length, PAIR), lambda pair: (0, pair)),
            pl.BlockSpec((length, PAIR), lambda pair: (0, pairs + pair)),
            pl.BlockSpec((length, PAIR), lambda pair: (0, 2 * pairs + pair)),
            whole((length, 1)),
            whole((1, length)),
        ],
        out_specs=[
            pl.BlockSpec((length, PAIR), lambda pair: (0, pair)),
            pl.BlockSpec((1, 2, length), lambda pair: (pair, 0, 0)),
        ],
        out_shape=[
            jax.ShapeDtypeStruct((length, D), BF16),
            jax.ShapeDtypeStruct((pairs, 2, length), F32),
        ],
        scratch_shapes=[pltpu.VMEM((length, length), F32)],
        compiler_params=params(),
        cost_estimate=cost(8 * length * length * D, 8 * length * D, length * length * 8),
        name="attend_forward",
    )(packed, packed, packed, seg_column, seg_row)


def attend_backward_kernel(
    query_ref,
    key_ref,
    value_ref,
    grad_ref,
    logsum_ref,
    seg_column_ref,
    seg_row_ref,
    out_ref,
    bias_ref,
    key_sum,
    value_sum,
):
    length, block = query_ref.shape[0], BLOCK

    @pl.when(pl.program_id(0) == 0)
    def _():
        fill_bias(seg_column_ref, seg_row_ref, bias_ref, block)

    for low in reversed(range(0, length, block)):
        high = low + block
        for head in range(2):
            lanes = slice(head * HEAD_DIM, (head + 1) * HEAD_DIM)
            queries = query_ref[low:high, lanes] * score_scale
            grads = grad_ref[low:high, lanes]
            keys = key_ref[:high, lanes]
            scores = dot(keys, queries, NT) + bias_ref[:high, low:high]
            weights = jnp.exp(scores - logsum_ref[0, head : head + 1, low:high])
            grad_weights = dot(value_ref[:high, lanes], grads, NT)
            grad_values = dot(weights.astype(BF16), grads)
            centred = jnp.sum(weights * grad_weights, axis=0, keepdims=True)
            grad_raw = (weights * (grad_weights - centred)).astype(BF16)
            grad_keys = dot(grad_raw, queries)
            if high == length:
                key_sum[:, lanes] = grad_keys
                value_sum[:, lanes] = grad_values
            else:
                key_sum[:high, lanes] += grad_keys
                value_sum[:high, lanes] += grad_values
            out_ref[0, low:high, lanes] = dot(keys * score_scale, grad_raw, TN).T.astype(BF16)
    out_ref[1] = key_sum[...].astype(BF16)
    out_ref[2] = value_sum[...].astype(BF16)


def attend_backward(packed, grad, logsum, seg_column, seg_row):
    length = packed.shape[0]
    pairs = D // PAIR
    return pl.pallas_call(
        attend_backward_kernel,
        grid=(pairs,),
        in_specs=[
            pl.BlockSpec((length, PAIR), lambda pair: (0, pair)),
            pl.BlockSpec((length, PAIR), lambda pair: (0, pairs + pair)),
            pl.BlockSpec((length, PAIR), lambda pair: (0, 2 * pairs + pair)),
            pl.BlockSpec((length, PAIR), lambda pair: (0, pair)),
            pl.BlockSpec((1, 2, length), lambda pair: (pair, 0, 0)),
            whole((length, 1)),
            whole((1, length)),
        ],
        out_specs=pl.BlockSpec((3, length, PAIR), lambda pair: (0, 0, pair)),
        out_shape=jax.ShapeDtypeStruct((3, length, D), BF16),
        scratch_shapes=[
            pltpu.VMEM((length, length), F32),
            pltpu.VMEM((length, PAIR), F32),
            pltpu.VMEM((length, PAIR), F32),
        ],
        compiler_params=params(),
        cost_estimate=cost(20 * length * length * D, 14 * length * D, length * length * 8),
        name="attend_backward",
    )(packed, packed, packed, grad, logsum, seg_column, seg_row)


def route_kernel(
    hidden_ref,
    attended_ref,
    upstream_ref,
    extra_ref,
    routes_ref,
    targets_ref,
    gain_ref,
    weight_ref,
    small_ref,
    middle_ref,
    normed_ref,
    table_ref,
    rows_ref,
    normed_all,
    first_all,
    second_all,
    work,
    *,
    token_steps,
    experts,
    constant_count,
    slot_block,
):
    step = pl.program_id(0)
    block = hidden_ref.shape[0]
    kinds = extra_ref.shape[0]
    gate_end = kinds + 2 * constant_count

    @pl.when(step < token_steps)
    def _():
        middle = hidden_ref[...].astype(F32) + dot(attended_ref[...], weight_ref[...])
        scale = row_scale(middle)
        normed = (middle * scale * gain_ref[...]).astype(BF16)
        middle_ref[...] = middle
        normed_ref[...] = normed
        upstream = upstream_ref[...]
        wide = upstream.astype(F32)
        inner = jnp.sum(wide * normed.astype(F32), axis=1, keepdims=True)
        lane = iota((block, LANES), 1)
        small = jnp.where(lane >= gate_end, dot(upstream, small_ref[...]), dot(normed, small_ref[...]))
        small = jnp.where(lane == LANES - 1, inner, jnp.where(lane == LANES - 2, scale, small)).T
        inner = small[LANES - 1 : LANES]
        logits = small[:kinds] + extra_ref[...]
        powers = jnp.exp(logits - jnp.max(logits, axis=0, keepdims=True))
        probs = powers / jnp.sum(powers, axis=0, keepdims=True)
        places = iota((kinds, block), 0)
        work[...] = jnp.zeros_like(work)
        work[PROBS : PROBS + kinds] = probs
        work[SCALE : SCALE + 1] = small[LANES - 2 : LANES - 1]
        shares = []
        for which in range(constant_count):
            left = small[kinds + 2 * which : kinds + 2 * which + 1]
            right = small[kinds + 2 * which + 1 : kinds + 2 * which + 2]
            top = jnp.maximum(left, right)
            left, right = jnp.exp(left - top), jnp.exp(right - top)
            both = left + right
            shares.append((left / both, right / both))
        met = [small[gate_end + which : gate_end + which + 1] for which in range(constant_count)]
        nothing = jnp.zeros((1, block), F32)
        coef = nothing
        betas = [nothing] * constant_count
        amounts = [nothing] * constant_count
        for route in range(2):
            kind = routes_ref[route : route + 1, :]
            chosen = jnp.sum(jnp.where(places == kind, probs, 0.0), axis=0, keepdims=True)
            work[CHOSEN + route : CHOSEN + route + 1] = chosen
            part = jnp.where(kind == experts + 1, 1.0, 0.0)
            rest = nothing
            for which in range(constant_count):
                here = kind == experts + 2 + which
                part = part + jnp.where(here, shares[which][0], 0.0)
                rest = rest + jnp.where(here, shares[which][1] * met[which], 0.0)
                betas[which] = betas[which] + jnp.where(here, chosen * shares[which][1], 0.0)
                amounts[which] = amounts[which] + jnp.where(here, chosen, 0.0)
            coef = coef + chosen * part
            work[REST + route : REST + route + 1] = chosen * (rest + part * inner)
        work[COEF : COEF + 1] = coef
        for which in range(constant_count):
            work[BETA + which : BETA + which + 1] = betas[which]
            grad_left = amounts[which] * inner
            grad_right = amounts[which] * met[which]
            mean = shares[which][0] * grad_left + shares[which][1] * grad_right
            place = GATE_GRAD + 2 * which
            work[place : place + 1] = shares[which][0] * (grad_left - mean)
            work[place + 1 : place + 2] = shares[which][1] * (grad_right - mean)
        table = work[...].T
        table_ref[...] = table
        rows = pl.ds(pl.multiple_of(step * block, block), block)
        normed_all[rows, :] = normed
        for route, kept in enumerate((first_all, second_all)):
            rest = jnp.broadcast_to(table[:, CHOSEN + route : CHOSEN + route + 1], (block, LANES))
            pieces = jnp.zeros((block, LANES), F32)
            for piece in range(PIECES):
                upper = rest.astype(BF16).astype(F32)
                pieces = jnp.where(lane == piece, upper, pieces)
                rest = rest - upper
            kept[rows, :] = pieces.astype(BF16)

    @pl.when(step >= token_steps)
    def _():
        tokens = normed_all.shape[0]
        slots = (step - token_steps) * slot_block + iota((slot_block, tokens), 0)
        first = jnp.where(slots == targets_ref[0:1, :], 1.0, 0.0)
        second = jnp.where(slots == targets_ref[1:2, :], 1.0, 0.0)
        rows_ref[:, :D] = dot((first + second).astype(BF16), normed_all[...]).astype(BF16)
        rows_ref[:, D:] = (
            dot(first.astype(BF16), first_all[...]) + dot(second.astype(BF16), second_all[...])
        ).astype(BF16)


def place_kernel(rows_ref, targets_ref, out_ref):
    slot_block, tokens = out_ref.shape[0], rows_ref.shape[0]
    slots = pl.program_id(0) * slot_block + iota((slot_block, tokens), 0)
    hot = jnp.where(slots == targets_ref[0:1, :], 1.0, 0.0) + jnp.where(
        slots == targets_ref[1:2, :], 1.0, 0.0
    )
    out_ref[...] = dot(hot.astype(BF16), rows_ref[...]).astype(BF16)


def place_rows(rows, targets, slots):
    tokens = rows.shape[0]
    return pl.pallas_call(
        place_kernel,
        grid=(4,),
        in_specs=[whole((tokens, D)), whole((2, tokens))],
        out_specs=pl.BlockSpec((slots // 4, D), lambda step: (step, 0)),
        out_shape=jax.ShapeDtypeStruct((slots, D), BF16),
        compiler_params=params(),
        cost_estimate=cost(2 * tokens * D * slots, 4 * tokens * D),
        name="place_rows",
    )(rows, targets)


def route_tokens(
    hidden, attended, upstream, extra, routes, targets, gain, gathered, experts, constant_count, slots
):
    tokens = hidden.shape[0]
    kinds = extra.shape[0]
    block = TOKENS['route']
    steps = tokens // block
    slot_block = slots // 4
    token_block = lambda width: pl.BlockSpec(
        (block, width), lambda step: (jnp.minimum(step, steps - 1), 0)
    )
    token_lanes = lambda height: pl.BlockSpec(
        (height, block), lambda step: (0, jnp.minimum(step, steps - 1))
    )
    slot_rows = pl.BlockSpec((slot_block, D + LANES), lambda step: (jnp.maximum(step - steps, 0), 0))
    kernel = functools.partial(
        route_kernel,
        token_steps=steps,
        experts=experts,
        constant_count=constant_count,
        slot_block=slot_block,
    )
    return pl.pallas_call(
        kernel,
        grid=(steps + 4,),
        in_specs=[
            token_block(D),
            token_block(D),
            token_block(D),
            token_lanes(kinds),
            token_lanes(2),
            whole((2, tokens)),
            whole((1, D)),
            pl.BlockSpec((D, D), lambda step: (0, 3)),
            pl.BlockSpec((D, LANES), lambda step: (0, 4 * D // LANES)),
        ],
        out_specs=[
            token_block(D),
            token_block(D),
            token_block(LANES),
            slot_rows,
        ],
        out_shape=[
            jax.ShapeDtypeStruct((tokens, D), F32),
            jax.ShapeDtypeStruct((tokens, D), BF16),
            jax.ShapeDtypeStruct((tokens, LANES), F32),
            jax.ShapeDtypeStruct((slots, D + LANES), BF16),
        ],
        scratch_shapes=[
            pltpu.VMEM((tokens, D), BF16),
            pltpu.VMEM((tokens, LANES), BF16),
            pltpu.VMEM((tokens, LANES), BF16),
            pltpu.VMEM((LANES, block), F32),
        ],
        compiler_params=params(),
        cost_estimate=cost(2 * tokens * D * (D + slots), 20 * tokens * D),
        name="route_tokens",
    )(hidden, attended, upstream, extra, routes, targets, gain, gathered, gathered)


def inner_spec(weights, pieces, column):
    if weights.ndim == 2:
        return pl.BlockSpec((D, pieces * BLOCK), lambda step: (0, column(step)))
    shards = weights.shape[0]
    return pl.BlockSpec((shards, pieces * D // shards, BLOCK), lambda step: (0, column(step), 0))


def read_inner(ref):
    if len(ref.shape) == 2:
        return ref[...]
    shards = ref.shape[0]
    rows = D // shards
    pieces = [
        jnp.concatenate([ref[position(shards, k), low : low + rows, :] for k in range(shards)], axis=0)
        for low in range(0, ref.shape[1], rows)
    ]
    return jnp.concatenate(pieces, axis=1)


def outer_specs(weights, pieces):
    if weights.ndim == 2:
        return [pl.BlockSpec((pieces * BLOCK, D), lambda step: (step, 0))]
    shards = weights.shape[0]
    first = weights.shape[1] // BLOCK - D // BLOCK
    even = lambda c: pl.BlockSpec((1, BLOCK, BLOCK), lambda step: (step, first + c, 0))
    odd = lambda c: pl.BlockSpec((1, BLOCK, BLOCK), lambda step: (shards - 1 - step, first + c, 0))
    return [even(c) for c in range(D // BLOCK)] + [odd(c) for c in range(D // BLOCK)]


def read_outer(refs):
    if len(refs) == 1:
        return refs[0][...]
    half = len(refs) // 2
    return jnp.concatenate(
        [jnp.concatenate([ref[0] for ref in some], axis=1) for some in (refs[:half], refs[half:])], axis=0
    )


def expert_kernel(rows_ref, grads_ref, gate_ref, up_ref, *refs, outers):
    outer_refs, refs = refs[:outers], refs[outers:]
    joined_ref, active_ref, produced_ref, met_ref, weighed_ref, total = refs
    step = pl.program_id(0)

    @pl.when(step == 0)
    def _():
        chosen = jnp.sum(rows_ref[:, D:].astype(F32), axis=1, keepdims=True)
        weighed_ref[...] = (chosen * grads_ref[...].astype(F32)).astype(BF16)

    outer = read_outer(outer_refs)
    gates, ups = read_inner(gate_ref), read_inner(up_ref)
    parts = [slice(low, low + BLOCK) for low in range(0, outer.shape[0], BLOCK)]

    def enter(part):
        return (
            dot(rows_ref[:, :D], gates[:, part]),
            dot(rows_ref[:, :D], ups[:, part]),
            dot(weighed_ref[...], outer[part], NT),
        )

    part_total = 0.0
    entered = enter(parts[0])
    for index, part in enumerate(parts):
        gate, up, grad_active = entered
        if index + 1 < len(parts):
            entered = enter(parts[index + 1])
        sigmoid = 1.0 / (1.0 + jnp.exp(-gate))
        silu = gate * sigmoid
        active = (silu * up).astype(BF16)
        active_ref[:, part] = active
        slope = sigmoid * (1.0 + gate * (1.0 - sigmoid))
        joined_ref[0, :, part] = (grad_active * up * slope).astype(BF16)
        joined_ref[1, :, part] = (grad_active * silu).astype(BF16)
        part_total = part_total + dot(active, outer[part])
    total[...] = jnp.where(step == 0, part_total, total[...] + part_total)

    @pl.when(step == pl.num_programs(0) - 1)
    def _():
        produced = total[...].astype(BF16)
        produced_ref[...] = produced
        met = weighed_ref[...].astype(F32) * produced.astype(F32)
        met = sum(met[:, low : low + LANES] for low in range(0, D, LANES))
        met_ref[...] = jnp.sum(met.T, axis=0, keepdims=True)


def expert_forward(rows, grads, inner, outer):
    count = rows.shape[0]
    pieces = 2
    width = pieces * BLOCK
    steps = FF // width
    outers = outer_specs(outer, pieces)
    return pl.pallas_call(
        functools.partial(expert_kernel, outers=len(outers)),
        grid=(steps,),
        in_specs=[
            whole((count, D + LANES)),
            whole((count, D)),
            inner_spec(inner, pieces, lambda step: step),
            inner_spec(inner, pieces, lambda step: steps + step),
            *outers,
        ],
        out_specs=[
            pl.BlockSpec((2, count, width), lambda step: (0, 0, step)),
            pl.BlockSpec((count, width), lambda step: (0, step)),
            whole((count, D)),
            whole((1, count)),
            whole((count, D)),
        ],
        out_shape=[
            jax.ShapeDtypeStruct((2, count, FF), BF16),
            jax.ShapeDtypeStruct((count, FF), BF16),
            jax.ShapeDtypeStruct((count, D), BF16),
            jax.ShapeDtypeStruct((1, count), F32),
            jax.ShapeDtypeStruct((count, D), BF16),
        ],
        scratch_shapes=[pltpu.VMEM((count, D), F32)],
        compiler_params=params(),
        cost_estimate=cost(8 * count * D * FF, 6 * count * FF + 6 * D * FF, count * FF),
        name="expert_forward",
    )(rows, grads, inner, inner, *[outer] * len(outers))


def expert_weights_kernel(rows_ref, weighed_ref, joined_ref, active_ref, inner_ref, outer_ref, turned):
    @pl.when(pl.program_id(0) == 0)
    def _():
        turned[...] = rows_ref[:, :D].T

    shards, _, share, width = inner_ref.shape
    for half in range(2):
        grads = dot(turned[...], joined_ref[half]).astype(BF16)
        for k in range(shards):
            inner_ref[position(shards, k), half] = grads[k * share : (k + 1) * share]
    grads = dot(active_ref[...], weighed_ref[...], TN).astype(BF16)
    outer_ref[...] = grads.reshape(outer_ref.shape)


def expert_weights(rows, weighed, joined, active, shards):
    count = rows.shape[0]
    width = FF // shards
    share = D // shards
    place = lambda step: jnp.where(step < shards // 2, 2 * step, 2 * (shards - 1 - step) + 1)
    lanes = max(width, LANES)
    if lanes != width:
        place = lambda step: step
    steps = FF // lanes
    outer_block = (lanes // width, width, D)
    results = pl.pallas_call(
        expert_weights_kernel,
        grid=(steps,),
        in_specs=[
            whole((count, D + LANES)),
            whole((count, D)),
            pl.BlockSpec((2, count, lanes), lambda step: (0, 0, step)),
            pl.BlockSpec((count, lanes), lambda step: (0, place(step))),
        ],
        out_specs=[
            pl.BlockSpec((shards, 2, share, lanes), lambda step: (0, 0, 0, step)),
            pl.BlockSpec(outer_block, lambda step: (step, 0, 0)),
        ],
        out_shape=[
            jax.ShapeDtypeStruct((shards, 2, share, FF), BF16),
            jax.ShapeDtypeStruct((shards, width, D), BF16),
        ],
        scratch_shapes=[pltpu.VMEM((D, count), BF16)],
        compiler_params=params(),
        cost_estimate=cost(6 * count * D * FF, 6 * count * FF + 6 * D * FF),
        name="expert_weights",
    )(rows, weighed, joined, active)
    inner, outer = results
    if lanes != width:
        outer = jnp.concatenate([outer[k : k + 1] for k in around(shards)], axis=0)
    return inner, outer


def expert_backward_kernel(joined_ref, inner_ref, grads_ref, total):
    step = pl.program_id(0)
    part = dot(joined_ref[0], read_inner(inner_ref), NT)
    total[...] = jnp.where(step == 0, part, total[...] + part)

    @pl.when(step == pl.num_programs(0) - 1)
    def _():
        grads_ref[...] = total[...].astype(BF16)


def expert_backward(joined, inner):
    count = joined.shape[1]
    pieces = 4
    width = pieces * BLOCK
    half = FF // width
    return pl.pallas_call(
        expert_backward_kernel,
        grid=(2 * half,),
        in_specs=[
            pl.BlockSpec((1, count, width), lambda step: (step // half, 0, step % half)),
            inner_spec(inner, pieces, lambda step: step),
        ],
        out_specs=whole((count, D)),
        out_shape=jax.ShapeDtypeStruct((count, D), BF16),
        scratch_shapes=[pltpu.VMEM((count, D), F32)],
        compiler_params=params(),
        cost_estimate=cost(4 * count * D * FF, 4 * count * FF + 4 * D * FF),
        name="expert_backward",
    )(joined, inner)


def mix_kernel(
    returned_ref,
    targets_ref,
    table_ref,
    middle_ref,
    normed_ref,
    small_ref,
    out_ref,
    *,
    value_place,
    constant_count,
):
    block = middle_ref.shape[0]
    slots = returned_ref.shape[0]
    table = table_ref[...]
    columns = iota((block, slots), 1)
    lane = iota((block, LANES), 1)
    blended = normed_ref[...].astype(F32) * table[:, COEF : COEF + 1]
    for route in range(2):
        hot = jnp.where(columns == targets_ref[:, route : route + 1], 1.0, 0.0).astype(BF16)
        paired = dot(hot, returned_ref[...])
        blended = blended + table[:, CHOSEN + route : CHOSEN + route + 1] * paired
    values = jnp.zeros((block, LANES), F32)
    for which in range(constant_count):
        place = BETA + which
        values = jnp.where(lane == value_place + which, table[:, place : place + 1], values)
    upper = values.astype(BF16)
    lower = (values - upper.astype(F32)).astype(BF16)
    blended = blended + (dot(upper, small_ref[...], NT) + dot(lower, small_ref[...], NT))
    out_ref[...] = (middle_ref[...] + blended).astype(BF16)


def mix_branches(returned, targets, table, middle, normed, gathered, value_place, constant_count):
    block = TOKENS["mix"]
    tokens = middle.shape[0]
    slots = returned.shape[0]
    token_block = lambda width: pl.BlockSpec((block, width), lambda step: (step, 0))
    return pl.pallas_call(
        functools.partial(mix_kernel, value_place=value_place, constant_count=constant_count),
        grid=(tokens // block,),
        in_specs=[
            whole((slots, D)),
            token_block(2),
            token_block(LANES),
            token_block(D),
            token_block(D),
            pl.BlockSpec((D, LANES), lambda step: (0, 4 * D // LANES)),
        ],
        out_specs=token_block(D),
        out_shape=jax.ShapeDtypeStruct((tokens, D), BF16),
        compiler_params=params(),
        cost_estimate=cost(4 * tokens * D * slots, 12 * tokens * D),
        name="mix_branches",
    )(returned, targets, table, middle, normed, gathered)


def middle_kernel(
    returned_ref,
    met_ref,
    targets_ref,
    routes_ref,
    prior_ref,
    table_ref,
    middle_ref,
    normed_ref,
    upstream_ref,
    attended_ref,
    small_ref,
    gain_ref,
    weight_ref,
    grad_middle_ref,
    grad_attended_ref,
    grad_weight_ref,
    mixer_ref,
    work,
    grad_gain,
    grad_small,
    grad_weight,
    *,
    experts,
    constant_count,
):
    block = middle_ref.shape[0]
    slots = returned_ref.shape[0]
    kinds = prior_ref.shape[0]
    gates = 2 * constant_count
    first = pl.program_id(0) == 0
    table = table_ref[...]
    wide = upstream_ref[...].astype(F32)
    columns = iota((block, slots), 1)
    hot = jnp.where(columns == targets_ref[:, 0:1], 1.0, 0.0) + jnp.where(
        columns == targets_ref[:, 1:2], 1.0, 0.0
    )
    hot = hot.astype(BF16)
    total = dot(hot, returned_ref[...]) + wide * table[:, COEF : COEF + 1]
    met = met_ref[...]
    upper = met.astype(BF16).astype(F32)
    here = iota((LANES, slots), 1) // (slots // experts) == iota((LANES, slots), 0) % experts
    halves = jnp.where(iota((LANES, slots), 0) < experts, upper, met - upper)
    met = jnp.where(jnp.logical_and(here, iota((LANES, slots), 0) < 2 * experts), halves, 0.0)
    met = dot(hot, met.astype(BF16), NT)
    met = met.T
    turned = table.T
    probs = turned[PROBS : PROBS + kinds]
    places = iota((kinds, block), 0)
    met = met[:experts] + met[experts : 2 * experts]
    work[...] = jnp.zeros_like(work)
    work[:experts] = met
    weighed = work[:kinds]
    for route in range(2):
        rest = turned[REST + route : REST + route + 1]
        weighed = weighed + jnp.where(places == routes_ref[route : route + 1, :], rest, 0.0)
    grad_logits = weighed - probs * jnp.sum(weighed, axis=0, keepdims=True)
    part = lax.dot_general(
        prior_ref[...], grad_logits, NT, precision=highest, preferred_element_type=F32
    )
    mixer_ref[...] = jnp.where(first, part, mixer_ref[...] + part)
    work[:kinds] = grad_logits
    work[kinds : kinds + gates] = turned[GATE_GRAD : GATE_GRAD + gates]
    work[kinds + gates : kinds + gates + constant_count] = turned[BETA : BETA + constant_count]
    values = work[...].T
    upper = values.astype(BF16)
    lower = (values - upper.astype(F32)).astype(BF16)
    is_small = iota((block, LANES), 1) < kinds + gates
    nothing = jnp.zeros((block, LANES), BF16)
    total = total + (
        dot(jnp.where(is_small, upper, nothing), small_ref[...], NT)
        + dot(jnp.where(is_small, lower, nothing), small_ref[...], NT)
    )
    both = jnp.concatenate([upper, lower], axis=1)
    part = jnp.where(
        iota((1, 2 * LANES), 1) % LANES < kinds + gates,
        dot(normed_ref[...], both, TN),
        dot(upstream_ref[...], both, TN),
    )
    part = part[:, :LANES] + part[:, LANES:]
    grad_small[...] = jnp.where(first, part, grad_small[...] + part)

    scale = table[:, SCALE : SCALE + 1]
    unit = middle_ref[...] * scale
    part = jnp.sum(total * unit, axis=0, keepdims=True)
    grad_gain[...] = jnp.where(first, part, grad_gain[...] + part)
    inner = total * gain_ref[...]
    grad_middle = wide + scale * (inner - unit * jnp.mean(inner * unit, axis=1, keepdims=True))
    grad_middle_ref[...] = grad_middle
    rounded = grad_middle.astype(BF16)
    grad_attended_ref[...] = dot(rounded, weight_ref[...], NT).astype(BF16)
    part = dot(attended_ref[...], rounded, TN)
    grad_weight[...] = jnp.where(first, part, grad_weight[...] + part)

    @pl.when(pl.program_id(0) == pl.num_programs(0) - 1)
    def _():
        grad_weight_ref[:, :D] = grad_weight[...].astype(BF16)
        column = jnp.broadcast_to(grad_gain[...], (LANES, D)).T
        place = kinds + gates + constant_count
        grad_weight_ref[:, D:] = jnp.where(
            iota((D, LANES), 1) == place, column, grad_small[...]
        ).astype(BF16)


def middle_backward(
    returned,
    met,
    targets,
    routes,
    prior,
    table,
    middle,
    normed,
    upstream,
    attended,
    gain,
    gathered,
    experts,
    constant_count,
):
    block = TOKENS["middle"]
    tokens = middle.shape[0]
    slots = returned.shape[0]
    kinds = prior.shape[0]
    token_block = lambda width: pl.BlockSpec((block, width), lambda step: (step, 0))
    token_lanes = lambda height: pl.BlockSpec((height, block), lambda step: (0, step))
    return pl.pallas_call(
        functools.partial(middle_kernel, experts=experts, constant_count=constant_count),
        grid=(tokens // block,),
        in_specs=[
            whole((slots, D)),
            whole((1, slots)),
            token_block(2),
            token_lanes(2),
            token_lanes(kinds),
            token_block(LANES),
            token_block(D),
            token_block(D),
            token_block(D),
            token_block(D),
            pl.BlockSpec((D, LANES), lambda step: (0, 4 * D // LANES)),
            whole((1, D)),
            pl.BlockSpec((D, D), lambda step: (0, 3)),
        ],
        out_specs=[token_block(D), token_block(D), whole((D, D + LANES)), whole((kinds, kinds))],
        out_shape=[
            jax.ShapeDtypeStruct((tokens, D), F32),
            jax.ShapeDtypeStruct((tokens, D), BF16),
            jax.ShapeDtypeStruct((D, D + LANES), BF16),
            jax.ShapeDtypeStruct((kinds, kinds), F32),
        ],
        scratch_shapes=[
            pltpu.VMEM((LANES, block), F32),
            pltpu.VMEM((1, D), F32),
            pltpu.VMEM((D, LANES), F32),
            pltpu.VMEM((D, D), F32),
        ],
        compiler_params=params(),
        cost_estimate=cost(2 * tokens * D * (slots + 2 * D), 18 * tokens * D),
        name="middle_backward",
    )(
        returned,
        met,
        targets,
        routes,
        prior,
        table,
        middle,
        normed,
        upstream,
        attended,
        gathered,
        gain,
        gathered,
    )


def project_backward_kernel(normed_ref, packed_ref, out_ref, turned):
    @pl.when(pl.program_id(0) == 0)
    def _():
        turned[...] = normed_ref[...].T

    out_ref[...] = dot(turned[...], packed_ref[0]).astype(BF16)


def project_backward(normed, grad_packed):
    tokens = normed.shape[0]
    return pl.pallas_call(
        project_backward_kernel,
        grid=(3,),
        in_specs=[whole((tokens, D)), pl.BlockSpec((1, tokens, D), lambda step: (step, 0, 0))],
        out_specs=pl.BlockSpec((D, D), lambda step: (0, step)),
        out_shape=jax.ShapeDtypeStruct((D, 3 * D), BF16),
        scratch_shapes=[pltpu.VMEM((D, tokens), BF16)],
        compiler_params=params(),
        cost_estimate=cost(6 * tokens * D * D, 8 * tokens * D + 6 * D * D),
        name="project_backward",
    )(normed, grad_packed)


def input_kernel(packed_ref, weight_ref, hidden_ref, grad_middle_ref, gain_ref, out_ref, grad_gain_ref):
    total = sum(dot(packed_ref[c], weight_ref[:, c * D : (c + 1) * D], NT) for c in range(3))
    values = hidden_ref[...].astype(F32)
    scale = row_scale(values)
    unit = values * scale
    part = jnp.sum(total * unit, axis=0, keepdims=True)
    grad_gain_ref[...] = jnp.where(pl.program_id(0) == 0, part, grad_gain_ref[...] + part)
    inner = total * gain_ref[...]
    out_ref[...] = grad_middle_ref[...] + scale * (
        inner - unit * jnp.mean(inner * unit, axis=1, keepdims=True)
    )


def input_backward(grad_packed, gathered, hidden, grad_middle, gain):
    block = TOKENS['input']
    tokens = hidden.shape[0]
    token_block = lambda width: pl.BlockSpec((block, width), lambda step: (step, 0))
    return pl.pallas_call(
        input_kernel,
        grid=(tokens // block,),
        in_specs=[
            pl.BlockSpec((3, block, D), lambda step: (0, step, 0)),
            pl.BlockSpec((D, 3 * D), lambda step: (0, 0)),
            token_block(D),
            token_block(D),
            whole((1, D)),
        ],
        out_specs=[token_block(D), whole((1, D))],
        out_shape=[
            jax.ShapeDtypeStruct((tokens, D), F32),
            jax.ShapeDtypeStruct((1, D), F32),
        ],
        compiler_params=params(),
        cost_estimate=cost(6 * tokens * D * D, 16 * tokens * D),
        name="input_backward",
    )(grad_packed, gathered, hidden, grad_middle, gain)


def pair_targets(routes, priority, experts, total_kinds, capacity):
    kind_ids = jnp.arange(total_kinds, dtype=jnp.int32)
    hot = [(routes[:, k : k + 1] == kind_ids[None, :]).astype(F32) for k in range(2)]
    earlier = (priority[None, :] < priority[:, None]).astype(BF16)
    before = dot(earlier, (hot[0] + hot[1]).astype(BF16))
    slots = jnp.stack([jnp.sum(before * one, axis=1) for one in hot], axis=1).astype(jnp.int32)
    kept_pairs = jnp.logical_and(routes < experts, slots < capacity)
    return jnp.where(kept_pairs, routes * capacity + slots, experts * capacity)


def exchange(blocks, axis):
    return lax.all_to_all(blocks, axis, split_axis=0, concat_axis=0, tiled=True)


def flip(axis):
    return [(i, i ^ 1) for i in range(lax.axis_size(axis))]


def shift(axis, step):
    count = lax.axis_size(axis)
    return [(i, (i + 2 * step) % count) for i in range(count)]


def gather_far(mine):
    far, depth = lax.axis_size("dp") // 2, lax.axis_index("dp") // 2
    column = jnp.zeros((far, *mine.shape), mine.dtype)
    for step in range(far):
        came = mine if step == 0 else lax.ppermute(mine, "dp", shift("dp", step))
        column = lax.dynamic_update_slice(column, came[None], ((depth - step) % far, 0, 0))
    return column


def gather_all(column):
    far, rows, width = column.shape
    wide, side = lax.axis_size("expert") // 2, lax.axis_index("dp") % 2
    place, core = lax.axis_index("expert") // 2, lax.axis_index("expert") % 2
    near = [column, lax.ppermute(column, "dp", flip("dp"))]
    total = jnp.zeros((far, 2, wide, 2, rows, width), column.dtype)
    for step in range(wide):
        for other in range(2):
            piece = near[other]
            if step:
                piece = lax.ppermute(piece, "expert", shift("expert", step))
            twin = lax.ppermute(piece, "expert", flip("expert"))
            spot = (0, side ^ other, (place - step) % wide)
            shaped = (far, 1, 1, 1, rows, width)
            total = lax.dynamic_update_slice(total, piece.reshape(shaped), (*spot, core, 0, 0))
            total = lax.dynamic_update_slice(total, twin.reshape(shaped), (*spot, 1 - core, 0, 0))
    return total.reshape(-1, width)


def scatter_side(terms):
    width = terms.shape[1]
    count, wide = lax.axis_size("dp"), lax.axis_size("expert") // 2
    rows = terms.shape[0] // (2 * count * wide)
    place, core = lax.axis_index("expert") // 2, lax.axis_index("expert") % 2
    terms = terms.reshape(count, wide, 2, rows, width)
    pick = lambda array, index, axis: lax.dynamic_index_in_dim(array, index, axis, keepdims=False)
    came = lax.ppermute(pick(terms, 1 - core, 2), "expert", flip("expert"))
    pair = (pick(terms, core, 2).astype(F32) + came.astype(F32)).astype(BF16)
    total = pick(pair, place, 1).astype(F32)
    for step in range(1, wide):
        came = lax.ppermute(pick(pair, (place + step) % wide, 1), "expert", shift("expert", step))
        total = total + came.astype(F32)
    return total.astype(BF16)


def around(count):
    return list(range(0, count, 2)) + list(range(count - 1, 0, -2))


def position(count, place):
    return place // 2 if place % 2 == 0 else count - 1 - place // 2


def split_experts(expert_in, expert_out):
    inner, outer = expert_in[0].astype(BF16), expert_out[0].astype(BF16)
    if inner.shape[0] % 16 or outer.shape[0] != BLOCK:
        return [inner, outer]
    pieces = [
        array.reshape(array.shape[0], -1, BLOCK).transpose(1, 0, 2).reshape(-1, BLOCK)
        for array in (inner, outer)
    ]
    return [jnp.concatenate(pieces, axis=0)]


def gather_experts(pieces):
    ring = [around(lax.axis_size("dp"))]
    if len(pieces) == 1:
        both = lax.all_gather(pieces[0], "dp", axis=0, axis_index_groups=ring)
        return both, both
    return [lax.all_gather(piece, "dp", axis=0, tiled=True) for piece in pieces]


def scatter_expert(grads):
    ring = [around(lax.axis_size("dp"))]
    return lax.psum_scatter(grads, "dp", scatter_dimension=0, tiled=True, axis_index_groups=ring)[0]


def own_kernel(
    shares_ref, inner_ref, outer_ref, gain_ref, mixer_ref, own_ref, out_ref, own_outer_ref, few_ref, *, kinds
):
    total = jnp.sum(shares_ref[...].astype(F32), axis=0)
    own_ref[...] = total[:, : 3 * D]
    out_ref[...] = total[:, 3 * D :]
    inner, outer = inner_ref[...].astype(F32), outer_ref[...].astype(F32)
    own_outer_ref[...] = outer
    width = few_ref.shape[2]
    square = jnp.sum(jnp.sum(inner * inner, axis=0), axis=(0, 1), keepdims=True)
    for member in (total, outer):
        square = square + jnp.sum(member * member, axis=(0, 1), keepdims=True)
    few = few_ref.at[0]
    few[...] = jnp.zeros_like(few)
    few[0:1, :D] = gain_ref[...]
    for row in range(kinds):
        place = D + row * kinds
        few[0:1, place : place + kinds] = mixer_ref[row : row + 1, :]
    few[0:1, width - LANES :] = jnp.broadcast_to(square, (1, LANES))
    row = few[...]
    for device in range(1, few_ref.shape[0]):
        few_ref[device] = row


def own_sums(shares, inner, outer, grad_gain, grad_mixer, devices):
    kinds = grad_mixer.shape[0]
    width = D + (-(-kinds * kinds // LANES) + 1) * LANES
    rows = shares.shape[1]
    return pl.pallas_call(
        functools.partial(own_kernel, kinds=kinds),
        out_shape=[
            jax.ShapeDtypeStruct((rows, 3 * D), F32),
            jax.ShapeDtypeStruct((rows, D + LANES), F32),
            jax.ShapeDtypeStruct(outer.shape, F32),
            jax.ShapeDtypeStruct((devices, 1, width), F32),
        ],
        compiler_params=params(),
        cost_estimate=cost(6 * D * FF, 3 * D * FF),
        name="own_sums",
    )(shares, inner, outer, grad_gain, grad_mixer)


def adam(master, first, second, grad, factor, step_rate):
    clipped = grad * factor
    first_new = beta_moment * first + (1.0 - beta_moment) * clipped
    second_new = beta_moment * second + (1.0 - beta_moment) * clipped * clipped
    correct = 1.0 - beta_moment**step_number
    update = (
        first_new / correct / (jnp.sqrt(second_new / correct) + adam_epsilon) + decay_rate * master
    )
    return (master - step_rate * update, first_new, second_new)


def update_kernel(*refs, kinds, constant_count):
    index_ref, few_ref, in_ref, out_ref, inner_ref, outer_ref = refs[:6]
    states = [refs[6 + 3 * which : 9 + 3 * which] for which in range(8)]
    norm_ref, results = refs[30], refs[31:]
    width = out_ref.shape[1]
    few = jnp.sum(few_ref[...], axis=0)
    gain_total = few[:, :D]
    mixer_total = few[:, D : D + kinds * kinds]
    square = (
        few[:, few.shape[1] - 1 :]
        + jnp.sum(gain_total * gain_total, axis=1, keepdims=True)
        + jnp.sum(mixer_total * mixer_total, axis=1, keepdims=True)
    )
    norm = jnp.sqrt(square)
    factor = clip_limit / jnp.maximum(norm, clip_limit)
    places = iter(results)
    slots = [[next(places) for _ in range(4 if which in (0, 7) else 5)] for which in range(8)]

    def step(which, grad):
        master, first, second = states[which]
        outs = slots[which]
        if len(outs) == 5:
            outs[0][...] = grad.reshape(outs[0].shape)
            outs = outs[1:]
        shape = outs[0].shape
        lay = lambda value: value.reshape(grad.shape)
        new = adam(lay(master[...]), lay(first[...]), lay(second[...]), grad, factor, learn_rates[which])
        for ref, value in zip(outs, new + (new[0],)):
            ref[...] = value.reshape(shape).astype(ref.dtype)

    step(6, inner_ref[0].astype(F32))
    step(7, outer_ref[...])

    @pl.when(pl.program_id(0) == 0)
    def _():
        norm_ref[...] = norm
        step(0, in_ref[...])
        step(1, out_ref[:, :D])
        rows = out_ref.shape[0]
        narrow = jnp.pad(out_ref[:, D:], ((0, LANES - rows), (0, 0))).T
        step(2, narrow[:kinds, :rows])
        step(3, jnp.concatenate([mixer_total[:, k * kinds : (k + 1) * kinds] for k in range(kinds)], axis=0))
        small = kinds + 3 * constant_count
        step(4, narrow[kinds:small, :rows])
        start = index_ref[0] * rows
        picked = (iota((D, LANES), 0) == start + iota((D, LANES), 1)).astype(F32)
        own = lax.dot_general(
            jnp.broadcast_to(gain_total, (8, D)), picked, NN, precision=highest, preferred_element_type=F32
        )
        step(5, jnp.concatenate([own[0:1, :rows], narrow[small : small + 1, :rows]], axis=0))


def update(index, few, in_own, out_own, inner_own, outer_own, states, kinds, constant_count):
    steps = 4
    turn = lambda which, array: array.T if which in (2, 4) else array
    states = [[turn(which, array) for array in state] for which, state in enumerate(states)]
    half = steps // 2
    flat = [array for state in states for array in state]

    def spec(shape):
        if len(shape) == 3 and shape[2] == 2 * FF:
            return pl.BlockSpec((1, shape[1], shape[2] // steps), lambda step, index: (0, 0, step))
        if len(shape) == 3:
            return pl.BlockSpec((1, shape[1] // steps, shape[2]), lambda step, index: (0, step, 0))
        return pl.BlockSpec(shape, lambda step, index: (0, 0))

    out_shape = [jax.ShapeDtypeStruct((1, 1), F32)]
    for which in range(8):
        shape = states[which][0].shape
        kept = 3 if which in (0, 7) else 4
        out_shape += [jax.ShapeDtypeStruct(shape, F32)] * kept + [jax.ShapeDtypeStruct(shape, BF16)]
    results = pl.pallas_call(
        functools.partial(update_kernel, kinds=kinds, constant_count=constant_count),
        grid_spec=pltpu.PrefetchScalarGridSpec(
            num_scalar_prefetch=1,
            grid=(steps,),
            in_specs=[
                pl.BlockSpec(few.shape, lambda step, index: (0, 0, 0)),
                spec(in_own.shape),
                spec(out_own.shape),
                pl.BlockSpec(
                    (1, inner_own.shape[1], FF // half), lambda step, index: (step // half, 0, step % half)
                ),
                pl.BlockSpec((outer_own.shape[0] // steps, D), lambda step, index: (step, 0)),
            ]
            + [spec(array.shape) for array in flat],
            out_specs=[spec(leaf.shape) for leaf in out_shape],
        ),
        out_shape=out_shape,
        compiler_params=params(),
        cost_estimate=cost(40 * D * FF, 60 * D * FF // 2),
        name="update",
    )(index, few, in_own, out_own, inner_own, outer_own, *flat)
    norm, rest = results[0].reshape(()), list(results[1:])
    grads = {0: in_own, 7: outer_own[None]}
    ordered = []
    for which in range(8):
        taken = 4 if which in grads else 5
        ordered += [grads[which]] if which in grads else []
        ordered += [turn(which, array) for array in rest[:taken]]
        rest = rest[taken:]
    return norm, ordered


def body(
    hidden_in,
    gate_prior,
    routes,
    priority,
    segments,
    cotangent,
    attend_in,
    first_attend_in,
    second_attend_in,
    attend_out,
    first_attend_out,
    second_attend_out,
    router,
    first_router,
    second_router,
    gate_mix,
    first_gate_mix,
    second_gate_mix,
    constants,
    first_constants,
    second_constants,
    norm_gains,
    first_norm_gains,
    second_norm_gains,
    expert_in,
    first_expert_in,
    second_expert_in,
    expert_out,
    first_expert_out,
    second_expert_out,
):
    groups = lax.axis_size("expert")
    devices = lax.axis_size("dp") * groups
    kinds = gate_prior.shape[1]
    constant_count = constants.shape[1] // 3
    experts = kinds - 2 - constant_count
    token_count = hidden_in.shape[0]
    width_top = routes.shape[1]
    capacity = max(2, width_top * token_count // kinds // 8 * 8)
    slots = experts * capacity
    small_width = kinds + 3 * constant_count
    gate_end = kinds + 2 * constant_count

    expert_pieces = split_experts(expert_in, expert_out)
    mine = jnp.concatenate(
        [
            attend_in,
            attend_out,
            router,
            constants,
            norm_gains.T,
            jnp.zeros((attend_in.shape[0], LANES - small_width - 2), F32),
        ],
        axis=1,
    ).astype(BF16)
    mine, expert_pieces = lax.optimization_barrier((mine, expert_pieces))
    gathered = gather_all(gather_far(mine))
    expert_inner, expert_outer = gather_experts(expert_pieces)
    gains = gathered[:, 4 * D + small_width : 4 * D + small_width + 2].astype(F32).T
    gain_first, gain_second = gains[0:1], gains[1:2]

    targets = pair_targets(routes, priority[0], experts, kinds, capacity)
    target_rows = targets.T
    split = (groups, slots // groups, -1)
    arrived_grad = exchange(place_rows(cotangent, target_rows, slots).reshape(split), "expert")
    arrived_grad = arrived_grad.reshape(slots, D)
    route_rows = routes.T
    prior_rows = gate_prior.T
    extra = jnp.dot(gate_mix.astype(BF16).astype(F32).T, prior_rows, precision=highest)
    seg_row = segments
    seg_column = segments.reshape(token_count, 1)

    normed_first, packed = project(hidden_in, gain_first, gathered)
    attended, logsum = attend_forward(packed, seg_column, seg_row)
    middle, normed_second, table, rows = route_tokens(
        hidden_in,
        attended,
        cotangent,
        extra,
        route_rows,
        target_rows,
        gain_second,
        gathered,
        experts,
        constant_count,
        slots,
    )
    arrived = exchange(rows.reshape(split), "expert").reshape(slots, D + LANES)
    grad_joined, active, produced, met, weighed = expert_forward(
        arrived, arrived_grad, expert_inner, expert_outer
    )
    met = exchange(met.reshape(groups, 1, slots // groups), "expert").reshape(1, slots)
    grad_rows = expert_backward(grad_joined, expert_inner)
    met, grad_rows = lax.optimization_barrier((met, grad_rows))
    grad_returned = exchange(grad_rows.reshape(split), "expert").reshape(slots, D)
    grad_inner, grad_outer = expert_weights(
        arrived, weighed, grad_joined, active, lax.axis_size("dp")
    )
    grad_returned, produced, grad_inner, grad_outer = lax.optimization_barrier(
        (grad_returned, produced, grad_inner, grad_outer)
    )
    inner_own = scatter_expert(grad_inner)
    outer_own = scatter_expert(grad_outer)
    returned = exchange(produced.reshape(split), "expert").reshape(slots, D)
    grad_middle, grad_attended, grad_out_and_small, grad_mixer = middle_backward(
        grad_returned,
        met,
        targets,
        route_rows,
        prior_rows,
        table,
        middle,
        normed_second,
        cotangent,
        attended,
        gain_second,
        gathered,
        experts,
        constant_count,
    )
    out_sum = scatter_side(grad_out_and_small)

    grad_packed = attend_backward(packed, grad_attended, logsum, seg_column, seg_row)
    grad_packed, returned, out_sum = lax.optimization_barrier((grad_packed, returned, out_sum))
    in_sum = scatter_side(project_backward(normed_first, grad_packed))
    shares = exchange(jnp.concatenate([in_sum, out_sum], axis=2), "dp")
    input_grad, grad_gain_first = input_backward(
        grad_packed, gathered, hidden_in, grad_middle, gain_first
    )
    activations = mix_branches(
        returned, targets, table, middle, normed_second, gathered, gate_end, constant_count
    )

    in_own, out_own, outer_own, few = own_sums(
        shares, inner_own, outer_own, grad_gain_first, grad_mixer, devices
    )
    few = exchange(few, BOTH)
    index = lax.axis_index("dp") * groups + lax.axis_index("expert")
    states = (
        (attend_in, first_attend_in, second_attend_in),
        (attend_out, first_attend_out, second_attend_out),
        (router, first_router, second_router),
        (gate_mix, first_gate_mix, second_gate_mix),
        (constants, first_constants, second_constants),
        (norm_gains, first_norm_gains, second_norm_gains),
        (expert_in, first_expert_in, second_expert_in),
        (expert_out, first_expert_out, second_expert_out),
    )
    grad_norm, updated = update(
        index.reshape(1).astype(jnp.int32),
        few,
        in_own,
        out_own,
        inner_own,
        outer_own,
        states,
        kinds,
        constant_count,
    )
    return (activations, input_grad, grad_norm, *updated)


def solution(mesh):
    in_specs = (
        P(("dp", "expert"), None),
        P(("dp", "expert"), None),
        P(("dp", "expert"), None),
        P(("dp", "expert"), None),
        P(("dp", "expert"), None),
        P(("dp", "expert"), None),
        P(("dp", "expert"), None),
        P(("dp", "expert"), None),
        P(("dp", "expert"), None),
        P(("dp", "expert"), None),
        P(("dp", "expert"), None),
        P(("dp", "expert"), None),
        P(("dp", "expert"), None),
        P(("dp", "expert"), None),
        P(("dp", "expert"), None),
        P(),
        P(),
        P(),
        P(("dp", "expert"), None),
        P(("dp", "expert"), None),
        P(("dp", "expert"), None),
        P(None, ("dp", "expert")),
        P(None, ("dp", "expert")),
        P(None, ("dp", "expert")),
        P("expert", "dp", None),
        P("expert", "dp", None),
        P("expert", "dp", None),
        P("expert", "dp", None),
        P("expert", "dp", None),
        P("expert", "dp", None),
    )
    out_specs = (
        P(("dp", "expert"), None),
        P(("dp", "expert"), None),
        P(),
        P(("dp", "expert"), None),
        P(("dp", "expert"), None),
        P(("dp", "expert"), None),
        P(("dp", "expert"), None),
        P(("dp", "expert"), None),
        P(("dp", "expert"), None),
        P(("dp", "expert"), None),
        P(("dp", "expert"), None),
        P(("dp", "expert"), None),
        P(("dp", "expert"), None),
        P(("dp", "expert"), None),
        P(("dp", "expert"), None),
        P(("dp", "expert"), None),
        P(("dp", "expert"), None),
        P(("dp", "expert"), None),
        P(),
        P(),
        P(),
        P(),
        P(),
        P(("dp", "expert"), None),
        P(("dp", "expert"), None),
        P(("dp", "expert"), None),
        P(("dp", "expert"), None),
        P(("dp", "expert"), None),
        P(None, ("dp", "expert")),
        P(None, ("dp", "expert")),
        P(None, ("dp", "expert")),
        P(None, ("dp", "expert")),
        P(None, ("dp", "expert")),
        P("expert", "dp", None),
        P("expert", "dp", None),
        P("expert", "dp", None),
        P("expert", "dp", None),
        P("expert", "dp", None),
        P("expert", "dp", None),
        P("expert", "dp", None),
        P("expert", "dp", None),
        P("expert", "dp", None),
        P("expert", "dp", None),
    )
    return jax.shard_map(body, mesh=mesh, in_specs=in_specs, out_specs=out_specs, check_vma=False)
```

profile of v0, /device:TPU:0, one launch (start us, length us, event | category | flops | bytes accessed | tf_op | source)
XLA Modules:
  0.0 383.4 jit_solution(3571364375403677294)
XLA Ops:
  14.8 5.1 %collective-permute-start.2 = (bf16[24,3200]{1,0:T(8,128)(2,1)S(1)}, bf16[24,3200]{1,0:T(8,128)(2,1)S(1)}, u32[]{:S(2)}, u32[]{:S(2)}) collective-permute-start(bf16[24,3200]{1,0:T(8,128)(2,1)S(1)} %concatenate.10), channel_id=1, source_target_pairs={{0,24},{4,28},{8,0},{12,4},{16,8},{20,12},{24,16},{28,20},{1,25},{... | collective-permute-start | bytes 460808 | tf_op jit(solution)/shard_map/ppermute | solution.py:951
  23.9 4.9 %place_rows.1 = bf16[1024,768]{1,0:T(8,128)(2,1)} custom-call(bf16[1024,768]{1,0:T(8,128)(2,1)} %upstream_ref.3, s32[2,1024]{1,0:T(2,128)} %copy.210.targets_ref), custom_call_target="tpu_custom_call" | custom-call | flops 25165824 | bytes 49152 | tf_op jit(solution)/shard_map/place_rows/pallas_call | solution.py:354
  28.8 3.9 %all-to-all-start.1 = ((bf16[4,256,768]{2,1,0:T(8,128)(2,1)}), bf16[4,256,768]{2,1,0:T(8,128)(2,1)S(1)}, u32[]{:S(2)}, u32[]{:S(2)}) async-start(bf16[4,256,768]{2,1,0:T(8,128)(2,1)} %bitcast.144), calls=%async_computation.1 | async-start | bytes 3145728 | tf_op jit(solution)/shard_map/all_to_all | solution.py:935
  34.8 2.4 collective-permute-done
  40.6 27.0 %collective-permute-done.4 = bf16[4,24,3200]{2,1,0:T(8,128)(2,1)S(1)} collective-permute-done((bf16[4,24,3200]{2,1,0:T(8,128)(2,1)S(1)}, bf16[4,24,3200]{2,1,0:T(8,128)(2,1)S(1)}, u32[]{:S(2)}, u32[]{:S(2)}) %collective-permute-start.4) | collective-permute-done | bytes 614432 | tf_op jit(solution)/shard_map/ppermute | solution.py:960
  68.9 11.9 %collective-permute-done.8 = bf16[4,24,3200]{2,1,0:T(8,128)(2,1)S(1)} collective-permute-done((bf16[4,24,3200]{2,1,0:T(8,128)(2,1)S(1)}, bf16[4,24,3200]{2,1,0:T(8,128)(2,1)S(1)}, u32[]{:S(2)}, u32[]{:S(2)}) %collective-permute-start.8) | collective-permute-done | bytes 614432 | tf_op jit(solution)/shard_map/ppermute | solution.py:966
  82.9 2.2 copy-done
  86.0 8.3 %project.1 = (bf16[1024,768]{1,0:T(8,128)(2,1)}, bf16[1024,2304]{1,0:T(8,128)(2,1)}) custom-call(bf16[1024,768]{1,0:T(8,128)(2,1)} %hidden_ref.5, f32[1,768]{1,0:T(1,128)} %get-tuple-element.202.gain_ref, bf16[768,3200]{1,0:T(8,128)(2,1)} %bitcast.133), custom_call_target="tpu_custom_call" | custom-call | flops 56623104 | bytes 178176 | tf_op jit(solution)/shard_map/project/pallas_call | solution.py:79
  94.3 20.6 %attend_forward.1 = (bf16[1024,768]{1,0:T(8,128)(2,1)}, f32[6,2,1024]{2,1,0:T(2,128)}) custom-call(bf16[1024,2304]{1,0:T(8,128)(2,1)} %get-tuple-element.119.query_ref.key_ref.value_ref, bf16[1024,2304]{1,0:T(8,128)(2,1)} %get-tuple-element.119.query_ref.key_ref.value_ref, bf16[1024,2304]{1,0:T(8,128)(2,1)} %get-tuple-element.119.query_ref.key_ref.value_ref, ...), custom_call_target="tpu_custom_call" | custom-call | flops 100663296 | bytes 98304 | tf_op jit(solution)/shard_map/attend_forward/pallas_call | solution.py:135
  114.8 11.9 %route_tokens.1 = (f32[1024,768]{1,0:T(8,128)}, bf16[1024,768]{1,0:T(8,128)(2,1)}, f32[1024,128]{1,0:T(8,128)}, bf16[1024,896]{1,0:T(8,128)(2,1)}) custom-call(bf16[1024,768]{1,0:T(8,128)(2,1)} %hidden_ref.5, bf16[1024,768]{1,0:T(8,128)(2,1)} %get-tuple-element.120.attended_ref, bf16[1024,768]{1,0:T(8,128)(2,1)} %upstream_ref.3, ...), custom_call_target="tpu_custom_call" | custom-call | flops 44040192 | bytes 245760 | tf_op jit(solution)/shard_map/route_tokens/pallas_call | solution.py:388
  126.7 27.5 %all_to_all.35 = bf16[4,256,896]{2,1,0:T(8,128)(2,1)} all-to-all(bf16[4,256,896]{2,1,0:T(8,128)(2,1)} %bitcast.154), channel_id=1, replica_groups=mesh['dp'=8,'expert'=4] {'expert'}, dimensions={0} | all-to-all | bytes 3670016 | tf_op jit(solution)/shard_map/all_to_all | solution.py:935
  154.3 20.8 %expert_forward.1 = (bf16[2,1024,2048]{2,1,0:T(8,128)(2,1)}, bf16[1024,2048]{1,0:T(8,128)(2,1)}, bf16[1024,768]{1,0:T(8,128)(2,1)}, f32[1,1024]{1,0:T(1,128)}, bf16[1024,768]{1,0:T(8,128)(2,1)}) custom-call(bf16[1024,896]{1,0:T(8,128)(2,1)} %bitcast.140, bf16[1024,768]{1,0:T(8,128)(2,1)} %bitcast.148, bf16[8,2304,256]{2,1,0:T(8,128)(2,1)} %bitcast.123, ...), custom_call_target="tpu_custom_call" | custom-call | flops 201326592 | bytes 344064 | tf_op jit(solution)/shard_map/expert_forward/pallas_call | solution.py:516
  175.1 3.3 all-to-all-start.2
  178.4 11.0 %expert_backward.1 = bf16[1024,768]{1,0:T(8,128)(2,1)} custom-call(bf16[2,1024,2048]{2,1,0:T(8,128)(2,1)} %get-tuple-element.124.joined_ref, bf16[8,2304,256]{2,1,0:T(8,128)(2,1)} %bitcast.131), custom_call_target="tpu_custom_call" | custom-call | flops 100663296 | bytes 229376 | tf_op jit(solution)/shard_map/expert_backward/pallas_call | solution.py:614
  189.3 3.6 all-to-all-start.3
  193.0 15.4 %expert_weights.1 = (bf16[8,2,96,2048]{3,2,1,0:T(8,128)(2,1)}, bf16[8,256,768]{2,1,0:T(8,128)(2,1)}) custom-call(bf16[1024,896]{1,0:T(8,128)(2,1)} %bitcast.141, bf16[1024,768]{1,0:T(8,128)(2,1)} %get-tuple-element.127.weighed_ref, bf16[2,1024,2048]{2,1,0:T(8,128)(2,1)} %get-tuple-element.124.joined_ref, bf16[1024,2048]{1,0:T(8,128)(2,1)} %get-tuple-element.128.active_ref), custom_call_target="tpu_custom_call" | custom-call | flops 150994944 | bytes 344064 | tf_op jit(solution)/shard_map/expert_weights/pallas_call | solution.py:571
  208.4 4.6 %all-to-all-done.3 = bf16[4,256,768]{2,1,0:T(8,128)(2,1)S(1)} async-done(((bf16[4,256,768]{2,1,0:T(8,128)(2,1)}), bf16[4,256,768]{2,1,0:T(8,128)(2,1)S(1)}, u32[]{:S(2)}, u32[]{:S(2)}) %all-to-all-start.3) | async-done | bytes 1572896 | tf_op jit(solution)/shard_map/all_to_all | solution.py:935
  214.1 14.2 %middle_backward.1 = (f32[1024,768]{1,0:T(8,128)}, bf16[1024,768]{1,0:T(8,128)(2,1)}, bf16[768,896]{1,0:T(8,128)(2,1)}, f32[8,8]{1,0:T(8,128)}) custom-call(bf16[1024,768]{1,0:T(8,128)(2,1)} %bitcast.145, f32[1,1024]{1,0:T(1,128)} %bitcast.174, s32[1024,2]{1,0:T(8,128)} %copy-done.1, s32[2,1024]{1,0:T(2,128)} %bitcast.163, f32[8,1024]{1,0:T(8,128)} %bitcast.164, ...), custom_call_target="tpu_custom_call" | custom-call | flops 62914560 | bytes 221184 | tf_op jit(solution)/shard_map/middle_backward/pallas_call | solution.py:812
  230.7 4.0 %all-to-all-start.4 = ((bf16[4,256,768]{2,1,0:T(8,128)(2,1)}), bf16[4,256,768]{2,1,0:T(8,128)(2,1)S(1)}, u32[]{:S(2)}, u32[]{:S(2)}) async-start(bf16[4,256,768]{2,1,0:T(8,128)(2,1)} %bitcast.156), calls=%async_computation.4 | async-start | bytes 3145728 | tf_op jit(solution)/shard_map/all_to_all | solution.py:935
  236.9 2.1 collective-permute-start.11
  238.9 33.2 %attend_backward.1.packed_ref = bf16[3,1024,768]{2,1,0:T(8,128)(2,1)} custom-call(bf16[1024,2304]{1,0:T(8,128)(2,1)} %get-tuple-element.119.query_ref.key_ref.value_ref, bf16[1024,2304]{1,0:T(8,128)(2,1)} %get-tuple-element.119.query_ref.key_ref.value_ref, bf16[1024,2304]{1,0:T(8,128)(2,1)} %get-tuple-element.119.query_ref.key_ref.value_ref, ...), custom_call_target="tpu_custom_call" | custom-call | flops 251658240 | bytes 172032 | tf_op jit(solution)/shard_map/attend_backward/pallas_call | solution.py:207
  272.2 8.7 %project_backward.1 = bf16[768,2304]{1,0:T(8,128)(2,1)} custom-call(bf16[1024,768]{1,0:T(8,128)(2,1)} %get-tuple-element.144.normed_ref, bf16[3,1024,768]{2,1,0:T(8,128)(2,1)} %attend_backward.1.packed_ref), custom_call_target="tpu_custom_call" | custom-call | flops 56623104 | bytes 153600 | tf_op jit(solution)/shard_map/project_backward/pallas_call | solution.py:873
  280.9 2.3 constant_dynamic-slice_fusion.1
  283.4 3.7 collective-permute-done.12
  287.8 21.5 %collective-permute-done.13 = bf16[8,24,2304]{2,1,0:T(8,128)(2,1)S(1)} collective-permute-done((bf16[8,24,2304]{2,1,0:T(8,128)(2,1)S(1)}, bf16[8,24,2304]{2,1,0:T(8,128)(2,1)S(1)}, u32[]{:S(2)}, u32[]{:S(2)}) %collective-permute-start.13) | collective-permute-done | bytes 884768 | tf_op jit(solution)/shard_map/ppermute | solution.py:986
  310.7 5.8 %all-to-all-start.5 = ((bf16[8,24,3200]{2,1,0:T(8,128)(2,1)}), bf16[8,24,3200]{2,1,0:T(8,128)(2,1)S(1)}, u32[]{:S(2)}, u32[]{:S(2)}) async-start(bf16[8,24,3200]{2,1,0:T(8,128)(2,1)} %pad_maximum_fusion), calls=%async_computation.5 | async-start | bytes 2457600 | tf_op jit(solution)/shard_map/all_to_all | solution.py:935
  316.5 9.6 %input_backward.1 = (f32[1024,768]{1,0:T(8,128)}, f32[1,768]{1,0:T(1,128)}) custom-call(bf16[3,1024,768]{2,1,0:T(8,128)(2,1)} %attend_backward.1.packed_ref, bf16[768,3200]{1,0:T(8,128)(2,1)} %bitcast.138, bf16[1024,768]{1,0:T(8,128)(2,1)} %hidden_ref.5, f32[1024,768]{1,0:T(8,128)} %get-tuple-element.142.grad_middle_ref, f32[1,768]{1,0:T(1,128)} %get-tuple-element.202.gain_ref), custom_call_target="tpu_custom_call" | custom-call | flops 56623104 | bytes 196608 | tf_op jit(solution)/shard_map/input_backward/pallas_call | solution.py:903
  326.1 22.3 %all-to-all-done.5.shares_ref = bf16[8,24,3200]{2,1,0:T(8,128)(2,1)S(1)} async-done(((bf16[8,24,3200]{2,1,0:T(8,128)(2,1)}), bf16[8,24,3200]{2,1,0:T(8,128)(2,1)S(1)}, u32[]{:S(2)}, u32[]{:S(2)}) %all-to-all-start.5) | async-done | bytes 1228832 | tf_op jit(solution)/shard_map/all_to_all | solution.py:935
  349.4 3.2 own_sums.1
  352.6 3.8 all-to-all-start.6
  356.4 7.9 %mix_branches.1 = bf16[1024,768]{1,0:T(8,128)(2,1)} custom-call(bf16[1024,768]{1,0:T(8,128)(2,1)} %bitcast.147, s32[1024,2]{1,0:T(8,128)} %copy-done.1, f32[1024,128]{1,0:T(8,128)} %get-tuple-element.133.table_ref, f32[1024,768]{1,0:T(8,128)} %get-tuple-element.134.middle_ref, bf16[1024,768]{1,0:T(8,128)(2,1)} %get-tuple-element.135.normed_ref, ...), custom_call_target="tpu_custom_call" | custom-call | flops 50331648 | bytes 147456 | tf_op jit(solution)/shard_map/mix_branches/pallas_call | solution.py:667
  365.3 11.3 %update.1 = (f32[1,1]{1,0:T(1,128)}, f32[24,2304]{1,0:T(8,128)}, f32[24,2304]{1,0:T(8,128)}, f32[24,2304]{1,0:T(8,128)}, bf16[24,2304]{1,0:T(8,128)(2,1)}, /*ind...) custom-call(s32[1]{0:T(128)} %bitcast.53.refs_0_, ...), custom_call_target="tpu_custom_call" | custom-call | flops 983040 | bytes 737280 | tf_op jit(solution)/shard_map/update/pallas_call | solution.py:1147
  (120 shorter events, 30.9 us)
Async XLA Ops:
  7.2 5.8 %copy-start.3 = (f32[1,96,4096]{2,1,0:T(8,128)S(1)}, f32[1,96,4096]{2,1,0:T(8,128)}, u32[]{:S(2)}) copy-start(f32[1,96,4096]{2,1,0:T(8,128)} %refs_24_.1) | copy-start | bytes 4718596
  7.2 147.0 %all-gather.3.cloned.1.call-start = ((), (), s32[]{:S(2)}) async-start(), calls=%async_computation.11 | async-start | bytes 10616832 | tf_op jit(solution)/shard_map/all_gather | solution.py:1013
  13.6 7.4 %copy-start.9 = (s32[1024,2]{0,1:T(2,128)S(1)}, s32[1024,2]{0,1:T(2,128)}, u32[]{:S(2)}) copy-start(s32[1024,2]{0,1:T(2,128)} %param.32) | copy-start | bytes 24580
  13.6 7.4 %copy-start.14 = (s32[1,1024]{1,0:T(1,128)S(1)}, s32[1,1024]{1,0:T(1,128)}, u32[]{:S(2)}) copy-start(s32[1,1024]{1,0:T(1,128)} %param.33) | copy-start | bytes 12292
  14.8 22.4 %collective-permute-start.2 = (bf16[24,3200]{1,0:T(8,128)(2,1)S(1)}, bf16[24,3200]{1,0:T(8,128)(2,1)S(1)}, u32[]{:S(2)}, u32[]{:S(2)}) collective-permute-start(bf16[24,3200]{1,0:T(8,128)(2,1)S(1)} %concatenate.10), channel_id=1, source_target_pairs={{0,24},{4,28},{8,0},{12,4},{16,8},{20,12},{24,16},{28,20},{1,25},{... | collective-permute-start | bytes 460808 | tf_op jit(solution)/shard_map/ppermute | solution.py:951
  19.9 17.3 %collective-permute-start.1 = (bf16[24,3200]{1,0:T(8,128)(2,1)S(1)}, bf16[24,3200]{1,0:T(8,128)(2,1)S(1)}, u32[]{:S(2)}, u32[]{:S(2)}) collective-permute-start(bf16[24,3200]{1,0:T(8,128)(2,1)S(1)} %concatenate.10), channel_id=1, source_target_pairs={{0,16},{4,20},{8,24},{12,28},{16,0},{20,4},{24,8},{28,12},{1,17},{... | collective-permute-start | bytes 460808 | tf_op jit(solution)/shard_map/ppermute | solution.py:951
  19.9 17.3 %collective-permute-start = (bf16[24,3200]{1,0:T(8,128)(2,1)S(1)}, bf16[24,3200]{1,0:T(8,128)(2,1)S(1)}, u32[]{:S(2)}, u32[]{:S(2)}) collective-permute-start(bf16[24,3200]{1,0:T(8,128)(2,1)S(1)} %concatenate.10), channel_id=1, source_target_pairs={{0,8},{4,12},{8,16},{12,20},{16,24},{20,28},{24,0},{28,4},{1,9},{5... | collective-permute-start | bytes 460808 | tf_op jit(solution)/shard_map/ppermute | solution.py:951
  23.1 5.7 %copy-start.1 = (s32[1024,2]{1,0:T(8,128)}, s32[1024,2]{1,0:T(8,128)S(1)}, u32[]{:S(2)}) copy-start(s32[1024,2]{1,0:T(8,128)S(1)} %add_select_fusion.targets_ref) | copy-start | bytes 24580
  28.8 5.2 %copy-start.10 = (f32[1024,8]{0,1:T(8,128)S(1)}, f32[1024,8]{0,1:T(8,128)}, u32[]{:S(2)}) copy-start(f32[1024,8]{0,1:T(8,128)} %param.31) | copy-start | bytes 98308
  28.8 5.2 %copy-start.12 = (f32[8,8]{1,0:T(8,128)S(1)}, f32[8,8]{1,0:T(8,128)}, u32[]{:S(2)}) copy-start(f32[8,8]{1,0:T(8,128)} %refs_15_.1) | copy-start | bytes 772
  28.8 98.0 %all-to-all-start.1 = ((bf16[4,256,768]{2,1,0:T(8,128)(2,1)}), bf16[4,256,768]{2,1,0:T(8,128)(2,1)S(1)}, u32[]{:S(2)}, u32[]{:S(2)}) async-start(bf16[4,256,768]{2,1,0:T(8,128)(2,1)} %bitcast.144), calls=%async_computation.1 | async-start | bytes 3145728 | tf_op jit(solution)/shard_map/all_to_all | solution.py:935
  37.3 30.9 %collective-permute-start.6 = (bf16[4,24,3200]{2,1,0:T(8,128)(2,1)S(1)}, bf16[4,24,3200]{2,1,0:T(8,128)(2,1)S(1)}, u32[]{:S(2)}, u32[]{:S(2)}) collective-permute-start(bf16[4,24,3200]{2,1,0:T(8,128)(2,1)S(1)} %bitcast_dynamic-update-slice_fusion.8), channel_id=1, source_target_pairs={{0,2},{1,3},{2,0},{3,1},{4,6},{5,7},{6,4},{7,5},{8,10},{9,11},{10,... | collective-permute-start | bytes 1843208 | tf_op jit(solution)/shard_map/ppermute | solution.py:966
  38.6 28.9 %collective-permute-start.4 = (bf16[4,24,3200]{2,1,0:T(8,128)(2,1)S(1)}, bf16[4,24,3200]{2,1,0:T(8,128)(2,1)S(1)}, u32[]{:S(2)}, u32[]{:S(2)}) collective-permute-start(bf16[4,24,3200]{2,1,0:T(8,128)(2,1)S(1)} %bitcast_dynamic-update-slice_fusion.8), channel_id=1, source_target_pairs={{0,4},{4,0},{8,12},{12,8},{16,20},{20,16},{24,28},{28,24},{1,5},{5... | collective-permute-start | bytes 1843208 | tf_op jit(solution)/shard_map/ppermute | solution.py:960
  40.2 28.5 %collective-permute-start.3 = (bf16[4,24,3200]{2,1,0:T(8,128)(2,1)S(1)}, bf16[4,24,3200]{2,1,0:T(8,128)(2,1)S(1)}, u32[]{:S(2)}, u32[]{:S(2)}) collective-permute-start(bf16[4,24,3200]{2,1,0:T(8,128)(2,1)S(1)} %bitcast_dynamic-update-slice_fusion.8), channel_id=1, source_target_pairs={{0,1},{1,0},{2,3},{3,2},{4,5},{5,4},{6,7},{7,6},{8,9},{9,8},{10,11... | collective-permute-start | bytes 1843208 | tf_op jit(solution)/shard_map/ppermute | solution.py:967
  67.6 13.2 %collective-permute-start.8 = (bf16[4,24,3200]{2,1,0:T(8,128)(2,1)S(1)}, bf16[4,24,3200]{2,1,0:T(8,128)(2,1)S(1)}, u32[]{:S(2)}, u32[]{:S(2)}) collective-permute-start(bf16[4,24,3200]{2,1,0:T(8,128)(2,1)S(1)} %collective-permute-done.4), channel_id=1, source_target_pairs={{0,2},{1,3},{2,0},{3,1},{4,6},{5,7},{6,4},{7,5},{8,10},{9,11},{10,... | collective-permute-start | bytes 1843208 | tf_op jit(solution)/shard_map/ppermute | solution.py:966
  68.2 12.6 %collective-permute-start.5 = (bf16[4,24,3200]{2,1,0:T(8,128)(2,1)S(1)}, bf16[4,24,3200]{2,1,0:T(8,128)(2,1)S(1)}, u32[]{:S(2)}, u32[]{:S(2)}) collective-permute-start(bf16[4,24,3200]{2,1,0:T(8,128)(2,1)S(1)} %collective-permute-done.4), channel_id=1, source_target_pairs={{0,1},{1,0},{2,3},{3,2},{4,5},{5,4},{6,7},{7,6},{8,9},{9,8},{10,11... | collective-permute-start | bytes 1843208 | tf_op jit(solution)/shard_map/ppermute | solution.py:967
  68.2 12.7 %collective-permute-start.7 = (bf16[4,24,3200]{2,1,0:T(8,128)(2,1)S(1)}, bf16[4,24,3200]{2,1,0:T(8,128)(2,1)S(1)}, u32[]{:S(2)}, u32[]{:S(2)}) collective-permute-start(bf16[4,24,3200]{2,1,0:T(8,128)(2,1)S(1)} %collective-permute-done.6), channel_id=1, source_target_pairs={{0,1},{1,0},{2,3},{3,2},{4,5},{5,4},{6,7},{7,6},{8,9},{9,8},{10,11... | collective-permute-start | bytes 1843208 | tf_op jit(solution)/shard_map/ppermute | solution.py:967
  80.8 2.0 collective-permute-start.9
  126.7 27.5 %copy-start.5 = (bf16[4,256,768]{2,1,0:T(8,128)(2,1)}, bf16[4,256,768]{2,1,0:T(8,128)(2,1)S(1)}, u32[]{:S(2)}) copy-start(bf16[4,256,768]{2,1,0:T(8,128)(2,1)S(1)} %all-to-all-done.1) | copy-start | bytes 4718596
  175.1 14.2 %all-to-all-start.2 = ((f32[4,1,256]{2,1,0:T(1,128)}), f32[4,1,256]{2,1,0:T(1,128)S(1)}, u32[]{:S(2)}, u32[]{:S(2)}) async-start(f32[4,1,256]{2,1,0:T(1,128)} %bitcast.179), calls=%async_computation.2 | async-start | bytes 8192 | tf_op jit(solution)/shard_map/all_to_all | solution.py:935
  189.3 19.0 %copy-start.13 = (f32[4,1,256]{2,1,0:T(1,128)}, f32[4,1,256]{2,1,0:T(1,128)S(1)}, u32[]{:S(2)}) copy-start(f32[4,1,256]{2,1,0:T(1,128)S(1)} %all-to-all-done.2) | copy-start | bytes 12292
  189.3 23.6 %all-to-all-start.3 = ((bf16[4,256,768]{2,1,0:T(8,128)(2,1)}), bf16[4,256,768]{2,1,0:T(8,128)(2,1)S(1)}, u32[]{:S(2)}, u32[]{:S(2)}) async-start(bf16[4,256,768]{2,1,0:T(8,128)(2,1)} %bitcast.146), calls=%async_computation.3 | async-start | bytes 3145728 | tf_op jit(solution)/shard_map/all_to_all | solution.py:935
  192.9 155.5 %reduce-scatter.5.cloned.1.call-start = ((), (), s32[]{:S(2)}) async-start(), calls=%async_computation.10 | async-start | bytes 3538944 | tf_op jit(solution)/shard_map/reduce_scatter | solution.py:1020
  213.0 135.4 %reduce-scatter.3.cloned.1.call-start = ((), (), s32[]{:S(2)}) async-start(), calls=%async_computation.9 | async-start | bytes 7077888 | tf_op jit(solution)/shard_map/reduce_scatter | solution.py:1020
  230.7 4.0 %collective-permute-start.10 = (bf16[8,2,24,896]{3,2,0,1:T(8,128)(2,1)}, bf16[8,2,24,896]{3,2,0,1:T(8,128)(2,1)S(1)}, u32[]{:S(2)}, u32[]{:S(2)}) collective-permute-start(bf16[8,2,24,896]{3,2,0,1:T(8,128)(2,1)} %bitcast.122), channel_id=1, source_target_pairs={{0,1},{1,0},{2,3},{3,2},{4,5},{5,4},{6,7},{7,6},{8,9},{9,8},{10,11... | collective-permute-start | bytes 2064392 | tf_op jit(solution)/shard_map/ppermute | solution.py:982
  230.7 41.5 %all-to-all-start.4 = ((bf16[4,256,768]{2,1,0:T(8,128)(2,1)}), bf16[4,256,768]{2,1,0:T(8,128)(2,1)S(1)}, u32[]{:S(2)}, u32[]{:S(2)}) async-start(bf16[4,256,768]{2,1,0:T(8,128)(2,1)} %bitcast.156), calls=%async_computation.4 | async-start | bytes 3145728 | tf_op jit(solution)/shard_map/all_to_all | solution.py:935
  236.9 35.3 %collective-permute-start.11 = (bf16[8,24,896]{2,1,0:T(8,128)(2,1)S(1)}, bf16[8,24,896]{2,1,0:T(8,128)(2,1)S(1)}, u32[]{:S(2)}, u32[]{:S(2)}) collective-permute-start(bf16[8,24,896]{2,1,0:T(8,128)(2,1)S(1)} %dynamic-slice_bitcast_fusion.1), channel_id=1, source_target_pairs={{0,2},{1,3},{2,0},{3,1},{4,6},{5,7},{6,4},{7,5},{8,10},{9,11},{10,... | collective-permute-start | bytes 1032200 | tf_op jit(solution)/shard_map/ppermute | solution.py:986
  272.2 8.7 %copy-start.4 = (bf16[4,256,768]{2,1,0:T(8,128)(2,1)}, bf16[4,256,768]{2,1,0:T(8,128)(2,1)S(1)}, u32[]{:S(2)}) copy-start(bf16[4,256,768]{2,1,0:T(8,128)(2,1)S(1)} %all-to-all-done.4) | copy-start | bytes 4718596
  283.3 3.8 collective-permute-start.12
  287.6 21.8 %collective-permute-start.13 = (bf16[8,24,2304]{2,1,0:T(8,128)(2,1)S(1)}, bf16[8,24,2304]{2,1,0:T(8,128)(2,1)S(1)}, u32[]{:S(2)}, u32[]{:S(2)}) collective-permute-start(bf16[8,24,2304]{2,1,0:T(8,128)(2,1)S(1)} %dynamic-slice_bitcast_fusion), channel_id=1, source_target_pairs={{0,2},{1,3},{2,0},{3,1},{4,6},{5,7},{6,4},{7,5},{8,10},{9,11},{10,... | collective-permute-start | bytes 2654216 | tf_op jit(solution)/shard_map/ppermute | solution.py:986
  310.7 37.7 %all-to-all-start.5 = ((bf16[8,24,3200]{2,1,0:T(8,128)(2,1)}), bf16[8,24,3200]{2,1,0:T(8,128)(2,1)S(1)}, u32[]{:S(2)}, u32[]{:S(2)}) async-start(bf16[8,24,3200]{2,1,0:T(8,128)(2,1)} %pad_maximum_fusion), calls=%async_computation.5 | async-start | bytes 2457600 | tf_op jit(solution)/shard_map/all_to_all | solution.py:935
  352.6 12.0 %all-to-all-start.6 = ((f32[32,1,1024]{2,1,0:T(1,128)}), f32[32,1,1024]{2,1,0:T(1,128)S(1)}, u32[]{:S(2)}, u32[]{:S(2)}) async-start(f32[32,1,1024]{2,1,0:T(1,128)} %get-tuple-element.150), calls=%async_computation.8 | async-start | bytes 262144 | tf_op jit(solution)/shard_map/all_to_all | solution.py:935
  (6 other events, 10.0 us)
Sparse Core Ops, SparseCore 0:
  15.0 112.9 all-gather.2
  213.1 38.8 reduce-scatter.4
  254.3 71.2 reduce-scatter.2
where the time goes:
time: 388 us; the launch traced here: 383 us
  Pallas kernels  181 us (47%)
  waiting for transfers between devices  96.1 us (25%)
  starting transfers between devices  36.8 us (9%)
  blocking collectives  27.5 us (7%)
  local copies, waits for them, and re-layouts  17 us (4%)
  between operations  14.7 us (4%)
  other arithmetic  8.65 us (2%)
    pallas_call x1, Pallas kernels, attend_backward(): pl.pallas_call(attend_backward_kernel, grid=(pairs,), in_specs=[pl.BlockS...  33.2 us
    all_to_all x1, blocking collectives, exchange(): return lax.all_to_all(blocks, axis, split_axis=0, concat_axis=0, tiled=True)  27.5 us
    all_to_all x6, waiting for transfers between devices, exchange(): return lax.all_to_all(blocks, axis, split_axis=0, concat_axis=0, tiled=True)  27.2 us
    ppermute x1, waiting for transfers between devices, gather_all(): near = [column, lax.ppermute(column, 'dp', flip('dp'))]  27 us
    all_to_all x6, starting transfers between devices, exchange(): return lax.all_to_all(blocks, axis, split_axis=0, concat_axis=0, tiled=True)  24.2 us
    ppermute x2, waiting for transfers between devices, scatter_side(): lax.ppermute(pick(pair, (place + step) % wide, 1), 'expert', shift('exper...  21.5 us
    pallas_call x1, Pallas kernels, expert_forward(): pl.pallas_call(functools.partial(expert_kernel, outers=len(outers)), grid...  20.8 us
    pallas_call x1, Pallas kernels, attend_forward(): pl.pallas_call(attend_forward_kernel, grid=(pairs,), in_specs=[pl.BlockSp...  20.6 us
  transfers between devices with their start and end apart: 23, of which 9 were waited for; matrix products, arithmetic and copies ran while one was open for 4% of the time, Pallas kernels for 38%

commit v1 on v0

--- a/solution.py
+++ b/solution.py
@@ -36,6 +36,7 @@
 CHOSEN, COEF, SCALE, REST, BETA, GATE_GRAD, PROBS = 0, 2, 3, 4, 8, 16, 32
 PIECES = 3
 HINT = 64
+UPDATE_STEPS = 4
 
 
 def dot(left, right, form=NN):
@@ -63,36 +64,6 @@
     return pl.CostEstimate(
         flops=flops // share, bytes_accessed=moved // share, transcendentals=transcendentals // share
     )
-
-
-def project_kernel(hidden_ref, gain_ref, weight_ref, normed_ref, packed_ref):
-    @pl.when(pl.program_id(0) == 0)
-    def _():
-        values = hidden_ref[...].astype(F32)
-        normed_ref[...] = (values * row_scale(values) * gain_ref[...]).astype(BF16)
-
-    packed_ref[...] = dot(normed_ref[...], weight_ref[...]).astype(BF16)
-
-
-def project(hidden, gain, weights):
-    tokens = hidden.shape[0]
-    return pl.pallas_call(
-        project_kernel,
-        grid=(3,),
-        in_specs=[
-            whole((tokens, D)),
-            whole((1, D)),
-            pl.BlockSpec((D, D), lambda step: (0, step)),
-        ],
-        out_specs=[whole((tokens, D)), pl.BlockSpec((tokens, D), lambda step: (0, step))],
-        out_shape=[
-            jax.ShapeDtypeStruct((tokens, D), BF16),
-            jax.ShapeDtypeStruct((tokens, 3 * D), BF16),
-        ],
-        compiler_params=params(),
-        cost_estimate=cost(6 * tokens * D * D, 10 * tokens * D + 6 * D * D),
-        name="project",
-    )(hidden, gain, weights)
 
 
 def fill_bias(seg_column_ref, seg_row_ref, bias_ref, block):
@@ -107,46 +78,69 @@
 
 
 def attend_forward_kernel(
-    query_ref, key_ref, value_ref, seg_column_ref, seg_row_ref, out_ref, logsum_ref, bias_ref
+    hidden_ref,
+    gain_ref,
+    query_weight_ref,
+    key_weight_ref,
+    value_weight_ref,
+    seg_column_ref,
+    seg_row_ref,
+    normed_ref,
+    packed_ref,
+    out_ref,
+    logsum_ref,
+    bias_ref,
 ):
-    length, block = query_ref.shape[0], BLOCK
+    length, block = hidden_ref.shape[0], BLOCK
 
     @pl.when(pl.program_id(0) == 0)
     def _():
         fill_bias(seg_column_ref, seg_row_ref, bias_ref, block)
-
+        values = hidden_ref[...].astype(F32)
+        normed_ref[...] = (values * row_scale(values) * gain_ref[...]).astype(BF16)
+
+    weights = jnp.concatenate([query_weight_ref[...], key_weight_ref[...], value_weight_ref[...]], axis=1)
+    packed = dot(normed_ref[...], weights).astype(BF16)
+    for part in range(3):
+        packed_ref[part] = packed[:, part * PAIR : (part + 1) * PAIR]
     for low in range(0, length, block):
         high = low + block
         for head in range(2):
             lanes = slice(head * HEAD_DIM, (head + 1) * HEAD_DIM)
-            queries = query_ref[low:high, lanes] * score_scale
-            scores = dot(key_ref[:high, lanes], queries, NT) + bias_ref[:high, low:high]
+            queries = packed_ref[0, low:high, lanes] * score_scale
+            scores = dot(packed_ref[1, :high, lanes], queries, NT) + bias_ref[:high, low:high]
             maximum = jnp.max(scores, axis=0, keepdims=True)
             powers = jnp.exp(scores - maximum)
             totals = jnp.sum(powers, axis=0, keepdims=True)
-            weights = (powers * (1.0 / totals)).astype(BF16)
-            out_ref[low:high, lanes] = dot(weights, value_ref[:high, lanes], TN).astype(BF16)
+            chances = (powers * (1.0 / totals)).astype(BF16)
+            out_ref[low:high, lanes] = dot(chances, packed_ref[2, :high, lanes], TN).astype(BF16)
             logsum_ref[0, head : head + 1, low:high] = maximum + jnp.log(totals)
 
 
-def attend_forward(packed, seg_column, seg_row):
-    length = packed.shape[0]
+def attend_forward(hidden, gain, gathered, seg_column, seg_row):
+    length = hidden.shape[0]
     pairs = D // PAIR
     return pl.pallas_call(
         attend_forward_kernel,
         grid=(pairs,),
         in_specs=[
-            pl.BlockSpec((length, PAIR), lambda pair: (0, pair)),
-            pl.BlockSpec((length, PAIR), lambda pair: (0, pairs + pair)),
-            pl.BlockSpec((length, PAIR), lambda pair: (0, 2 * pairs + pair)),
+            whole((length, D)),
+            whole((1, D)),
+            pl.BlockSpec((D, PAIR), lambda pair: (0, pair)),
+            pl.BlockSpec((D, PAIR), lambda pair: (0, pairs + pair)),
+            pl.BlockSpec((D, PAIR), lambda pair: (0, 2 * pairs + pair)),
             whole((length, 1)),
             whole((1, length)),
         ],
         out_specs=[
+            whole((length, D)),
+            pl.BlockSpec((3, length, PAIR), lambda pair: (0, 0, pair)),
             pl.BlockSpec((length, PAIR), lambda pair: (0, pair)),
             pl.BlockSpec((1, 2, length), lambda pair: (pair, 0, 0)),
         ],
         out_shape=[
+            jax.ShapeDtypeStruct((length, D), BF16),
+            jax.ShapeDtypeStruct((3, length, D), BF16),
             jax.ShapeDtypeStruct((length, D), BF16),
             jax.ShapeDtypeStruct((pairs, 2, length), F32),
         ],
@@ -154,10 +148,19 @@
         compiler_params=params(),
         cost_estimate=cost(8 * length * length * D, 8 * length * D, length * length * 8),
         name="attend_forward",
-    )(packed, packed, packed, seg_column, seg_row)
+    )(hidden, gain, gathered, gathered, gathered, seg_column, seg_row)
+
+
+def part_rows(total, core, send_ref, keep_ref):
+    rows = send_ref.shape[1]
+    for k in range(send_ref.shape[0]):
+        for ref, which in ((keep_ref, core), (send_ref, 1 - core)):
+            start = pl.multiple_of((2 * k + which) * rows, 8)
+            ref[k] = total[pl.ds(start, rows), :].astype(BF16)
 
 
 def attend_backward_kernel(
+    core_ref,
     query_ref,
     key_ref,
     value_ref,
@@ -165,68 +168,109 @@
     logsum_ref,
     seg_column_ref,
     seg_row_ref,
+    normed_ref,
     out_ref,
-    bias_ref,
-    key_sum,
-    value_sum,
+    *refs,
 ):
-    length, block = query_ref.shape[0], BLOCK
+    weight_refs, (bias_ref, key_sum, value_sum, turned, total) = refs[:-5], refs[-5:]
+    length, block = seg_row_ref.shape[1], BLOCK
 
     @pl.when(pl.program_id(0) == 0)
     def _():
         fill_bias(seg_column_ref, seg_row_ref, bias_ref, block)
-
-    for low in reversed(range(0, length, block)):
+        turned[...] = normed_ref[...].T
+
+    def lanes(head):
+        return slice(head * HEAD_DIM, (head + 1) * HEAD_DIM)
+
+    def scores(low, head):
+        high, here = low + block, lanes(head)
+        queries = query_ref[0, low:high, here] * score_scale
+        return (
+            dot(key_ref[0, :high, here], queries, NT),
+            dot(value_ref[0, :high, here], grad_ref[low:high, here], NT),
+        )
+
+    def chances(low, head, raw, grad_weights):
         high = low + block
-        for head in range(2):
-            lanes = slice(head * HEAD_DIM, (head + 1) * HEAD_DIM)
-            queries = query_ref[low:high, lanes] * score_scale
-            grads = grad_ref[low:high, lanes]
-            keys = key_ref[:high, lanes]
-            scores = dot(keys, queries, NT) + bias_ref[:high, low:high]
-            weights = jnp.exp(scores - logsum_ref[0, head : head + 1, low:high])
-            grad_weights = dot(value_ref[:high, lanes], grads, NT)
-            grad_values = dot(weights.astype(BF16), grads)
-            centred = jnp.sum(weights * grad_weights, axis=0, keepdims=True)
-            grad_raw = (weights * (grad_weights - centred)).astype(BF16)
-            grad_keys = dot(grad_raw, queries)
-            if high == length:
-                key_sum[:, lanes] = grad_keys
-                value_sum[:, lanes] = grad_values
-            else:
-                key_sum[:high, lanes] += grad_keys
-                value_sum[:high, lanes] += grad_values
-            out_ref[0, low:high, lanes] = dot(keys * score_scale, grad_raw, TN).T.astype(BF16)
+        weights = jnp.exp(raw + bias_ref[:high, low:high] - logsum_ref[0, head : head + 1, low:high])
+        centred = jnp.sum(weights * grad_weights, axis=0, keepdims=True)
+        return weights.astype(BF16), (weights * (grad_weights - centred)).astype(BF16)
+
+    def gradients(low, head, weights, grad_raw):
+        high, here = low + block, lanes(head)
+        grad_values = dot(weights, grad_ref[low:high, here])
+        grad_keys = dot(grad_raw, query_ref[0, low:high, here] * score_scale)
+        if high == length:
+            key_sum[:, here] = grad_keys
+            value_sum[:, here] = grad_values
+        else:
+            key_sum[:high, here] += grad_keys
+            value_sum[:high, here] += grad_values
+        keys = key_ref[0, :high, here] * score_scale
+        out_ref[0, low:high, here] = dot(keys, grad_raw, TN).T.astype(BF16)
+
+    blocks = [(low, head) for low in reversed(range(0, length, block)) for head in range(2)]
+    ready, before = scores(*blocks[0]), None
+    for index, place in enumerate(blocks):
+        after = scores(*blocks[index + 1]) if index + 1 < len(blocks) else None
+        now = chances(*place, *ready)
+        if before is not None:
+            gradients(*before)
+        before, ready = (*place, *now), after
+    gradients(*before)
     out_ref[1] = key_sum[...].astype(BF16)
     out_ref[2] = value_sum[...].astype(BF16)
-
-
-def attend_backward(packed, grad, logsum, seg_column, seg_row):
-    length = packed.shape[0]
+    weights = dot(turned[...], jnp.concatenate([out_ref[part] for part in range(3)], axis=1))
+    if len(weight_refs) == 1:
+        weight_refs[0][...] = weights.astype(BF16)
+    else:
+        total[...] = weights
+        part_rows(total, core_ref[0], *weight_refs)
+
+
+def attend_backward(core, packed, grad, logsum, seg_column, seg_row, normed, shards):
+    length = packed.shape[1]
     pairs = D // PAIR
-    return pl.pallas_call(
+    rows = D // shards
+    spec = lambda shape, place: pl.BlockSpec(shape, lambda pair, core: place(pair))
+    always = lambda shape: spec(shape, lambda pair: (0,) * len(shape))
+    if rows % 8:
+        weight_specs = [spec((D, 3 * PAIR), lambda pair: (0, pair))]
+        weight_shapes = [jax.ShapeDtypeStruct((D, 3 * D), BF16)]
+    else:
+        weight_specs = [spec((shards // 2, rows, 3 * PAIR), lambda pair: (0, 0, pair))] * 2
+        weight_shapes = [jax.ShapeDtypeStruct((shards // 2, rows, 3 * D), BF16)] * 2
+    results = pl.pallas_call(
         attend_backward_kernel,
-        grid=(pairs,),
-        in_specs=[
-            pl.BlockSpec((length, PAIR), lambda pair: (0, pair)),
-            pl.BlockSpec((length, PAIR), lambda pair: (0, pairs + pair)),
-            pl.BlockSpec((length, PAIR), lambda pair: (0, 2 * pairs + pair)),
-            pl.BlockSpec((length, PAIR), lambda pair: (0, pair)),
-            pl.BlockSpec((1, 2, length), lambda pair: (pair, 0, 0)),
-            whole((length, 1)),
-            whole((1, length)),
-        ],
-        out_specs=pl.BlockSpec((3, length, PAIR), lambda pair: (0, 0, pair)),
-        out_shape=jax.ShapeDtypeStruct((3, length, D), BF16),
-        scratch_shapes=[
-            pltpu.VMEM((length, length), F32),
-            pltpu.VMEM((length, PAIR), F32),
-            pltpu.VMEM((length, PAIR), F32),
-        ],
+        grid_spec=pltpu.PrefetchScalarGridSpec(
+            num_scalar_prefetch=1,
+            grid=(pairs,),
+            in_specs=[
+                spec((1, length, PAIR), lambda pair: (0, 0, pair)),
+                spec((1, length, PAIR), lambda pair: (1, 0, pair)),
+                spec((1, length, PAIR), lambda pair: (2, 0, pair)),
+                spec((length, PAIR), lambda pair: (0, pair)),
+                spec((1, 2, length), lambda pair: (pair, 0, 0)),
+                always((length, 1)),
+                always((1, length)),
+                always((length, D)),
+            ],
+            out_specs=[spec((3, length, PAIR), lambda pair: (0, 0, pair)), *weight_specs],
+            scratch_shapes=[
+                pltpu.VMEM((length, length), F32),
+                pltpu.VMEM((length, PAIR), F32),
+                pltpu.VMEM((length, PAIR), F32),
+                pltpu.VMEM((D, length), BF16),
+                pltpu.VMEM((D, 3 * PAIR), F32),
+            ],
+        ),
+        out_shape=[jax.ShapeDtypeStruct((3, length, D), BF16), *weight_shapes],
         compiler_params=params(),
         cost_estimate=cost(20 * length * length * D, 14 * length * D, length * length * 8),
         name="attend_backward",
-    )(packed, packed, packed, grad, logsum, seg_column, seg_row)
+    )(core, packed, packed, packed, grad, logsum, seg_column, seg_row, normed)
+    return results[0], results[1:]
 
 
 def route_kernel(
@@ -544,56 +588,69 @@
     )(rows, grads, inner, inner, *[outer] * len(outers))
 
 
-def expert_weights_kernel(rows_ref, weighed_ref, joined_ref, active_ref, inner_ref, outer_ref, turned):
+def outer_weights_kernel(*refs):
+    *active_refs, weighed_ref, out_ref = refs
+    active = jnp.concatenate([ref[...] for ref in active_refs], axis=1)
+    out_ref[...] = dot(active, weighed_ref[...], TN).astype(BF16).reshape(out_ref.shape)
+
+
+def outer_weights(active, weighed, shards):
+    count = active.shape[0]
+    width = FF // shards
+    if width % LANES:
+        lanes, taken, places = LANES, LANES // width, [lambda step: step]
+    else:
+        lanes, taken = width, 4
+        place = lambda at: jnp.where(at < shards // 2, 2 * at, 2 * (shards - 1 - at) + 1)
+        places = [lambda step, k=k: place(4 * step + k) for k in range(4)]
+    out = pl.pallas_call(
+        outer_weights_kernel,
+        grid=(shards // taken,),
+        in_specs=[
+            pl.BlockSpec((count, lanes), lambda step, place=place: (0, place(step))) for place in places
+        ]
+        + [whole((count, D))],
+        out_specs=pl.BlockSpec((taken, width, D), lambda step: (step, 0, 0)),
+        out_shape=jax.ShapeDtypeStruct((shards, width, D), BF16),
+        compiler_params=params(),
+        cost_estimate=cost(2 * count * D * FF, 2 * count * FF + 2 * D * FF),
+        name="outer_weights",
+    )(*[active] * len(places), weighed)
+    if width % LANES:
+        out = jnp.concatenate([out[k : k + 1] for k in around(shards)], axis=0)
+    return out
+
+
+def inner_weights_kernel(rows_ref, joined_ref, out_ref, turned):
     @pl.when(pl.program_id(0) == 0)
     def _():
-        turned[...] = rows_ref[:, :D].T
-
-    shards, _, share, width = inner_ref.shape
+        turned[...] = rows_ref[...].T
+
+    shards, _, share, _ = out_ref.shape
     for half in range(2):
         grads = dot(turned[...], joined_ref[half]).astype(BF16)
         for k in range(shards):
-            inner_ref[position(shards, k), half] = grads[k * share : (k + 1) * share]
-    grads = dot(active_ref[...], weighed_ref[...], TN).astype(BF16)
-    outer_ref[...] = grads.reshape(outer_ref.shape)
-
-
-def expert_weights(rows, weighed, joined, active, shards):
+            out_ref[position(shards, k), half] = grads[k * share : (k + 1) * share]
+
+
+def inner_weights(rows, joined, shards):
     count = rows.shape[0]
-    width = FF // shards
+    width = 2 * BLOCK
     share = D // shards
-    place = lambda step: jnp.where(step < shards // 2, 2 * step, 2 * (shards - 1 - step) + 1)
-    lanes = max(width, LANES)
-    if lanes != width:
-        place = lambda step: step
-    steps = FF // lanes
-    outer_block = (lanes // width, width, D)
-    results = pl.pallas_call(
-        expert_weights_kernel,
-        grid=(steps,),
+    return pl.pallas_call(
+        inner_weights_kernel,
+        grid=(FF // width,),
         in_specs=[
-            whole((count, D + LANES)),
-            whole((count, D)),
-            pl.BlockSpec((2, count, lanes), lambda step: (0, 0, step)),
-            pl.BlockSpec((count, lanes), lambda step: (0, place(step))),
-        ],
-        out_specs=[
-            pl.BlockSpec((shards, 2, share, lanes), lambda step: (0, 0, 0, step)),
-            pl.BlockSpec(outer_block, lambda step: (step, 0, 0)),
-        ],
-        out_shape=[
-            jax.ShapeDtypeStruct((shards, 2, share, FF), BF16),
-            jax.ShapeDtypeStruct((shards, width, D), BF16),
-        ],
+            pl.BlockSpec((count, D), lambda step: (0, 0)),
+            pl.BlockSpec((2, count, width), lambda step: (0, 0, step)),
+        ],
+        out_specs=pl.BlockSpec((shards, 2, share, width), lambda step: (0, 0, 0, step)),
+        out_shape=jax.ShapeDtypeStruct((shards, 2, share, FF), BF16),
         scratch_shapes=[pltpu.VMEM((D, count), BF16)],
         compiler_params=params(),
-        cost_estimate=cost(6 * count * D * FF, 6 * count * FF + 6 * D * FF),
-        name="expert_weights",
-    )(rows, weighed, joined, active)
-    inner, outer = results
-    if lanes != width:
-        outer = jnp.concatenate([outer[k : k + 1] for k in around(shards)], axis=0)
-    return inner, outer
+        cost_estimate=cost(4 * count * D * FF, 4 * count * FF + 4 * D * FF),
+        name="inner_weights",
+    )(rows, joined)
 
 
 def expert_backward_kernel(joined_ref, inner_ref, grads_ref, total):
@@ -684,6 +741,7 @@
 
 
 def middle_kernel(
+    core_ref,
     returned_ref,
     met_ref,
     targets_ref,
@@ -699,16 +757,12 @@
     weight_ref,
     grad_middle_ref,
     grad_attended_ref,
-    grad_weight_ref,
     mixer_ref,
-    work,
-    grad_gain,
-    grad_small,
-    grad_weight,
-    *,
+    *refs,
     experts,
     constant_count,
 ):
+    weight_refs, (work, grad_gain, grad_small, grad_weight) = refs[:-4], refs[-4:]
     block = middle_ref.shape[0]
     slots = returned_ref.shape[0]
     kinds = prior_ref.shape[0]
@@ -775,19 +829,21 @@
     rounded = grad_middle.astype(BF16)
     grad_attended_ref[...] = dot(rounded, weight_ref[...], NT).astype(BF16)
     part = dot(attended_ref[...], rounded, TN)
-    grad_weight[...] = jnp.where(first, part, grad_weight[...] + part)
+    grad_weight[:, :D] = jnp.where(first, part, grad_weight[:, :D] + part)
 
     @pl.when(pl.program_id(0) == pl.num_programs(0) - 1)
     def _():
-        grad_weight_ref[:, :D] = grad_weight[...].astype(BF16)
         column = jnp.broadcast_to(grad_gain[...], (LANES, D)).T
         place = kinds + gates + constant_count
-        grad_weight_ref[:, D:] = jnp.where(
-            iota((D, LANES), 1) == place, column, grad_small[...]
-        ).astype(BF16)
+        grad_weight[:, D:] = jnp.where(iota((D, LANES), 1) == place, column, grad_small[...])
+        if len(weight_refs) == 1:
+            weight_refs[0][...] = grad_weight[...].astype(BF16)
+        else:
+            part_rows(grad_weight, core_ref[0], *weight_refs)
 
 
 def middle_backward(
+    core,
     returned,
     met,
     targets,
@@ -802,48 +858,61 @@
     gathered,
     experts,
     constant_count,
+    shards,
 ):
     block = TOKENS["middle"]
     tokens = middle.shape[0]
     slots = returned.shape[0]
     kinds = prior.shape[0]
-    token_block = lambda width: pl.BlockSpec((block, width), lambda step: (step, 0))
-    token_lanes = lambda height: pl.BlockSpec((height, block), lambda step: (0, step))
-    return pl.pallas_call(
+    rows = D // shards
+    spec = lambda shape, place: pl.BlockSpec(shape, lambda step, core: place(step))
+    always = lambda shape: spec(shape, lambda step: (0,) * len(shape))
+    token_block = lambda width: spec((block, width), lambda step: (step, 0))
+    token_lanes = lambda height: spec((height, block), lambda step: (0, step))
+    if rows % 8:
+        weights = [(D, D + LANES)]
+    else:
+        weights = [(shards // 2, rows, D + LANES)] * 2
+    results = pl.pallas_call(
         functools.partial(middle_kernel, experts=experts, constant_count=constant_count),
-        grid=(tokens // block,),
-        in_specs=[
-            whole((slots, D)),
-            whole((1, slots)),
-            token_block(2),
-            token_lanes(2),
-            token_lanes(kinds),
-            token_block(LANES),
-            token_block(D),
-            token_block(D),
-            token_block(D),
-            token_block(D),
-            pl.BlockSpec((D, LANES), lambda step: (0, 4 * D // LANES)),
-            whole((1, D)),
-            pl.BlockSpec((D, D), lambda step: (0, 3)),
-        ],
-        out_specs=[token_block(D), token_block(D), whole((D, D + LANES)), whole((kinds, kinds))],
+        grid_spec=pltpu.PrefetchScalarGridSpec(
+            num_scalar_prefetch=1,
+            grid=(tokens // block,),
+            in_specs=[
+                always((slots, D)),
+                always((1, slots)),
+                token_block(2),
+                token_lanes(2),
+                token_lanes(kinds),
+                token_block(LANES),
+                token_block(D),
+                token_block(D),
+                token_block(D),
+                token_block(D),
+                spec((D, LANES), lambda step: (0, 4 * D // LANES)),
+                always((1, D)),
+                spec((D, D), lambda step: (0, 3)),
+            ],
+            out_specs=[token_block(D), token_block(D), always((kinds, kinds))]
+            + [always(shape) for shape in weights],
+            scratch_shapes=[
+                pltpu.VMEM((LANES, block), F32),
+                pltpu.VMEM((1, D), F32),
+                pltpu.VMEM((D, LANES), F32),
+                pltpu.VMEM((D, D + LANES), F32),
+            ],
+        ),
         out_shape=[
             jax.ShapeDtypeStruct((tokens, D), F32),
             jax.ShapeDtypeStruct((tokens, D), BF16),
-            jax.ShapeDtypeStruct((D, D + LANES), BF16),
             jax.ShapeDtypeStruct((kinds, kinds), F32),
-        ],
-        scratch_shapes=[
-            pltpu.VMEM((LANES, block), F32),
-            pltpu.VMEM((1, D), F32),
-            pltpu.VMEM((D, LANES), F32),
-            pltpu.VMEM((D, D), F32),
-        ],
+        ]
+        + [jax.ShapeDtypeStruct(shape, BF16) for shape in weights],
         compiler_params=params(),
         cost_estimate=cost(2 * tokens * D * (slots + 2 * D), 18 * tokens * D),
         name="middle_backward",
     )(
+        core,
         returned,
         met,
         targets,
@@ -858,29 +927,7 @@
         gain,
         gathered,
     )
-
-
-def project_backward_kernel(normed_ref, packed_ref, out_ref, turned):
-    @pl.when(pl.program_id(0) == 0)
-    def _():
-        turned[...] = normed_ref[...].T
-
-    out_ref[...] = dot(turned[...], packed_ref[0]).astype(BF16)
-
-
-def project_backward(normed, grad_packed):
-    tokens = normed.shape[0]
-    return pl.pallas_call(
-        project_backward_kernel,
-        grid=(3,),
-        in_specs=[whole((tokens, D)), pl.BlockSpec((1, tokens, D), lambda step: (step, 0, 0))],
-        out_specs=pl.BlockSpec((D, D), lambda step: (0, step)),
-        out_shape=jax.ShapeDtypeStruct((D, 3 * D), BF16),
-        scratch_shapes=[pltpu.VMEM((D, tokens), BF16)],
-        compiler_params=params(),
-        cost_estimate=cost(6 * tokens * D * D, 8 * tokens * D + 6 * D * D),
-        name="project_backward",
-    )(normed, grad_packed)
+    return *results[:3], results[3:]
 
 
 def input_kernel(packed_ref, weight_ref, hidden_ref, grad_middle_ref, gain_ref, out_ref, grad_gain_ref):
@@ -933,6 +980,17 @@
 
 def exchange(blocks, axis):
     return lax.all_to_all(blocks, axis, split_axis=0, concat_axis=0, tiled=True)
+
+
+def exchange_apart(blocks, axis):
+    count, me = lax.axis_size(axis), lax.axis_index(axis)
+    out = jnp.zeros_like(blocks)
+    for step in range(count):
+        block = pick(blocks, (me + step) % count, 0)
+        if step:
+            block = lax.ppermute(block, axis, [(i, (i + step) % count) for i in range(count)])
+        out = lax.dynamic_update_slice(out, block[None], ((me - step) % count,) + (0,) * block.ndim)
+    return out
 
 
 def flip(axis):
@@ -972,15 +1030,20 @@
     return total.reshape(-1, width)
 
 
-def scatter_side(terms):
-    width = terms.shape[1]
-    count, wide = lax.axis_size("dp"), lax.axis_size("expert") // 2
-    rows = terms.shape[0] // (2 * count * wide)
+def pick(array, index, axis):
+    return lax.dynamic_index_in_dim(array, index, axis, keepdims=False)
+
+
+def scatter_side(parted):
+    wide = lax.axis_size("expert") // 2
     place, core = lax.axis_index("expert") // 2, lax.axis_index("expert") % 2
-    terms = terms.reshape(count, wide, 2, rows, width)
-    pick = lambda array, index, axis: lax.dynamic_index_in_dim(array, index, axis, keepdims=False)
-    came = lax.ppermute(pick(terms, 1 - core, 2), "expert", flip("expert"))
-    pair = (pick(terms, core, 2).astype(F32) + came.astype(F32)).astype(BF16)
+    if len(parted) == 1:
+        terms = parted[0].reshape(lax.axis_size("dp") * wide, 2, -1, parted[0].shape[1])
+        parted = (pick(terms, 1 - core, 1), pick(terms, core, 1))
+    send, keep = parted
+    came = lax.ppermute(send, "expert", flip("expert"))
+    pair = (keep.astype(F32) + came.astype(F32)).astype(BF16)
+    pair = pair.reshape(lax.axis_size("dp"), wide, *pair.shape[1:])
     total = pick(pair, place, 1).astype(F32)
     for step in range(1, wide):
         came = lax.ppermute(pick(pair, (place + step) % wide, 1), "expert", shift("expert", step))
@@ -1021,16 +1084,20 @@
 
 
 def own_kernel(
-    shares_ref, inner_ref, outer_ref, gain_ref, mixer_ref, own_ref, out_ref, own_outer_ref, few_ref, *, kinds
+    in_ref, shares_ref, inner_ref, outer_ref, gain_ref, mixer_ref, own_ref, out_ref, own_outer_ref, few_ref, *, kinds
 ):
-    total = jnp.sum(shares_ref[...].astype(F32), axis=0)
-    own_ref[...] = total[:, : 3 * D]
-    out_ref[...] = total[:, 3 * D :]
+    total = jnp.sum(in_ref[...].astype(F32), axis=0)
+    out = jnp.sum(shares_ref[...].astype(F32), axis=0)
+    for pair in range(D // PAIR):
+        for part in range(3):
+            low, place = (3 * pair + part) * PAIR, part * D + pair * PAIR
+            own_ref[:, place : place + PAIR] = total[:, low : low + PAIR]
+    out_ref[...] = out
     inner, outer = inner_ref[...].astype(F32), outer_ref[...].astype(F32)
     own_outer_ref[...] = outer
     width = few_ref.shape[2]
     square = jnp.sum(jnp.sum(inner * inner, axis=0), axis=(0, 1), keepdims=True)
-    for member in (total, outer):
+    for member in (total, out, outer):
         square = square + jnp.sum(member * member, axis=(0, 1), keepdims=True)
     few = few_ref.at[0]
     few[...] = jnp.zeros_like(few)
@@ -1044,10 +1111,10 @@
         few_ref[device] = row
 
 
-def own_sums(shares, inner, outer, grad_gain, grad_mixer, devices):
+def own_sums(in_shares, out_shares, inner, outer, grad_gain, grad_mixer, devices):
     kinds = grad_mixer.shape[0]
     width = D + (-(-kinds * kinds // LANES) + 1) * LANES
-    rows = shares.shape[1]
+    rows = in_shares.shape[1]
     return pl.pallas_call(
         functools.partial(own_kernel, kinds=kinds),
         out_shape=[
@@ -1059,7 +1126,7 @@
         compiler_params=params(),
         cost_estimate=cost(6 * D * FF, 3 * D * FF),
         name="own_sums",
-    )(shares, inner, outer, grad_gain, grad_mixer)
+    )(in_shares, out_shares, inner, outer, grad_gain, grad_mixer)
 
 
 def adam(master, first, second, grad, factor, step_rate):
@@ -1126,7 +1193,7 @@
 
 
 def update(index, few, in_own, out_own, inner_own, outer_own, states, kinds, constant_count):
-    steps = 4
+    steps = UPDATE_STEPS
     turn = lambda which, array: array.T if which in (2, 4) else array
     states = [[turn(which, array) for array in state] for which, state in enumerate(states)]
     half = steps // 2
@@ -1233,25 +1300,26 @@
         ],
         axis=1,
     ).astype(BF16)
-    mine, expert_pieces = lax.optimization_barrier((mine, expert_pieces))
-    gathered = gather_all(gather_far(mine))
+    targets = pair_targets(routes, priority[0], experts, kinds, capacity)
+    target_rows = targets.T
+    split = (groups, slots // groups, -1)
+    placed = place_rows(cotangent, target_rows, slots).reshape(split)
+    column = gather_far(mine)
+    column, placed = lax.optimization_barrier((column, placed))
+    gathered = gather_all(column)
     expert_inner, expert_outer = gather_experts(expert_pieces)
     gains = gathered[:, 4 * D + small_width : 4 * D + small_width + 2].astype(F32).T
     gain_first, gain_second = gains[0:1], gains[1:2]
-
-    targets = pair_targets(routes, priority[0], experts, kinds, capacity)
-    target_rows = targets.T
-    split = (groups, slots // groups, -1)
-    arrived_grad = exchange(place_rows(cotangent, target_rows, slots).reshape(split), "expert")
-    arrived_grad = arrived_grad.reshape(slots, D)
+    arrived_grad = exchange(placed, "expert").reshape(slots, D)
     route_rows = routes.T
     prior_rows = gate_prior.T
     extra = jnp.dot(gate_mix.astype(BF16).astype(F32).T, prior_rows, precision=highest)
     seg_row = segments
     seg_column = segments.reshape(token_count, 1)
 
-    normed_first, packed = project(hidden_in, gain_first, gathered)
-    attended, logsum = attend_forward(packed, seg_column, seg_row)
+    normed_first, packed, attended, logsum = attend_forward(
+        hidden_in, gain_first, gathered, seg_column, seg_row
+    )
     middle, normed_second, table, rows = route_tokens(
         hidden_in,
         attended,
@@ -1269,20 +1337,17 @@
     grad_joined, active, produced, met, weighed = expert_forward(
         arrived, arrived_grad, expert_inner, expert_outer
     )
+    outer_own = scatter_expert(outer_weights(active, weighed, lax.axis_size("dp")))
     met = exchange(met.reshape(groups, 1, slots // groups), "expert").reshape(1, slots)
     grad_rows = expert_backward(grad_joined, expert_inner)
-    met, grad_rows = lax.optimization_barrier((met, grad_rows))
+    met, grad_rows, grad_joined = lax.optimization_barrier((met, grad_rows, grad_joined))
     grad_returned = exchange(grad_rows.reshape(split), "expert").reshape(slots, D)
-    grad_inner, grad_outer = expert_weights(
-        arrived, weighed, grad_joined, active, lax.axis_size("dp")
-    )
-    grad_returned, produced, grad_inner, grad_outer = lax.optimization_barrier(
-        (grad_returned, produced, grad_inner, grad_outer)
-    )
+    grad_inner = inner_weights(arrived, grad_joined, lax.axis_size("dp"))
+    grad_returned, produced, grad_inner = lax.optimization_barrier((grad_returned, produced, grad_inner))
     inner_own = scatter_expert(grad_inner)
-    outer_own = scatter_expert(grad_outer)
-    returned = exchange(produced.reshape(split), "expert").reshape(slots, D)
-    grad_middle, grad_attended, grad_out_and_small, grad_mixer = middle_backward(
+    core = (lax.axis_index("expert") % 2).reshape(1).astype(jnp.int32)
+    grad_middle, grad_attended, grad_mixer, grad_out_and_small = middle_backward(
+        core,
         grad_returned,
         met,
         targets,
@@ -1297,13 +1362,19 @@
         gathered,
         experts,
         constant_count,
+        devices,
     )
     out_sum = scatter_side(grad_out_and_small)
 
-    grad_packed = attend_backward(packed, grad_attended, logsum, seg_column, seg_row)
-    grad_packed, returned, out_sum = lax.optimization_barrier((grad_packed, returned, out_sum))
-    in_sum = scatter_side(project_backward(normed_first, grad_packed))
-    shares = exchange(jnp.concatenate([in_sum, out_sum], axis=2), "dp")
+    grad_packed, grad_weight_in = attend_backward(
+        core, packed, grad_attended, logsum, seg_column, seg_row, normed_first, devices
+    )
+    grad_weight_in, out_sum = lax.optimization_barrier((grad_weight_in, out_sum))
+    in_sum = scatter_side(grad_weight_in)
+    out_shares = exchange(out_sum, "dp")
+    in_sum, out_shares, produced = lax.optimization_barrier((in_sum, out_shares, produced))
+    returned = exchange_apart(produced.reshape(split), "expert").reshape(slots, D)
+    in_shares = exchange(in_sum, "dp")
     input_grad, grad_gain_first = input_backward(
         grad_packed, gathered, hidden_in, grad_middle, gain_first
     )
@@ -1312,7 +1383,7 @@
     )
 
     in_own, out_own, outer_own, few = own_sums(
-        shares, inner_own, outer_own, grad_gain_first, grad_mixer, devices
+        in_shares, out_shares, inner_own, outer_own, grad_gain_first, grad_mixer, devices
     )
     few = exchange(few, BOTH)
     index = lax.axis_index("dp") * groups + lax.axis_index("expert")

time: 388 us -> 373 us (0.961)
  waiting for transfers between devices: 96.1 us -> 74.4 us
  starting transfers between devices: 36.8 us -> 48.3 us
  Pallas kernels: 181 us -> 175 us
    all_to_all x6, waiting for transfers between devices: 27.2 us -> 15 us  [exchange(): return lax.all_to_all(blocks, axis, split_axis=0, concat_axis=0, tiled=True)]
    ppermute x2, waiting for transfers between devices: 21.5 us -> 12.2 us  [scatter_side(): lax.ppermute(pick(pair, (place + step) % wide, 1), 'expert', shift('exper...]
    pallas_call x5 -> x4, Pallas kernels: 86.1 us -> 79.7 us  [the longest x1 36.2 us: attend_backward(): pl.pallas_call(attend_backward_kernel, grid_spec=pltpu.PrefetchScalarGrid...]
    all_to_all x6, starting transfers between devices: 24.2 us -> 30.2 us  [exchange(): return lax.all_to_all(blocks, axis, split_axis=0, concat_axis=0, tiled=True)]
    ppermute x1, waiting for transfers between devices: 27 us -> 22.1 us  [gather_all(): near = [column, lax.ppermute(column, 'dp', flip('dp'))]]
    dynamic_slice x4 -> x0, local copies, waits for them, and re-layouts: 4.72 us -> none  [scatter_side(): lax.dynamic_index_in_dim(array, index, axis, keepdims=False)]
    another operation x5 -> x3, other arithmetic: 4.01 us -> 0.03 us
    unnamed x33 -> x45, local copies, waits for them, and re-layouts: 6.79 us -> 8.01 us
  transfers between devices with their start and end apart: 23 -> 26, of which waited for: 9 -> 9; matrix products, arithmetic and copies ran while one was open for 4% -> 5% of each run, Pallas kernels for 38% -> 37%
where the time goes in v1:
time: 373 us; the launch traced here: 368 us
  Pallas kernels  175 us (47%)
  waiting for transfers between devices  74.4 us (20%)
  starting transfers between devices  48.3 us (13%)
  blocking collectives  27.5 us (7%)
  local copies, waits for them, and re-layouts  18.9 us (5%)
  between operations  14.7 us (4%)
  other arithmetic  7.81 us (2%)
    pallas_call x1, Pallas kernels, attend_backward(): pl.pallas_call(attend_backward_kernel, grid_spec=pltpu.PrefetchScalarGrid...  36.2 us
    all_to_all x6, starting transfers between devices, exchange(): return lax.all_to_all(blocks, axis, split_axis=0, concat_axis=0, tiled=True)  30.2 us
    all_to_all x1, blocking collectives, exchange(): return lax.all_to_all(blocks, axis, split_axis=0, concat_axis=0, tiled=True)  27.5 us
    pallas_call x1, Pallas kernels, attend_forward(): pl.pallas_call(attend_forward_kernel, grid=(pairs,), in_specs=[whole((len...  24.9 us
    ppermute x1, waiting for transfers between devices, gather_all(): near = [column, lax.ppermute(column, 'dp', flip('dp'))]  22.1 us
    pallas_call x1, Pallas kernels, expert_forward(): pl.pallas_call(functools.partial(expert_kernel, outers=len(outers)), grid...  20.8 us
    all_to_all x6, waiting for transfers between devices, exchange(): return lax.all_to_all(blocks, axis, split_axis=0, concat_axis=0, tiled=True)  15 us
    ppermute x2, waiting for transfers between devices, gather_all(): piece = lax.ppermute(piece, 'expert', shift('expert', step))  14.8 us
  transfers between devices with their start and end apart: 26, of which 9 were waited for; matrix products, arithmetic and copies ran while one was open for 5% of the time, Pallas kernels for 37%

profile of v1, /device:TPU:0, one launch (start us, length us, event | category | flops | bytes accessed | tf_op | source)
XLA Modules:
  0.0 367.9 jit_solution(14411707823492262184)
XLA Ops:
  11.0 3.1 collective-permute-start
  14.1 2.6 collective-permute-start.1
  22.1 4.8 %place_rows.1 = bf16[1024,768]{1,0:T(8,128)(2,1)} custom-call(bf16[1024,768]{1,0:T(8,128)(2,1)} %upstream_ref.3, s32[2,1024]{1,0:T(2,128)} %copy.204.targets_ref), custom_call_target="tpu_custom_call" | custom-call | flops 25165824 | bytes 49152 | tf_op jit(solution)/shard_map/place_rows/pallas_call | solution.py:398
  27.9 2.2 collective-permute-done.1
  33.3 3.6 all-to-all-start.1
  37.9 22.1 %collective-permute-done.4 = bf16[4,24,3200]{2,1,0:T(8,128)(2,1)S(1)} collective-permute-done((bf16[4,24,3200]{2,1,0:T(8,128)(2,1)S(1)}, bf16[4,24,3200]{2,1,0:T(8,128)(2,1)S(1)}, u32[]{:S(2)}, u32[]{:S(2)}) %collective-permute-start.4) | collective-permute-done | bytes 614432 | tf_op jit(solution)/shard_map/ppermute | solution.py:1018
  62.9 14.8 %collective-permute-done.8 = bf16[4,24,3200]{2,1,0:T(8,128)(2,1)S(1)} collective-permute-done((bf16[4,24,3200]{2,1,0:T(8,128)(2,1)S(1)}, bf16[4,24,3200]{2,1,0:T(8,128)(2,1)S(1)}, u32[]{:S(2)}, u32[]{:S(2)}) %collective-permute-start.8) | collective-permute-done | bytes 614432 | tf_op jit(solution)/shard_map/ppermute | solution.py:1024
  83.0 24.9 %attend_forward.1 = (bf16[1024,768]{1,0:T(8,128)(2,1)}, bf16[3,1024,768]{2,1,0:T(8,128)(2,1)}, bf16[1024,768]{1,0:T(8,128)(2,1)}, f32[6,2,1024]{2,1,0:T(2,128)}) custom-call(bf16[1024,768]{1,0:T(8,128)(2,1)} %hidden_ref.5, f32[1,768]{1,0:T(1,128)} %get-tuple-element.212.gain_ref, bf16[768,3200]{1,0:T(8,128)(2,1)} %bitcast.140, bf16[768,3200]{1,0:T(8,128)(2,1)} %bitcast.141, ...), custom_call_target="tpu_custom_call" | custom-call | flops 100663296 | bytes 98304 | tf_op jit(solution)/shard_map/attend_forward/pallas_call | solution.py:123
  107.8 11.9 %route_tokens.1 = (f32[1024,768]{1,0:T(8,128)}, bf16[1024,768]{1,0:T(8,128)(2,1)}, f32[1024,128]{1,0:T(8,128)}, bf16[1024,896]{1,0:T(8,128)(2,1)}) custom-call(bf16[1024,768]{1,0:T(8,128)(2,1)} %hidden_ref.5, bf16[1024,768]{1,0:T(8,128)(2,1)} %get-tuple-element.125.attended_ref, bf16[1024,768]{1,0:T(8,128)(2,1)} %upstream_ref.3, f32[8,1024]{1,0:T(8,128)} %fusion.8.extra_ref, ...), custom_call_target="tpu_custom_call" | custom-call | flops 44040192 | bytes 245760 | tf_op jit(solution)/shard_map/route_tokens/pallas_call | solution.py:432
  119.8 27.5 %all_to_all.35 = bf16[4,256,896]{2,1,0:T(8,128)(2,1)} all-to-all(bf16[4,256,896]{2,1,0:T(8,128)(2,1)} %bitcast.165), channel_id=1, replica_groups=mesh['dp'=8,'expert'=4] {'expert'}, dimensions={0} | all-to-all | bytes 3670016 | tf_op jit(solution)/shard_map/all_to_all | solution.py:982
  147.3 20.8 %expert_forward.1 = (bf16[2,1024,2048]{2,1,0:T(8,128)(2,1)}, bf16[1024,2048]{1,0:T(8,128)(2,1)}, bf16[1024,768]{1,0:T(8,128)(2,1)}, f32[1,1024]{1,0:T(1,128)}, bf16[1024,768]{1,0:T(8,128)(2,1)}) custom-call(bf16[1024,896]{1,0:T(8,128)(2,1)} %bitcast.149, bf16[1024,768]{1,0:T(8,128)(2,1)} %bitcast.157, bf16[8,2304,256]{2,1,0:T(8,128)(2,1)} %bitcast.130, ...), custom_call_target="tpu_custom_call" | custom-call | flops 201326592 | bytes 344064 | tf_op jit(solution)/shard_map/expert_forward/pallas_call | solution.py:560
  168.1 7.2 %outer_weights.1 = bf16[8,256,768]{2,1,0:T(8,128)(2,1)} custom-call(bf16[1024,2048]{1,0:T(8,128)(2,1)} %get-tuple-element.156.refs_0_.refs_1_.refs_2_.refs_3_, bf16[1024,2048]{1,0:T(8,128)(2,1)} %get-tuple-element.156.refs_0_.refs_1_.refs_2_.refs_3_, bf16[1024,2048]{1,0:T(8,128)(2,1)} %get-tuple-element.156.refs_0_.refs_1_.refs_2_.refs_3_, ...), custom_call_target="tpu_custom_call" | custom-call | flops 50331648 | bytes 114688 | tf_op jit(solution)/shard_map/outer_weights/pallas_call | solution.py:606
  175.3 3.3 all-to-all-start.2
  178.6 11.2 %expert_backward.1 = bf16[1024,768]{1,0:T(8,128)(2,1)} custom-call(bf16[2,1024,2048]{2,1,0:T(8,128)(2,1)} %get-tuple-element.132.joined_ref, bf16[8,2304,256]{2,1,0:T(8,128)(2,1)} %bitcast.138), custom_call_target="tpu_custom_call" | custom-call | flops 100663296 | bytes 229376 | tf_op jit(solution)/shard_map/expert_backward/pallas_call | solution.py:671
  189.8 3.6 all-to-all-start.3
  193.6 11.5 %inner_weights.1 = bf16[8,2,96,2048]{3,2,1,0:T(8,128)(2,1)} custom-call(bf16[1024,896]{1,0:T(8,128)(2,1)} %bitcast.150, bf16[2,1024,2048]{2,1,0:T(8,128)(2,1)} %get-tuple-element.132.joined_ref), custom_call_target="tpu_custom_call" | custom-call | flops 100663296 | bytes 229376 | tf_op jit(solution)/shard_map/inner_weights/pallas_call | solution.py:640
  205.1 8.3 %all-to-all-done.3 = bf16[4,256,768]{2,1,0:T(8,128)(2,1)S(1)} async-done(((bf16[4,256,768]{2,1,0:T(8,128)(2,1)}), bf16[4,256,768]{2,1,0:T(8,128)(2,1)S(1)}, u32[]{:S(2)}, u32[]{:S(2)}) %all-to-all-start.3) | async-done | bytes 1572896 | tf_op jit(solution)/shard_map/all_to_all | solution.py:982
  214.5 14.4 %middle_backward.1 = (f32[1024,768]{1,0:T(8,128)}, bf16[1024,768]{1,0:T(8,128)(2,1)}, f32[8,8]{1,0:T(8,128)}, bf16[16,24,896]{2,1,0:T(8,128)(2,1)}, bf16[16,24,896]{2,1,0:T(8,128)(2,1)}) custom-call(s32[1]{0:T(128)} %bitcast.core_ref, bf16[1024,768]{1,0:T(8,128)(2,1)} %bitcast.154, f32[1,1024]{1,0:T(1,128)} %bitcast.182, s32[1024,2]{1,0:T(8,128)} %copy-done.1, ...), custom_call_target="tpu_custom_call" | custom-call | flops 62914560 | bytes 221184 | tf_op jit(solution)/shard_map/middle_backward/pallas_call | solution.py:876
  229.1 2.3 collective-permute-done.10
  233.2 36.2 %attend_backward.1 = (bf16[3,1024,768]{2,1,0:T(8,128)(2,1)}, bf16[16,24,2304]{2,1,0:T(8,128)(2,1)}, bf16[16,24,2304]{2,1,0:T(8,128)(2,1)}) custom-call(s32[1]{0:T(128)} %bitcast.core_ref, bf16[3,1024,768]{2,1,0:T(8,128)(2,1)} %get-tuple-element.124.query_ref.key_ref.value_ref, bf16[3,1024,768]{2,1,0:T(8,128)(2,1)} %get-tuple-element.124.query_ref.key_ref.value_ref, ...), custom_call_target="tpu_custom_call" | custom-call | flops 251658240 | bytes 172032 | tf_op jit(solution)/shard_map/attend_backward/pallas_call | solution.py:244
  270.2 3.9 %collective-permute-done.12 = bf16[16,24,2304]{2,1,0:T(8,128)(2,1)S(1)} collective-permute-done((bf16[16,24,2304]{2,1,0:T(8,128)(2,1)}, bf16[16,24,2304]{2,1,0:T(8,128)(2,1)S(1)}, u32[]{:S(2)}, u32[]{:S(2)}) %collective-permute-start.12) | collective-permute-done | bytes 1769504 | tf_op jit(solution)/shard_map/ppermute | solution.py:1044
  278.7 8.1 %all-to-all-start.4 = ((bf16[8,24,896]{2,1,0:T(8,128)(2,1)}), bf16[8,24,896]{2,1,0:T(8,128)(2,1)S(1)}, u32[]{:S(2)}, u32[]{:S(2)}) async-start(bf16[8,24,896]{2,1,0:T(8,128)(2,1)} %fusion.5), calls=%async_computation.4 | async-start | bytes 688128 | tf_op jit(solution)/shard_map/all_to_all | solution.py:982
  286.8 12.2 %collective-permute-done.13 = bf16[8,24,2304]{2,1,0:T(8,128)(2,1)} collective-permute-done((bf16[8,24,2304]{2,1,0:T(8,128)(2,1)}, bf16[8,24,2304]{2,1,0:T(8,128)(2,1)}, u32[]{:S(2)}, u32[]{:S(2)}) %collective-permute-start.13) | collective-permute-done | bytes 884768 | tf_op jit(solution)/shard_map/ppermute | solution.py:1049
  299.0 2.3 fusion.4
  301.3 8.1 %all-to-all-start.5 = ((bf16[8,24,2304]{2,1,0:T(8,128)(2,1)}), bf16[8,24,2304]{2,1,0:T(8,128)(2,1)S(1)}, u32[]{:S(2)}, u32[]{:S(2)}) async-start(bf16[8,24,2304]{2,1,0:T(8,128)(2,1)} %fusion.4), calls=%async_computation.5 | async-start | bytes 1769472 | tf_op jit(solution)/shard_map/all_to_all | solution.py:982
  309.5 2.4 dynamic-slice_bitcast_fusion.1
  313.7 9.5 %input_backward.1 = (f32[1024,768]{1,0:T(8,128)}, f32[1,768]{1,0:T(1,128)}) custom-call(bf16[3,1024,768]{2,1,0:T(8,128)(2,1)} %get-tuple-element.150.packed_ref, bf16[768,3200]{1,0:T(8,128)(2,1)} %bitcast.147, bf16[1024,768]{1,0:T(8,128)(2,1)} %hidden_ref.5, f32[1024,768]{1,0:T(8,128)} %get-tuple-element.151.grad_middle_ref, ...), custom_call_target="tpu_custom_call" | custom-call | flops 56623104 | bytes 196608 | tf_op jit(solution)/shard_map/input_backward/pallas_call | solution.py:950
  324.6 6.7 %all-to-all-done.5.in_ref = bf16[8,24,2304]{2,1,0:T(8,128)(2,1)S(1)} async-done(((bf16[8,24,2304]{2,1,0:T(8,128)(2,1)}), bf16[8,24,2304]{2,1,0:T(8,128)(2,1)S(1)}, u32[]{:S(2)}, u32[]{:S(2)}) %all-to-all-start.5) | async-done | bytes 884768 | tf_op jit(solution)/shard_map/all_to_all | solution.py:982
  332.2 3.0 own_sums.1
  335.3 3.6 all-to-all-start.6
  341.1 7.9 %mix_branches.1 = bf16[1024,768]{1,0:T(8,128)(2,1)} custom-call(bf16[1024,768]{1,0:T(8,128)(2,1)} %bitcast.156, s32[1024,2]{1,0:T(8,128)} %copy-done.1, f32[1024,128]{1,0:T(8,128)} %get-tuple-element.135.table_ref, f32[1024,768]{1,0:T(8,128)} %get-tuple-element.136.middle_ref, bf16[1024,768]{1,0:T(8,128)(2,1)} %get-tuple-element.137.normed_ref, ...), custom_call_target="tpu_custom_call" | custom-call | flops 50331648 | bytes 147456 | tf_op jit(solution)/shard_map/mix_branches/pallas_call | solution.py:724
  349.7 11.3 %update.1 = (f32[1,1]{1,0:T(1,128)}, f32[24,2304]{1,0:T(8,128)}, f32[24,2304]{1,0:T(8,128)}, f32[24,2304]{1,0:T(8,128)}, bf16[24,2304]{1,0:T(8,128)(2,1)}, /*ind...) custom-call(s32[1]{0:T(128)} %bitcast.65.refs_0_, ...), custom_call_target="tpu_custom_call" | custom-call | flops 983040 | bytes 737280 | tf_op jit(solution)/shard_map/update/pallas_call | solution.py:1214
  (137 shorter events, 37.9 us)
Async XLA Ops:
  7.2 140.0 %all-gather.3.cloned.1.call-start = ((), (), s32[]{:S(2)}) async-start(), calls=%async_computation.11 | async-start | bytes 10616832 | tf_op jit(solution)/shard_map/all_gather | solution.py:1076
  9.5 8.6 %copy-start.11 = (s32[1024,2]{0,1:T(2,128)S(1)}, s32[1024,2]{0,1:T(2,128)}, u32[]{:S(2)}) copy-start(s32[1024,2]{0,1:T(2,128)} %param.32) | copy-start | bytes 24580
  10.6 7.7 %copy-start.19 = (s32[1,1024]{1,0:T(1,128)S(1)}, s32[1,1024]{1,0:T(1,128)}, u32[]{:S(2)}) copy-start(s32[1,1024]{1,0:T(1,128)} %param.33) | copy-start | bytes 12292
  11.0 16.8 %collective-permute-start = (bf16[24,3200]{1,0:T(8,128)(2,1)S(1)}, bf16[24,3200]{1,0:T(8,128)(2,1)S(1)}, u32[]{:S(2)}, u32[]{:S(2)}) collective-permute-start(bf16[24,3200]{1,0:T(8,128)(2,1)S(1)} %concatenate.33), channel_id=1, source_target_pairs={{0,8},{4,12},{8,16},{12,20},{16,24},{20,28},{24,0},{28,4},{1,9},{5... | collective-permute-start | bytes 460808 | tf_op jit(solution)/shard_map/ppermute | solution.py:1009
  14.1 16.0 %collective-permute-start.1 = (bf16[24,3200]{1,0:T(8,128)(2,1)S(1)}, bf16[24,3200]{1,0:T(8,128)(2,1)S(1)}, u32[]{:S(2)}, u32[]{:S(2)}) collective-permute-start(bf16[24,3200]{1,0:T(8,128)(2,1)S(1)} %concatenate.33), channel_id=1, source_target_pairs={{0,16},{4,20},{8,24},{12,28},{16,0},{20,4},{24,8},{28,12},{1,17},{... | collective-permute-start | bytes 460808 | tf_op jit(solution)/shard_map/ppermute | solution.py:1009
  16.7 13.4 %collective-permute-start.2 = (bf16[24,3200]{1,0:T(8,128)(2,1)S(1)}, bf16[24,3200]{1,0:T(8,128)(2,1)S(1)}, u32[]{:S(2)}, u32[]{:S(2)}) collective-permute-start(bf16[24,3200]{1,0:T(8,128)(2,1)S(1)} %concatenate.33), channel_id=1, source_target_pairs={{0,24},{4,28},{8,0},{12,4},{16,8},{20,12},{24,16},{28,20},{1,25},{... | collective-permute-start | bytes 460808 | tf_op jit(solution)/shard_map/ppermute | solution.py:1009
  20.2 6.8 %copy-start.1 = (s32[1024,2]{1,0:T(8,128)}, s32[1024,2]{1,0:T(8,128)S(1)}, u32[]{:S(2)}) copy-start(s32[1024,2]{1,0:T(8,128)S(1)} %add_select_fusion.targets_ref) | copy-start | bytes 24580
  30.1 31.6 %collective-permute-start.3 = (bf16[4,24,3200]{2,1,0:T(8,128)(2,1)S(1)}, bf16[4,24,3200]{2,1,0:T(8,128)(2,1)}, u32[]{:S(2)}, u32[]{:S(2)}) collective-permute-start(bf16[4,24,3200]{2,1,0:T(8,128)(2,1)S(1)} %bitcast_dynamic-update-slice_fusion.11), channel_id=1, source_target_pairs={{0,1},{1,0},{2,3},{3,2},{4,5},{5,4},{6,7},{7,6},{8,9},{9,8},{10,11... | collective-permute-start | bytes 1843208 | tf_op jit(solution)/shard_map/ppermute | solution.py:1025
  30.2 29.7 %collective-permute-start.4 = (bf16[4,24,3200]{2,1,0:T(8,128)(2,1)S(1)}, bf16[4,24,3200]{2,1,0:T(8,128)(2,1)S(1)}, u32[]{:S(2)}, u32[]{:S(2)}) collective-permute-start(bf16[4,24,3200]{2,1,0:T(8,128)(2,1)S(1)} %bitcast_dynamic-update-slice_fusion.11), channel_id=1, source_target_pairs={{0,4},{4,0},{8,12},{12,8},{16,20},{20,16},{24,28},{28,24},{1,5},{5... | collective-permute-start | bytes 1843208 | tf_op jit(solution)/shard_map/ppermute | solution.py:1018
  31.8 29.7 %collective-permute-start.6 = (bf16[4,24,3200]{2,1,0:T(8,128)(2,1)S(1)}, bf16[4,24,3200]{2,1,0:T(8,128)(2,1)S(1)}, u32[]{:S(2)}, u32[]{:S(2)}) collective-permute-start(bf16[4,24,3200]{2,1,0:T(8,128)(2,1)S(1)} %bitcast_dynamic-update-slice_fusion.11), channel_id=1, source_target_pairs={{0,2},{1,3},{2,0},{3,1},{4,6},{5,7},{6,4},{7,5},{8,10},{9,11},{10,... | collective-permute-start | bytes 1843208 | tf_op jit(solution)/shard_map/ppermute | solution.py:1024
  33.3 86.5 %all-to-all-start.1 = ((bf16[4,256,768]{2,1,0:T(8,128)(2,1)}), bf16[4,256,768]{2,1,0:T(8,128)(2,1)S(1)}, u32[]{:S(2)}, u32[]{:S(2)}) async-start(bf16[4,256,768]{2,1,0:T(8,128)(2,1)} %bitcast.16), calls=%async_computation.1 | async-start | bytes 3145728 | tf_op jit(solution)/shard_map/all_to_all | solution.py:982
  36.9 287.7 %reduce-scatter.5.cloned.1.call-start = ((), (), s32[]{:S(2)}) async-start(), calls=%async_computation.10 | async-start | bytes 3538944 | tf_op jit(solution)/shard_map/reduce_scatter | solution.py:1083
  60.0 17.8 %collective-permute-start.5 = (bf16[4,24,3200]{2,1,0:T(8,128)(2,1)S(1)}, bf16[4,24,3200]{2,1,0:T(8,128)(2,1)S(1)}, u32[]{:S(2)}, u32[]{:S(2)}) collective-permute-start(bf16[4,24,3200]{2,1,0:T(8,128)(2,1)S(1)} %collective-permute-done.4), channel_id=1, source_target_pairs={{0,1},{1,0},{2,3},{3,2},{4,5},{5,4},{6,7},{7,6},{8,9},{9,8},{10,11... | collective-permute-start | bytes 1843208 | tf_op jit(solution)/shard_map/ppermute | solution.py:1025
  60.0 17.8 %collective-permute-start.8 = (bf16[4,24,3200]{2,1,0:T(8,128)(2,1)S(1)}, bf16[4,24,3200]{2,1,0:T(8,128)(2,1)S(1)}, u32[]{:S(2)}, u32[]{:S(2)}) collective-permute-start(bf16[4,24,3200]{2,1,0:T(8,128)(2,1)S(1)} %collective-permute-done.4), channel_id=1, source_target_pairs={{0,2},{1,3},{2,0},{3,1},{4,6},{5,7},{6,4},{7,5},{8,10},{9,11},{10,... | collective-permute-start | bytes 1843208 | tf_op jit(solution)/shard_map/ppermute | solution.py:1024
  61.5 16.5 %collective-permute-start.7 = (bf16[4,24,3200]{2,1,0:T(8,128)(2,1)S(1)}, bf16[4,24,3200]{2,1,0:T(8,128)(2,1)S(1)}, u32[]{:S(2)}, u32[]{:S(2)}) collective-permute-start(bf16[4,24,3200]{2,1,0:T(8,128)(2,1)S(1)} %collective-permute-done.6), channel_id=1, source_target_pairs={{0,1},{1,0},{2,3},{3,2},{4,5},{5,4},{6,7},{7,6},{8,9},{9,8},{10,11... | collective-permute-start | bytes 1843208 | tf_op jit(solution)/shard_map/ppermute | solution.py:1025
  77.7 2.0 collective-permute-start.9
  119.8 27.5 %copy-start.5 = (bf16[4,256,768]{2,1,0:T(8,128)(2,1)}, bf16[4,256,768]{2,1,0:T(8,128)(2,1)S(1)}, u32[]{:S(2)}) copy-start(bf16[4,256,768]{2,1,0:T(8,128)(2,1)S(1)} %all-to-all-done.1) | copy-start | bytes 4718596
  175.3 14.5 %all-to-all-start.2 = ((f32[4,1,256]{2,1,0:T(1,128)}), f32[4,1,256]{2,1,0:T(1,128)S(1)}, u32[]{:S(2)}, u32[]{:S(2)}) async-start(f32[4,1,256]{2,1,0:T(1,128)} %bitcast.46), calls=%async_computation.2 | async-start | bytes 8192 | tf_op jit(solution)/shard_map/all_to_all | solution.py:982
  189.8 15.3 %copy-start.17 = (f32[4,1,256]{2,1,0:T(1,128)}, f32[4,1,256]{2,1,0:T(1,128)S(1)}, u32[]{:S(2)}) copy-start(f32[4,1,256]{2,1,0:T(1,128)S(1)} %all-to-all-done.2) | copy-start | bytes 12292
  189.8 23.6 %all-to-all-start.3 = ((bf16[4,256,768]{2,1,0:T(8,128)(2,1)}), bf16[4,256,768]{2,1,0:T(8,128)(2,1)S(1)}, u32[]{:S(2)}, u32[]{:S(2)}) async-start(bf16[4,256,768]{2,1,0:T(8,128)(2,1)} %bitcast.155), calls=%async_computation.3 | async-start | bytes 3145728 | tf_op jit(solution)/shard_map/all_to_all | solution.py:982
  193.3 138.0 %reduce-scatter.3.cloned.1.call-start = ((), (), s32[]{:S(2)}) async-start(), calls=%async_computation.9 | async-start | bytes 7077888 | tf_op jit(solution)/shard_map/reduce_scatter | solution.py:1083
  229.0 2.4 collective-permute-start.10
  232.7 36.6 %collective-permute-start.11 = (bf16[8,24,896]{2,1,0:T(8,128)(2,1)S(1)}, bf16[8,24,896]{2,1,0:T(8,128)(2,1)S(1)}, u32[]{:S(2)}, u32[]{:S(2)}) collective-permute-start(bf16[8,24,896]{2,1,0:T(8,128)(2,1)S(1)} %dynamic-slice_bitcast_fusion.4), channel_id=1, source_target_pairs={{0,2},{1,3},{2,0},{3,1},{4,6},{5,7},{6,4},{7,5},{8,10},{9,11},{10,... | collective-permute-start | bytes 1032200 | tf_op jit(solution)/shard_map/ppermute | solution.py:1049
  270.2 3.9 %collective-permute-start.12 = (bf16[16,24,2304]{2,1,0:T(8,128)(2,1)}, bf16[16,24,2304]{2,1,0:T(8,128)(2,1)S(1)}, u32[]{:S(2)}, u32[]{:S(2)}) collective-permute-start(bf16[16,24,2304]{2,1,0:T(8,128)(2,1)} %get-tuple-element.146), channel_id=1, source_target_pairs={{0,1},{1,0},{2,3},{3,2},{4,5},{5,4},{6,7},{7,6},{8,9},{9,8},{10,11... | collective-permute-start | bytes 5308424 | tf_op jit(solution)/shard_map/ppermute | solution.py:1044
  277.0 22.0 %collective-permute-start.13 = (bf16[8,24,2304]{2,1,0:T(8,128)(2,1)}, bf16[8,24,2304]{2,1,0:T(8,128)(2,1)}, u32[]{:S(2)}, u32[]{:S(2)}) collective-permute-start(bf16[8,24,2304]{2,1,0:T(8,128)(2,1)} %dynamic-slice_bitcast_fusion), channel_id=1, source_target_pairs={{0,2},{1,3},{2,0},{3,1},{4,6},{5,7},{6,4},{7,5},{8,10},{9,11},{10,... | collective-permute-start | bytes 2654216 | tf_op jit(solution)/shard_map/ppermute | solution.py:1049
  278.7 22.6 %all-to-all-start.4 = ((bf16[8,24,896]{2,1,0:T(8,128)(2,1)}), bf16[8,24,896]{2,1,0:T(8,128)(2,1)S(1)}, u32[]{:S(2)}, u32[]{:S(2)}) async-start(bf16[8,24,896]{2,1,0:T(8,128)(2,1)} %fusion.5), calls=%async_computation.4 | async-start | bytes 688128 | tf_op jit(solution)/shard_map/all_to_all | solution.py:982
  301.3 10.6 %copy-start.8 = (bf16[8,24,896]{2,1,0:T(8,128)(2,1)}, bf16[8,24,896]{2,1,0:T(8,128)(2,1)S(1)}, u32[]{:S(2)}) copy-start(bf16[8,24,896]{2,1,0:T(8,128)(2,1)S(1)} %all-to-all-done.4.shares_ref) | copy-start | bytes 1032196
  301.3 30.0 %all-to-all-start.5 = ((bf16[8,24,2304]{2,1,0:T(8,128)(2,1)}), bf16[8,24,2304]{2,1,0:T(8,128)(2,1)S(1)}, u32[]{:S(2)}, u32[]{:S(2)}) async-start(bf16[8,24,2304]{2,1,0:T(8,128)(2,1)} %fusion.4), calls=%async_computation.5 | async-start | bytes 1769472 | tf_op jit(solution)/shard_map/all_to_all | solution.py:982
  311.9 12.7 %collective-permute-start.14 = (bf16[256,768]{1,0:T(8,128)(2,1)}, bf16[256,768]{1,0:T(8,128)(2,1)S(1)}, u32[]{:S(2)}, u32[]{:S(2)}) collective-permute-start(bf16[256,768]{1,0:T(8,128)(2,1)} %get-tuple-element.207), channel_id=1, source_target_pairs={{0,1},{1,2},{2,3},{3,0},{4,5},{5,6},{6,7},{7,4},{8,9},{9,10},{10,1... | collective-permute-start | bytes 1179656 | tf_op jit(solution)/shard_map/ppermute | solution.py:991
  311.9 27.0 %collective-permute-start.15 = (bf16[256,768]{1,0:T(8,128)(2,1)}, bf16[256,768]{1,0:T(8,128)(2,1)S(1)}, u32[]{:S(2)}, u32[]{:S(2)}) collective-permute-start(bf16[256,768]{1,0:T(8,128)(2,1)} %get-tuple-element.206), channel_id=1, source_target_pairs={{0,2},{1,3},{2,0},{3,1},{4,6},{5,7},{6,4},{7,5},{8,10},{9,11},{10,... | collective-permute-start | bytes 1179656 | tf_op jit(solution)/shard_map/ppermute | solution.py:991
  323.2 15.8 %collective-permute-start.16 = (bf16[256,768]{1,0:T(8,128)(2,1)}, bf16[256,768]{1,0:T(8,128)(2,1)}, u32[]{:S(2)}, u32[]{:S(2)}) collective-permute-start(bf16[256,768]{1,0:T(8,128)(2,1)} %get-tuple-element.205), channel_id=1, source_target_pairs={{0,3},{1,0},{2,1},{3,2},{4,7},{5,4},{6,5},{7,6},{8,11},{9,8},{10,9... | collective-permute-start | bytes 1179656 | tf_op jit(solution)/shard_map/ppermute | solution.py:991
  335.3 13.8 %all-to-all-start.6 = ((f32[32,1,1024]{2,1,0:T(1,128)}), f32[32,1,1024]{2,1,0:T(1,128)S(1)}, u32[]{:S(2)}, u32[]{:S(2)}) async-start(f32[32,1,1024]{2,1,0:T(1,128)} %get-tuple-element.160), calls=%async_computation.8 | async-start | bytes 262144 | tf_op jit(solution)/shard_map/all_to_all | solution.py:982
  (14 other events, 26.1 us)
Sparse Core Ops, SparseCore 0:
  10.7 112.9 all-gather.2
  175.4 41.3 reduce-scatter.4
  219.1 68.1 reduce-scatter.2

commit v2 on v1

--- a/solution.py
+++ b/solution.py
@@ -36,7 +36,6 @@
 CHOSEN, COEF, SCALE, REST, BETA, GATE_GRAD, PROBS = 0, 2, 3, 4, 8, 16, 32
 PIECES = 3
 HINT = 64
-UPDATE_STEPS = 4
 
 
 def dot(left, right, form=NN):
@@ -172,7 +171,8 @@
     out_ref,
     *refs,
 ):
-    weight_refs, (bias_ref, key_sum, value_sum, turned, total) = refs[:-5], refs[-5:]
+    weight_refs, (bias_ref, key_sum, value_sum, turned, total, kept) = refs[:-6], refs[-6:]
+    pair = pl.program_id(0)
     length, block = seg_row_ref.shape[1], BLOCK
 
     @pl.when(pl.program_id(0) == 0)
@@ -221,12 +221,18 @@
     gradients(*before)
     out_ref[1] = key_sum[...].astype(BF16)
     out_ref[2] = value_sum[...].astype(BF16)
-    weights = dot(turned[...], jnp.concatenate([out_ref[part] for part in range(3)], axis=1))
-    if len(weight_refs) == 1:
-        weight_refs[0][...] = weights.astype(BF16)
-    else:
-        total[...] = weights
-        part_rows(total, core_ref[0], *weight_refs)
+    for part in range(3):
+        kept[pair % 2, part] = out_ref[part]
+
+    @pl.when(pair % 2 == 1)
+    def _():
+        both = jnp.concatenate([kept[which, part] for which in range(2) for part in range(3)], axis=1)
+        weights = dot(turned[...], both)
+        if len(weight_refs) == 1:
+            weight_refs[0][...] = weights.astype(BF16)
+        else:
+            total[...] = weights
+            part_rows(total, core_ref[0], *weight_refs)
 
 
 def attend_backward(core, packed, grad, logsum, seg_column, seg_row, normed, shards):
@@ -236,10 +242,10 @@
     spec = lambda shape, place: pl.BlockSpec(shape, lambda pair, core: place(pair))
     always = lambda shape: spec(shape, lambda pair: (0,) * len(shape))
     if rows % 8:
-        weight_specs = [spec((D, 3 * PAIR), lambda pair: (0, pair))]
+        weight_specs = [spec((D, 6 * PAIR), lambda pair: (0, pair // 2))]
         weight_shapes = [jax.ShapeDtypeStruct((D, 3 * D), BF16)]
     else:
-        weight_specs = [spec((shards // 2, rows, 3 * PAIR), lambda pair: (0, 0, pair))] * 2
+        weight_specs = [spec((shards // 2, rows, 6 * PAIR), lambda pair: (0, 0, pair // 2))] * 2
         weight_shapes = [jax.ShapeDtypeStruct((shards // 2, rows, 3 * D), BF16)] * 2
     results = pl.pallas_call(
         attend_backward_kernel,
@@ -262,7 +268,8 @@
                 pltpu.VMEM((length, PAIR), F32),
                 pltpu.VMEM((length, PAIR), F32),
                 pltpu.VMEM((D, length), BF16),
-                pltpu.VMEM((D, 3 * PAIR), F32),
+                pltpu.VMEM((D, 6 * PAIR), F32),
+                pltpu.VMEM((2, 3, length, PAIR), BF16),
             ],
         ),
         out_shape=[jax.ShapeDtypeStruct((3, length, D), BF16), *weight_shapes],
@@ -734,7 +741,7 @@
         ],
         out_specs=token_block(D),
         out_shape=jax.ShapeDtypeStruct((tokens, D), BF16),
-        compiler_params=params(),
+        compiler_params=params(62),
         cost_estimate=cost(4 * tokens * D * slots, 12 * tokens * D),
         name="mix_branches",
     )(returned, targets, table, middle, normed, gathered)
@@ -908,7 +915,7 @@
             jax.ShapeDtypeStruct((kinds, kinds), F32),
         ]
         + [jax.ShapeDtypeStruct(shape, BF16) for shape in weights],
-        compiler_params=params(),
+        compiler_params=params(62),
         cost_estimate=cost(2 * tokens * D * (slots + 2 * D), 18 * tokens * D),
         name="middle_backward",
     )(
@@ -1123,7 +1130,7 @@
             jax.ShapeDtypeStruct(outer.shape, F32),
             jax.ShapeDtypeStruct((devices, 1, width), F32),
         ],
-        compiler_params=params(),
+        compiler_params=params(62),
         cost_estimate=cost(6 * D * FF, 3 * D * FF),
         name="own_sums",
     )(in_shares, out_shares, inner, outer, grad_gain, grad_mixer)
@@ -1193,7 +1200,7 @@
 
 
 def update(index, few, in_own, out_own, inner_own, outer_own, states, kinds, constant_count):
-    steps = UPDATE_STEPS
+    steps = 2
     turn = lambda which, array: array.T if which in (2, 4) else array
     states = [[turn(which, array) for array in state] for which, state in enumerate(states)]
     half = steps // 2
@@ -1304,11 +1311,13 @@
     target_rows = targets.T
     split = (groups, slots // groups, -1)
     placed = place_rows(cotangent, target_rows, slots).reshape(split)
+    mine, expert_pieces = lax.optimization_barrier((mine, expert_pieces))
     column = gather_far(mine)
-    column, placed = lax.optimization_barrier((column, placed))
+    column, placed, expert_pieces = lax.optimization_barrier((column, placed, expert_pieces))
     gathered = gather_all(column)
     expert_inner, expert_outer = gather_experts(expert_pieces)
     gains = gathered[:, 4 * D + small_width : 4 * D + small_width + 2].astype(F32).T
+    gains, placed = lax.optimization_barrier((gains, placed))
     gain_first, gain_second = gains[0:1], gains[1:2]
     arrived_grad = exchange(placed, "expert").reshape(slots, D)
     route_rows = routes.T

time: 373 us -> 369 us (0.989)
  waiting for transfers between devices: 74.4 us -> 69.2 us
    another operation x3 -> x5, other arithmetic: 0.03 us -> 4.01 us
    unnamed x45 -> x31, local copies, waits for them, and re-layouts: 8.01 us -> 6.77 us
where the time goes in v2:
time: 369 us; the launch traced here: 364 us
  Pallas kernels  172 us (47%)
  waiting for transfers between devices  69.2 us (19%)
  starting transfers between devices  49.9 us (14%)
  blocking collectives  27.6 us (7%)
  local copies, waits for them, and re-layouts  17.6 us (5%)
  between operations  14.7 us (4%)
  other arithmetic  10.6 us (3%)
    pallas_call x1, Pallas kernels, attend_backward(): pl.pallas_call(attend_backward_kernel, grid_spec=pltpu.PrefetchScalarGrid...  34.5 us
    all_to_all x6, starting transfers between devices, exchange(): return lax.all_to_all(blocks, axis, split_axis=0, concat_axis=0, tiled=True)  32.1 us
    all_to_all x1, blocking collectives, exchange(): return lax.all_to_all(blocks, axis, split_axis=0, concat_axis=0, tiled=True)  27.6 us
    pallas_call x1, Pallas kernels, attend_forward(): pl.pallas_call(attend_forward_kernel, grid=(pairs,), in_specs=[whole((len...  24.8 us
    pallas_call x1, Pallas kernels, expert_forward(): pl.pallas_call(functools.partial(expert_kernel, outers=len(outers)), grid...  20.8 us
    ppermute x1, waiting for transfers between devices, gather_all(): near = [column, lax.ppermute(column, 'dp', flip('dp'))]  19.2 us
    all_to_all x6, waiting for transfers between devices, exchange(): return lax.all_to_all(blocks, axis, split_axis=0, concat_axis=0, tiled=True)  15.2 us
    ppermute x2, waiting for transfers between devices, gather_all(): piece = lax.ppermute(piece, 'expert', shift('expert', step))  14.6 us
  transfers between devices with their start and end apart: 26, of which 9 were waited for; matrix products, arithmetic and copies ran while one was open for 5% of the time, Pallas kernels for 37%

profile of v2, /device:TPU:0, one launch (start us, length us, event | category | flops | bytes accessed | tf_op | source)
XLA Modules:
  0.0 363.6 jit_solution(1049664260273868390)
XLA Ops:
  14.8 3.1 collective-permute-start
  17.9 2.6 collective-permute-start.1
  24.8 4.8 %place_rows.1 = bf16[1024,768]{1,0:T(8,128)(2,1)} custom-call(bf16[1024,768]{1,0:T(8,128)(2,1)} %upstream_ref.3, s32[2,1024]{1,0:T(2,128)} %copy.196.targets_ref), custom_call_target="tpu_custom_call" | custom-call | flops 25165824 | bytes 49152 | tf_op jit(solution)/shard_map/place_rows/pallas_call | solution.py:405
  34.3 19.2 %collective-permute-done.4 = bf16[4,24,3200]{2,1,0:T(8,128)(2,1)S(1)} collective-permute-done((bf16[4,24,3200]{2,1,0:T(8,128)(2,1)S(1)}, bf16[4,24,3200]{2,1,0:T(8,128)(2,1)S(1)}, u32[]{:S(2)}, u32[]{:S(2)}) %collective-permute-start.4) | collective-permute-done | bytes 614432 | tf_op jit(solution)/shard_map/ppermute | solution.py:1025
  55.2 14.6 %collective-permute-done.8 = bf16[4,24,3200]{2,1,0:T(8,128)(2,1)S(1)} collective-permute-done((bf16[4,24,3200]{2,1,0:T(8,128)(2,1)S(1)}, bf16[4,24,3200]{2,1,0:T(8,128)(2,1)S(1)}, u32[]{:S(2)}, u32[]{:S(2)}) %collective-permute-start.8) | collective-permute-done | bytes 614432 | tf_op jit(solution)/shard_map/ppermute | solution.py:1031
  71.9 2.2 copy-done
  74.4 3.7 %all-to-all-start.1 = ((bf16[4,256,768]{2,1,0:T(8,128)(2,1)}), bf16[4,256,768]{2,1,0:T(8,128)(2,1)S(1)}, u32[]{:S(2)}, u32[]{:S(2)}) async-start(bf16[4,256,768]{2,1,0:T(8,128)(2,1)} %bitcast.17), calls=%async_computation.1 | async-start | bytes 3145728 | tf_op jit(solution)/shard_map/all_to_all | solution.py:989
  81.2 24.8 %attend_forward.1 = (bf16[1024,768]{1,0:T(8,128)(2,1)}, bf16[3,1024,768]{2,1,0:T(8,128)(2,1)}, bf16[1024,768]{1,0:T(8,128)(2,1)}, f32[6,2,1024]{2,1,0:T(2,128)}) custom-call(bf16[1024,768]{1,0:T(8,128)(2,1)} %hidden_ref.5, f32[1,768]{1,0:T(1,128)} %get-tuple-element.222.gain_ref, bf16[768,3200]{1,0:T(8,128)(2,1)} %bitcast.134, bf16[768,3200]{1,0:T(8,128)(2,1)} %bitcast.135, ...), custom_call_target="tpu_custom_call" | custom-call | flops 100663296 | bytes 98304 | tf_op jit(solution)/shard_map/attend_forward/pallas_call | solution.py:122
  105.9 11.8 %route_tokens.1 = (f32[1024,768]{1,0:T(8,128)}, bf16[1024,768]{1,0:T(8,128)(2,1)}, f32[1024,128]{1,0:T(8,128)}, bf16[1024,896]{1,0:T(8,128)(2,1)}) custom-call(bf16[1024,768]{1,0:T(8,128)(2,1)} %hidden_ref.5, bf16[1024,768]{1,0:T(8,128)(2,1)} %get-tuple-element.134.attended_ref, bf16[1024,768]{1,0:T(8,128)(2,1)} %upstream_ref.3, f32[8,1024]{1,0:T(8,128)} %fusion.8.extra_ref, ...), custom_call_target="tpu_custom_call" | custom-call | flops 44040192 | bytes 245760 | tf_op jit(solution)/shard_map/route_tokens/pallas_call | solution.py:439
  117.8 27.6 %all_to_all.35 = bf16[4,256,896]{2,1,0:T(8,128)(2,1)} all-to-all(bf16[4,256,896]{2,1,0:T(8,128)(2,1)} %bitcast.159), channel_id=1, replica_groups=mesh['dp'=8,'expert'=4] {'expert'}, dimensions={0} | all-to-all | bytes 3670016 | tf_op jit(solution)/shard_map/all_to_all | solution.py:989
  145.4 20.8 %expert_forward.1 = (bf16[2,1024,2048]{2,1,0:T(8,128)(2,1)}, bf16[1024,2048]{1,0:T(8,128)(2,1)}, bf16[1024,768]{1,0:T(8,128)(2,1)}, f32[1,1024]{1,0:T(1,128)}, bf16[1024,768]{1,0:T(8,128)(2,1)}) custom-call(bf16[1024,896]{1,0:T(8,128)(2,1)} %bitcast.143, bf16[1024,768]{1,0:T(8,128)(2,1)} %bitcast.151, bf16[8,2304,256]{2,1,0:T(8,128)(2,1)} %bitcast.124, ...), custom_call_target="tpu_custom_call" | custom-call | flops 201326592 | bytes 344064 | tf_op jit(solution)/shard_map/expert_forward/pallas_call | solution.py:567
  166.2 7.2 %outer_weights.1 = bf16[8,256,768]{2,1,0:T(8,128)(2,1)} custom-call(bf16[1024,2048]{1,0:T(8,128)(2,1)} %get-tuple-element.166.refs_0_.refs_1_.refs_2_.refs_3_, bf16[1024,2048]{1,0:T(8,128)(2,1)} %get-tuple-element.166.refs_0_.refs_1_.refs_2_.refs_3_, bf16[1024,2048]{1,0:T(8,128)(2,1)} %get-tuple-element.166.refs_0_.refs_1_.refs_2_.refs_3_, ...), custom_call_target="tpu_custom_call" | custom-call | flops 50331648 | bytes 114688 | tf_op jit(solution)/shard_map/outer_weights/pallas_call | solution.py:613
  173.4 3.3 all-to-all-start.2
  176.7 11.2 %expert_backward.1 = bf16[1024,768]{1,0:T(8,128)(2,1)} custom-call(bf16[2,1024,2048]{2,1,0:T(8,128)(2,1)} %get-tuple-element.142.joined_ref, bf16[8,2304,256]{2,1,0:T(8,128)(2,1)} %bitcast.132), custom_call_target="tpu_custom_call" | custom-call | flops 100663296 | bytes 229376 | tf_op jit(solution)/shard_map/expert_backward/pallas_call | solution.py:678
  187.9 3.6 all-to-all-start.3
  191.8 11.5 %inner_weights.1 = bf16[8,2,96,2048]{3,2,1,0:T(8,128)(2,1)} custom-call(bf16[1024,896]{1,0:T(8,128)(2,1)} %bitcast.144, bf16[2,1024,2048]{2,1,0:T(8,128)(2,1)} %get-tuple-element.142.joined_ref), custom_call_target="tpu_custom_call" | custom-call | flops 100663296 | bytes 229376 | tf_op jit(solution)/shard_map/inner_weights/pallas_call | solution.py:647
  203.3 8.3 %all-to-all-done.3 = bf16[4,256,768]{2,1,0:T(8,128)(2,1)S(1)} async-done(((bf16[4,256,768]{2,1,0:T(8,128)(2,1)}), bf16[4,256,768]{2,1,0:T(8,128)(2,1)S(1)}, u32[]{:S(2)}, u32[]{:S(2)}) %all-to-all-start.3) | async-done | bytes 1572896 | tf_op jit(solution)/shard_map/all_to_all | solution.py:989
  212.7 14.4 %middle_backward.1 = (f32[1024,768]{1,0:T(8,128)}, bf16[1024,768]{1,0:T(8,128)(2,1)}, f32[8,8]{1,0:T(8,128)}, bf16[16,24,896]{2,1,0:T(8,128)(2,1)}, bf16[16,24,896]{2,1,0:T(8,128)(2,1)}) custom-call(s32[1]{0:T(128)} %bitcast.core_ref, bf16[1024,768]{1,0:T(8,128)(2,1)} %bitcast.148, f32[1,1024]{1,0:T(1,128)} %bitcast.173, s32[1024,2]{1,0:T(8,128)} %copy-done.1, ...), custom_call_target="tpu_custom_call" | custom-call | flops 62914560 | bytes 221184 | tf_op jit(solution)/shard_map/middle_backward/pallas_call | solution.py:883
  227.2 2.3 collective-permute-done.10
  231.2 34.5 %attend_backward.1 = (bf16[3,1024,768]{2,1,0:T(8,128)(2,1)}, bf16[16,24,2304]{2,1,0:T(8,128)(2,1)}, bf16[16,24,2304]{2,1,0:T(8,128)(2,1)}) custom-call(s32[1]{0:T(128)} %bitcast.core_ref, bf16[3,1024,768]{2,1,0:T(8,128)(2,1)} %get-tuple-element.133.query_ref.key_ref.value_ref, bf16[3,1024,768]{2,1,0:T(8,128)(2,1)} %get-tuple-element.133.query_ref.key_ref.value_ref, ...), custom_call_target="tpu_custom_call" | custom-call | flops 251658240 | bytes 172032 | tf_op jit(solution)/shard_map/attend_backward/pallas_call | solution.py:250
  266.5 3.9 %collective-permute-done.12 = bf16[16,24,2304]{2,1,0:T(8,128)(2,1)S(1)} collective-permute-done((bf16[16,24,2304]{2,1,0:T(8,128)(2,1)}, bf16[16,24,2304]{2,1,0:T(8,128)(2,1)S(1)}, u32[]{:S(2)}, u32[]{:S(2)}) %collective-permute-start.12) | collective-permute-done | bytes 1769504 | tf_op jit(solution)/shard_map/ppermute | solution.py:1051
  270.4 1.9 add_convert_fusion
  275.1 8.9 %all-to-all-start.4 = ((bf16[8,24,896]{2,1,0:T(8,128)(2,1)}), bf16[8,24,896]{2,1,0:T(8,128)(2,1)S(1)}, u32[]{:S(2)}, u32[]{:S(2)}) async-start(bf16[8,24,896]{2,1,0:T(8,128)(2,1)} %fusion.5), calls=%async_computation.4 | async-start | bytes 688128 | tf_op jit(solution)/shard_map/all_to_all | solution.py:989
  284.0 11.2 %collective-permute-done.13 = bf16[8,24,2304]{2,1,0:T(8,128)(2,1)S(1)} collective-permute-done((bf16[8,24,2304]{2,1,0:T(8,128)(2,1)}, bf16[8,24,2304]{2,1,0:T(8,128)(2,1)S(1)}, u32[]{:S(2)}, u32[]{:S(2)}) %collective-permute-start.13) | collective-permute-done | bytes 884768 | tf_op jit(solution)/shard_map/ppermute | solution.py:1056
  296.4 9.0 %all-to-all-start.5 = ((bf16[8,24,2304]{2,1,0:T(8,128)(2,1)}), bf16[8,24,2304]{2,1,0:T(8,128)(2,1)}, u32[]{:S(2)}, u32[]{:S(2)}) async-start(bf16[8,24,2304]{2,1,0:T(8,128)(2,1)} %fusion.4), calls=%async_computation.5 | async-start | bytes 1769472 | tf_op jit(solution)/shard_map/all_to_all | solution.py:989
  305.5 2.3 dynamic-slice_bitcast_fusion.1
  309.6 9.5 %input_backward.1 = (f32[1024,768]{1,0:T(8,128)}, f32[1,768]{1,0:T(1,128)}) custom-call(bf16[3,1024,768]{2,1,0:T(8,128)(2,1)} %get-tuple-element.160.packed_ref, bf16[768,3200]{1,0:T(8,128)(2,1)} %bitcast.141, bf16[1024,768]{1,0:T(8,128)(2,1)} %hidden_ref.5, f32[1024,768]{1,0:T(8,128)} %get-tuple-element.161.grad_middle_ref, ...), custom_call_target="tpu_custom_call" | custom-call | flops 56623104 | bytes 196608 | tf_op jit(solution)/shard_map/input_backward/pallas_call | solution.py:957
  320.5 6.9 %all-to-all-done.5.in_ref = bf16[8,24,2304]{2,1,0:T(8,128)(2,1)} async-done(((bf16[8,24,2304]{2,1,0:T(8,128)(2,1)}), bf16[8,24,2304]{2,1,0:T(8,128)(2,1)}, u32[]{:S(2)}, u32[]{:S(2)}) %all-to-all-start.5) | async-done | bytes 884768 | tf_op jit(solution)/shard_map/all_to_all | solution.py:989
  327.4 3.0 own_sums.1
  330.4 3.6 all-to-all-start.6
  337.3 7.9 %mix_branches.1 = bf16[1024,768]{1,0:T(8,128)(2,1)} custom-call(bf16[1024,768]{1,0:T(8,128)(2,1)} %bitcast.150, s32[1024,2]{1,0:T(8,128)} %copy-done.1, f32[1024,128]{1,0:T(8,128)} %get-tuple-element.145.table_ref, f32[1024,768]{1,0:T(8,128)} %get-tuple-element.146.middle_ref, bf16[1024,768]{1,0:T(8,128)(2,1)} %get-tuple-element.147.normed_ref, ...), custom_call_target="tpu_custom_call" | custom-call | flops 50331648 | bytes 147456 | tf_op jit(solution)/shard_map/mix_branches/pallas_call | solution.py:731
  345.9 10.9 %update.1 = (f32[1,1]{1,0:T(1,128)}, f32[24,2304]{1,0:T(8,128)}, f32[24,2304]{1,0:T(8,128)}, f32[24,2304]{1,0:T(8,128)}, bf16[24,2304]{1,0:T(8,128)(2,1)}, /*ind...) custom-call(s32[1]{0:T(128)} %bitcast.61.refs_0_, ...), custom_call_target="tpu_custom_call" | custom-call | flops 983040 | bytes 737280 | tf_op jit(solution)/shard_map/update/pallas_call | solution.py:1221
  (123 shorter events, 38.3 us)
Async XLA Ops:
  7.2 5.8 %copy-start.3 = (f32[1,96,4096]{2,1,0:T(8,128)S(1)}, f32[1,96,4096]{2,1,0:T(8,128)}, u32[]{:S(2)}) copy-start(f32[1,96,4096]{2,1,0:T(8,128)} %refs_24_.1) | copy-start | bytes 4718596
  7.2 138.1 %all-gather.3.cloned.1.call-start = ((), (), s32[]{:S(2)}) async-start(), calls=%async_computation.11 | async-start | bytes 10616832 | tf_op jit(solution)/shard_map/all_gather | solution.py:1083
  13.6 8.2 %copy-start.8 = (s32[1024,2]{0,1:T(2,128)S(1)}, s32[1024,2]{0,1:T(2,128)}, u32[]{:S(2)}) copy-start(s32[1024,2]{0,1:T(2,128)} %param.32) | copy-start | bytes 24580
  13.6 8.3 %copy-start.13 = (s32[1,1024]{1,0:T(1,128)S(1)}, s32[1,1024]{1,0:T(1,128)}, u32[]{:S(2)}) copy-start(s32[1,1024]{1,0:T(1,128)} %param.33) | copy-start | bytes 12292
  14.8 14.8 %collective-permute-start = (bf16[24,3200]{1,0:T(8,128)(2,1)S(1)}, bf16[24,3200]{1,0:T(8,128)(2,1)S(1)}, u32[]{:S(2)}, u32[]{:S(2)}) collective-permute-start(bf16[24,3200]{1,0:T(8,128)(2,1)S(1)} %concatenate.7), channel_id=1, source_target_pairs={{0,8},{4,12},{8,16},{12,20},{16,24},{20,28},{24,0},{28,4},{1,9},{5... | collective-permute-start | bytes 460808 | tf_op jit(solution)/shard_map/ppermute | solution.py:1016
  17.9 12.7 %collective-permute-start.1 = (bf16[24,3200]{1,0:T(8,128)(2,1)S(1)}, bf16[24,3200]{1,0:T(8,128)(2,1)S(1)}, u32[]{:S(2)}, u32[]{:S(2)}) collective-permute-start(bf16[24,3200]{1,0:T(8,128)(2,1)S(1)} %concatenate.7), channel_id=1, source_target_pairs={{0,16},{4,20},{8,24},{12,28},{16,0},{20,4},{24,8},{28,12},{1,17},{... | collective-permute-start | bytes 460808 | tf_op jit(solution)/shard_map/ppermute | solution.py:1016
  20.5 10.1 %collective-permute-start.2 = (bf16[24,3200]{1,0:T(8,128)(2,1)S(1)}, bf16[24,3200]{1,0:T(8,128)(2,1)S(1)}, u32[]{:S(2)}, u32[]{:S(2)}) collective-permute-start(bf16[24,3200]{1,0:T(8,128)(2,1)S(1)} %concatenate.7), channel_id=1, source_target_pairs={{0,24},{4,28},{8,0},{12,4},{16,8},{20,12},{24,16},{28,20},{1,25},{... | collective-permute-start | bytes 460808 | tf_op jit(solution)/shard_map/ppermute | solution.py:1016
  30.7 24.3 %collective-permute-start.3 = (bf16[4,24,3200]{2,1,0:T(8,128)(2,1)S(1)}, bf16[4,24,3200]{2,1,0:T(8,128)(2,1)S(1)}, u32[]{:S(2)}, u32[]{:S(2)}) collective-permute-start(bf16[4,24,3200]{2,1,0:T(8,128)(2,1)S(1)} %bitcast_dynamic-update-slice_fusion.11), channel_id=1, source_target_pairs={{0,1},{1,0},{2,3},{3,2},{4,5},{5,4},{6,7},{7,6},{8,9},{9,8},{10,11... | collective-permute-start | bytes 1843208 | tf_op jit(solution)/shard_map/ppermute | solution.py:1032
  30.8 22.7 %collective-permute-start.4 = (bf16[4,24,3200]{2,1,0:T(8,128)(2,1)S(1)}, bf16[4,24,3200]{2,1,0:T(8,128)(2,1)S(1)}, u32[]{:S(2)}, u32[]{:S(2)}) collective-permute-start(bf16[4,24,3200]{2,1,0:T(8,128)(2,1)S(1)} %bitcast_dynamic-update-slice_fusion.11), channel_id=1, source_target_pairs={{0,4},{4,0},{8,12},{12,8},{16,20},{20,16},{24,28},{28,24},{1,5},{5... | collective-permute-start | bytes 1843208 | tf_op jit(solution)/shard_map/ppermute | solution.py:1025
  32.4 22.4 %collective-permute-start.6 = (bf16[4,24,3200]{2,1,0:T(8,128)(2,1)S(1)}, bf16[4,24,3200]{2,1,0:T(8,128)(2,1)S(1)}, u32[]{:S(2)}, u32[]{:S(2)}) collective-permute-start(bf16[4,24,3200]{2,1,0:T(8,128)(2,1)S(1)} %bitcast_dynamic-update-slice_fusion.11), channel_id=1, source_target_pairs={{0,2},{1,3},{2,0},{3,1},{4,6},{5,7},{6,4},{7,5},{8,10},{9,11},{10,... | collective-permute-start | bytes 1843208 | tf_op jit(solution)/shard_map/ppermute | solution.py:1031
  53.5 16.3 %collective-permute-start.5 = (bf16[4,24,3200]{2,1,0:T(8,128)(2,1)S(1)}, bf16[4,24,3200]{2,1,0:T(8,128)(2,1)S(1)}, u32[]{:S(2)}, u32[]{:S(2)}) collective-permute-start(bf16[4,24,3200]{2,1,0:T(8,128)(2,1)S(1)} %collective-permute-done.4), channel_id=1, source_target_pairs={{0,1},{1,0},{2,3},{3,2},{4,5},{5,4},{6,7},{7,6},{8,9},{9,8},{10,11... | collective-permute-start | bytes 1843208 | tf_op jit(solution)/shard_map/ppermute | solution.py:1032
  53.5 16.3 %collective-permute-start.8 = (bf16[4,24,3200]{2,1,0:T(8,128)(2,1)S(1)}, bf16[4,24,3200]{2,1,0:T(8,128)(2,1)S(1)}, u32[]{:S(2)}, u32[]{:S(2)}) collective-permute-start(bf16[4,24,3200]{2,1,0:T(8,128)(2,1)S(1)} %collective-permute-done.4), channel_id=1, source_target_pairs={{0,2},{1,3},{2,0},{3,1},{4,6},{5,7},{6,4},{7,5},{8,10},{9,11},{10,... | collective-permute-start | bytes 1843208 | tf_op jit(solution)/shard_map/ppermute | solution.py:1031
  54.8 15.2 %collective-permute-start.7 = (bf16[4,24,3200]{2,1,0:T(8,128)(2,1)S(1)}, bf16[4,24,3200]{2,1,0:T(8,128)(2,1)S(1)}, u32[]{:S(2)}, u32[]{:S(2)}) collective-permute-start(bf16[4,24,3200]{2,1,0:T(8,128)(2,1)S(1)} %collective-permute-done.6), channel_id=1, source_target_pairs={{0,1},{1,0},{2,3},{3,2},{4,5},{5,4},{6,7},{7,6},{8,9},{9,8},{10,11... | collective-permute-start | bytes 1843208 | tf_op jit(solution)/shard_map/ppermute | solution.py:1032
  69.8 2.0 collective-permute-start.9
  74.4 43.4 %all-to-all-start.1 = ((bf16[4,256,768]{2,1,0:T(8,128)(2,1)}), bf16[4,256,768]{2,1,0:T(8,128)(2,1)S(1)}, u32[]{:S(2)}, u32[]{:S(2)}) async-start(bf16[4,256,768]{2,1,0:T(8,128)(2,1)} %bitcast.17), calls=%async_computation.1 | async-start | bytes 3145728 | tf_op jit(solution)/shard_map/all_to_all | solution.py:989
  78.1 242.4 %reduce-scatter.5.cloned.1.call-start = ((), (), s32[]{:S(2)}) async-start(), calls=%async_computation.10 | async-start | bytes 3538944 | tf_op jit(solution)/shard_map/reduce_scatter | solution.py:1090
  117.8 27.6 %copy-start.5 = (bf16[4,256,768]{2,1,0:T(8,128)(2,1)}, bf16[4,256,768]{2,1,0:T(8,128)(2,1)S(1)}, u32[]{:S(2)}) copy-start(bf16[4,256,768]{2,1,0:T(8,128)(2,1)S(1)} %all-to-all-done.1) | copy-start | bytes 4718596
  173.4 14.5 %all-to-all-start.2 = ((f32[4,1,256]{2,1,0:T(1,128)}), f32[4,1,256]{2,1,0:T(1,128)S(1)}, u32[]{:S(2)}, u32[]{:S(2)}) async-start(f32[4,1,256]{2,1,0:T(1,128)} %bitcast.42), calls=%async_computation.2 | async-start | bytes 8192 | tf_op jit(solution)/shard_map/all_to_all | solution.py:989
  187.9 15.3 %copy-start.12 = (f32[4,1,256]{2,1,0:T(1,128)}, f32[4,1,256]{2,1,0:T(1,128)S(1)}, u32[]{:S(2)}) copy-start(f32[4,1,256]{2,1,0:T(1,128)S(1)} %all-to-all-done.2) | copy-start | bytes 12292
  187.9 23.6 %all-to-all-start.3 = ((bf16[4,256,768]{2,1,0:T(8,128)(2,1)}), bf16[4,256,768]{2,1,0:T(8,128)(2,1)S(1)}, u32[]{:S(2)}, u32[]{:S(2)}) async-start(bf16[4,256,768]{2,1,0:T(8,128)(2,1)} %bitcast.149), calls=%async_computation.3 | async-start | bytes 3145728 | tf_op jit(solution)/shard_map/all_to_all | solution.py:989
  191.5 135.9 %reduce-scatter.3.cloned.1.call-start = ((), (), s32[]{:S(2)}) async-start(), calls=%async_computation.9 | async-start | bytes 7077888 | tf_op jit(solution)/shard_map/reduce_scatter | solution.py:1090
  227.1 2.4 collective-permute-start.10
  230.9 34.8 %collective-permute-start.11 = (bf16[8,24,896]{2,1,0:T(8,128)(2,1)S(1)}, bf16[8,24,896]{2,1,0:T(8,128)(2,1)S(1)}, u32[]{:S(2)}, u32[]{:S(2)}) collective-permute-start(bf16[8,24,896]{2,1,0:T(8,128)(2,1)S(1)} %dynamic-slice_bitcast_fusion.4), channel_id=1, source_target_pairs={{0,2},{1,3},{2,0},{3,1},{4,6},{5,7},{6,4},{7,5},{8,10},{9,11},{10,... | collective-permute-start | bytes 1032200 | tf_op jit(solution)/shard_map/ppermute | solution.py:1056
  266.5 3.9 %collective-permute-start.12 = (bf16[16,24,2304]{2,1,0:T(8,128)(2,1)}, bf16[16,24,2304]{2,1,0:T(8,128)(2,1)S(1)}, u32[]{:S(2)}, u32[]{:S(2)}) collective-permute-start(bf16[16,24,2304]{2,1,0:T(8,128)(2,1)} %get-tuple-element.156), channel_id=1, source_target_pairs={{0,1},{1,0},{2,3},{3,2},{4,5},{5,4},{6,7},{7,6},{8,9},{9,8},{10,11... | collective-permute-start | bytes 5308424 | tf_op jit(solution)/shard_map/ppermute | solution.py:1051
  273.3 21.9 %collective-permute-start.13 = (bf16[8,24,2304]{2,1,0:T(8,128)(2,1)}, bf16[8,24,2304]{2,1,0:T(8,128)(2,1)S(1)}, u32[]{:S(2)}, u32[]{:S(2)}) collective-permute-start(bf16[8,24,2304]{2,1,0:T(8,128)(2,1)} %dynamic-slice_bitcast_fusion), channel_id=1, source_target_pairs={{0,2},{1,3},{2,0},{3,1},{4,6},{5,7},{6,4},{7,5},{8,10},{9,11},{10,... | collective-permute-start | bytes 2654216 | tf_op jit(solution)/shard_map/ppermute | solution.py:1056
  275.1 21.3 %all-to-all-start.4 = ((bf16[8,24,896]{2,1,0:T(8,128)(2,1)}), bf16[8,24,896]{2,1,0:T(8,128)(2,1)S(1)}, u32[]{:S(2)}, u32[]{:S(2)}) async-start(bf16[8,24,896]{2,1,0:T(8,128)(2,1)} %fusion.5), calls=%async_computation.4 | async-start | bytes 688128 | tf_op jit(solution)/shard_map/all_to_all | solution.py:989
  296.4 11.4 %copy-start.6 = (bf16[8,24,896]{2,1,0:T(8,128)(2,1)}, bf16[8,24,896]{2,1,0:T(8,128)(2,1)S(1)}, u32[]{:S(2)}) copy-start(bf16[8,24,896]{2,1,0:T(8,128)(2,1)S(1)} %all-to-all-done.4.shares_ref) | copy-start | bytes 1032196
  296.4 31.0 %all-to-all-start.5 = ((bf16[8,24,2304]{2,1,0:T(8,128)(2,1)}), bf16[8,24,2304]{2,1,0:T(8,128)(2,1)}, u32[]{:S(2)}, u32[]{:S(2)}) async-start(bf16[8,24,2304]{2,1,0:T(8,128)(2,1)} %fusion.4), calls=%async_computation.5 | async-start | bytes 1769472 | tf_op jit(solution)/shard_map/all_to_all | solution.py:989
  307.8 12.7 %collective-permute-start.14 = (bf16[256,768]{1,0:T(8,128)(2,1)S(1)}, bf16[256,768]{1,0:T(8,128)(2,1)S(1)}, u32[]{:S(2)}, u32[]{:S(2)}) collective-permute-start(bf16[256,768]{1,0:T(8,128)(2,1)S(1)} %get-tuple-element.217), channel_id=1, source_target_pairs={{0,1},{1,2},{2,3},{3,0},{4,5},{5,6},{6,7},{7,4},{8,9},{9,10},{10,1... | collective-permute-start | bytes 1179656 | tf_op jit(solution)/shard_map/ppermute | solution.py:998
  307.8 26.3 %collective-permute-start.15 = (bf16[256,768]{1,0:T(8,128)(2,1)}, bf16[256,768]{1,0:T(8,128)(2,1)}, u32[]{:S(2)}, u32[]{:S(2)}) collective-permute-start(bf16[256,768]{1,0:T(8,128)(2,1)} %get-tuple-element.216), channel_id=1, source_target_pairs={{0,2},{1,3},{2,0},{3,1},{4,6},{5,7},{6,4},{7,5},{8,10},{9,11},{10,... | collective-permute-start | bytes 1179656 | tf_op jit(solution)/shard_map/ppermute | solution.py:998
  319.1 16.0 %collective-permute-start.16 = (bf16[256,768]{1,0:T(8,128)(2,1)}, bf16[256,768]{1,0:T(8,128)(2,1)}, u32[]{:S(2)}, u32[]{:S(2)}) collective-permute-start(bf16[256,768]{1,0:T(8,128)(2,1)} %get-tuple-element.215), channel_id=1, source_target_pairs={{0,3},{1,0},{2,1},{3,2},{4,7},{5,4},{6,5},{7,6},{8,11},{9,8},{10,9... | collective-permute-start | bytes 1179656 | tf_op jit(solution)/shard_map/ppermute | solution.py:998
  330.4 14.8 %all-to-all-start.6 = ((f32[32,1,1024]{2,1,0:T(1,128)}), f32[32,1,1024]{2,1,0:T(1,128)S(1)}, u32[]{:S(2)}, u32[]{:S(2)}) async-start(f32[32,1,1024]{2,1,0:T(1,128)} %get-tuple-element.170), calls=%async_computation.8 | async-start | bytes 262144 | tf_op jit(solution)/shard_map/all_to_all | solution.py:989
  (8 other events, 25.9 us)
Sparse Core Ops, SparseCore 0:
  30.8 105.3 all-gather.2
  173.5 42.4 reduce-scatter.4
  218.4 68.1 reduce-scatter.2

commit v3 on v2

--- a/solution.py
+++ b/solution.py
@@ -692,26 +692,26 @@
 
 
 def mix_kernel(
-    returned_ref,
     targets_ref,
     table_ref,
     middle_ref,
     normed_ref,
     small_ref,
-    out_ref,
-    *,
+    *refs,
     value_place,
     constant_count,
 ):
     block = middle_ref.shape[0]
-    slots = returned_ref.shape[0]
+    *returned_refs, out_ref = refs
+    returned = jnp.concatenate([ref[...] for ref in returned_refs], axis=0)
+    slots = returned.shape[0]
     table = table_ref[...]
     columns = iota((block, slots), 1)
     lane = iota((block, LANES), 1)
     blended = normed_ref[...].astype(F32) * table[:, COEF : COEF + 1]
     for route in range(2):
         hot = jnp.where(columns == targets_ref[:, route : route + 1], 1.0, 0.0).astype(BF16)
-        paired = dot(hot, returned_ref[...])
+        paired = dot(hot, returned)
         blended = blended + table[:, CHOSEN + route : CHOSEN + route + 1] * paired
     values = jnp.zeros((block, LANES), F32)
     for which in range(constant_count):
@@ -726,25 +726,25 @@
 def mix_branches(returned, targets, table, middle, normed, gathered, value_place, constant_count):
     block = TOKENS["mix"]
     tokens = middle.shape[0]
-    slots = returned.shape[0]
+    slots = sum(block.shape[0] for block in returned)
     token_block = lambda width: pl.BlockSpec((block, width), lambda step: (step, 0))
     return pl.pallas_call(
         functools.partial(mix_kernel, value_place=value_place, constant_count=constant_count),
         grid=(tokens // block,),
         in_specs=[
-            whole((slots, D)),
             token_block(2),
             token_block(LANES),
             token_block(D),
             token_block(D),
             pl.BlockSpec((D, LANES), lambda step: (0, 4 * D // LANES)),
+            *[whole(array.shape) for array in returned],
         ],
         out_specs=token_block(D),
         out_shape=jax.ShapeDtypeStruct((tokens, D), BF16),
         compiler_params=params(62),
         cost_estimate=cost(4 * tokens * D * slots, 12 * tokens * D),
         name="mix_branches",
-    )(returned, targets, table, middle, normed, gathered)
+    )(targets, table, middle, normed, gathered, *returned)
 
 
 def middle_kernel(
@@ -991,13 +991,13 @@
 
 def exchange_apart(blocks, axis):
     count, me = lax.axis_size(axis), lax.axis_index(axis)
-    out = jnp.zeros_like(blocks)
+    came = []
     for step in range(count):
         block = pick(blocks, (me + step) % count, 0)
         if step:
             block = lax.ppermute(block, axis, [(i, (i + step) % count) for i in range(count)])
-        out = lax.dynamic_update_slice(out, block[None], ((me - step) % count,) + (0,) * block.ndim)
-    return out
+        came.append(block)
+    return came
 
 
 def flip(axis):
@@ -1309,6 +1309,10 @@
     ).astype(BF16)
     targets = pair_targets(routes, priority[0], experts, kinds, capacity)
     target_rows = targets.T
+    away = (lax.axis_index("expert") - targets // (slots // groups)) % groups
+    near_targets = jnp.where(
+        targets < slots, away * (slots // groups) + targets % (slots // groups), slots
+    )
     split = (groups, slots // groups, -1)
     placed = place_rows(cotangent, target_rows, slots).reshape(split)
     mine, expert_pieces = lax.optimization_barrier((mine, expert_pieces))
@@ -1382,13 +1386,16 @@
     in_sum = scatter_side(grad_weight_in)
     out_shares = exchange(out_sum, "dp")
     in_sum, out_shares, produced = lax.optimization_barrier((in_sum, out_shares, produced))
-    returned = exchange_apart(produced.reshape(split), "expert").reshape(slots, D)
+    returned = exchange_apart(produced.reshape(split), "expert")
+    share = slots // groups
+    if share % 16:
+        returned = [jnp.concatenate(returned, axis=0)]
     in_shares = exchange(in_sum, "dp")
     input_grad, grad_gain_first = input_backward(
         grad_packed, gathered, hidden_in, grad_middle, gain_first
     )
     activations = mix_branches(
-        returned, targets, table, middle, normed_second, gathered, gate_end, constant_count
+        returned, near_targets, table, middle, normed_second, gathered, gate_end, constant_count
     )
 
     in_own, out_own, outer_own, few = own_sums(

time: 369 us -> 369 us (level)
  no operation moved by 1% of the time
where the time goes in v3:
time: 369 us; the launch traced here: 363 us
  Pallas kernels  172 us (47%)
  waiting for transfers between devices  70.3 us (19%)
  starting transfers between devices  47.7 us (13%)
  blocking collectives  27.5 us (7%)
  local copies, waits for them, and re-layouts  15.2 us (4%)
  between operations  14.9 us (4%)
  other arithmetic  13.3 us (4%)
    pallas_call x1, Pallas kernels, attend_backward(): pl.pallas_call(attend_backward_kernel, grid_spec=pltpu.PrefetchScalarGrid...  34.4 us
    all_to_all x6, starting transfers between devices, exchange(): return lax.all_to_all(blocks, axis, split_axis=0, concat_axis=0, tiled=True)  29.8 us
    all_to_all x1, blocking collectives, exchange(): return lax.all_to_all(blocks, axis, split_axis=0, concat_axis=0, tiled=True)  27.5 us
    pallas_call x1, Pallas kernels, attend_forward(): pl.pallas_call(attend_forward_kernel, grid=(pairs,), in_specs=[whole((len...  24.8 us
    pallas_call x1, Pallas kernels, expert_forward(): pl.pallas_call(functools.partial(expert_kernel, outers=len(outers)), grid...  20.8 us
    ppermute x1, waiting for transfers between devices, gather_all(): near = [column, lax.ppermute(column, 'dp', flip('dp'))]  19.8 us
    all_to_all x6, waiting for transfers between devices, exchange(): return lax.all_to_all(blocks, axis, split_axis=0, concat_axis=0, tiled=True)  15.6 us
    ppermute x2, waiting for transfers between devices, gather_all(): piece = lax.ppermute(piece, 'expert', shift('expert', step))  14.6 us
  transfers between devices with their start and end apart: 26, of which 9 were waited for; matrix products, arithmetic and copies ran while one was open for 5% of the time, Pallas kernels for 37%

profile of v3, /device:TPU:0, one launch (start us, length us, event | category | flops | bytes accessed | tf_op | source)
XLA Modules:
  0.0 362.8 jit_solution(1973372754942149861)
XLA Ops:
  14.8 3.1 collective-permute-start
  17.9 2.6 collective-permute-start.1
  26.3 4.8 %place_rows.1 = bf16[1024,768]{1,0:T(8,128)(2,1)} custom-call(bf16[1024,768]{1,0:T(8,128)(2,1)} %upstream_ref.3, s32[2,1024]{1,0:T(2,128)} %copy.199.targets_ref), custom_call_target="tpu_custom_call" | custom-call | flops 25165824 | bytes 49152 | tf_op jit(solution)/shard_map/place_rows/pallas_call | solution.py:405
  34.9 19.8 %collective-permute-done.4 = bf16[4,24,3200]{2,1,0:T(8,128)(2,1)S(1)} collective-permute-done((bf16[4,24,3200]{2,1,0:T(8,128)(2,1)S(1)}, bf16[4,24,3200]{2,1,0:T(8,128)(2,1)S(1)}, u32[]{:S(2)}, u32[]{:S(2)}) %collective-permute-start.4) | collective-permute-done | bytes 614432 | tf_op jit(solution)/shard_map/ppermute | solution.py:1025
  56.4 14.6 %collective-permute-done.8 = bf16[4,24,3200]{2,1,0:T(8,128)(2,1)S(1)} collective-permute-done((bf16[4,24,3200]{2,1,0:T(8,128)(2,1)S(1)}, bf16[4,24,3200]{2,1,0:T(8,128)(2,1)S(1)}, u32[]{:S(2)}, u32[]{:S(2)}) %collective-permute-start.8) | collective-permute-done | bytes 614432 | tf_op jit(solution)/shard_map/ppermute | solution.py:1031
  73.1 2.2 copy-done
  75.6 3.6 all-to-all-start.1
  82.2 24.8 %attend_forward.1 = (bf16[1024,768]{1,0:T(8,128)(2,1)}, bf16[3,1024,768]{2,1,0:T(8,128)(2,1)}, bf16[1024,768]{1,0:T(8,128)(2,1)}, f32[6,2,1024]{2,1,0:T(2,128)}) custom-call(bf16[1024,768]{1,0:T(8,128)(2,1)} %hidden_ref.5, f32[1,768]{1,0:T(1,128)} %get-tuple-element.224.gain_ref, bf16[768,3200]{1,0:T(8,128)(2,1)} %bitcast.129, bf16[768,3200]{1,0:T(8,128)(2,1)} %bitcast.130, ...), custom_call_target="tpu_custom_call" | custom-call | flops 100663296 | bytes 98304 | tf_op jit(solution)/shard_map/attend_forward/pallas_call | solution.py:122
  107.0 11.9 %route_tokens.1 = (f32[1024,768]{1,0:T(8,128)}, bf16[1024,768]{1,0:T(8,128)(2,1)}, f32[1024,128]{1,0:T(8,128)}, bf16[1024,896]{1,0:T(8,128)(2,1)}) custom-call(bf16[1024,768]{1,0:T(8,128)(2,1)} %hidden_ref.5, bf16[1024,768]{1,0:T(8,128)(2,1)} %get-tuple-element.133.attended_ref, bf16[1024,768]{1,0:T(8,128)(2,1)} %upstream_ref.3, ...), custom_call_target="tpu_custom_call" | custom-call | flops 44040192 | bytes 245760 | tf_op jit(solution)/shard_map/route_tokens/pallas_call | solution.py:439
  118.8 27.5 %all_to_all.35 = bf16[4,256,896]{2,1,0:T(8,128)(2,1)} all-to-all(bf16[4,256,896]{2,1,0:T(8,128)(2,1)} %bitcast.153), channel_id=1, replica_groups=mesh['dp'=8,'expert'=4] {'expert'}, dimensions={0} | all-to-all | bytes 3670016 | tf_op jit(solution)/shard_map/all_to_all | solution.py:989
  146.4 20.8 %expert_forward.1 = (bf16[2,1024,2048]{2,1,0:T(8,128)(2,1)}, bf16[1024,2048]{1,0:T(8,128)(2,1)}, bf16[1024,768]{1,0:T(8,128)(2,1)}, f32[1,1024]{1,0:T(1,128)}, bf16[1024,768]{1,0:T(8,128)(2,1)}) custom-call(bf16[1024,896]{1,0:T(8,128)(2,1)} %bitcast.138, bf16[1024,768]{1,0:T(8,128)(2,1)} %bitcast.144, bf16[8,2304,256]{2,1,0:T(8,128)(2,1)} %bitcast.119, ...), custom_call_target="tpu_custom_call" | custom-call | flops 201326592 | bytes 344064 | tf_op jit(solution)/shard_map/expert_forward/pallas_call | solution.py:567
  167.2 7.2 %outer_weights.1 = bf16[8,256,768]{2,1,0:T(8,128)(2,1)} custom-call(bf16[1024,2048]{1,0:T(8,128)(2,1)} %get-tuple-element.166.refs_0_.refs_1_.refs_2_.refs_3_, bf16[1024,2048]{1,0:T(8,128)(2,1)} %get-tuple-element.166.refs_0_.refs_1_.refs_2_.refs_3_, bf16[1024,2048]{1,0:T(8,128)(2,1)} %get-tuple-element.166.refs_0_.refs_1_.refs_2_.refs_3_, ...), custom_call_target="tpu_custom_call" | custom-call | flops 50331648 | bytes 114688 | tf_op jit(solution)/shard_map/outer_weights/pallas_call | solution.py:613
  174.4 3.3 all-to-all-start.2
  177.7 11.2 %expert_backward.1 = bf16[1024,768]{1,0:T(8,128)(2,1)} custom-call(bf16[2,1024,2048]{2,1,0:T(8,128)(2,1)} %get-tuple-element.145.joined_ref, bf16[8,2304,256]{2,1,0:T(8,128)(2,1)} %bitcast.127), custom_call_target="tpu_custom_call" | custom-call | flops 100663296 | bytes 229376 | tf_op jit(solution)/shard_map/expert_backward/pallas_call | solution.py:678
  188.9 3.6 all-to-all-start.3
  192.7 11.5 %inner_weights.1 = bf16[8,2,96,2048]{3,2,1,0:T(8,128)(2,1)} custom-call(bf16[1024,896]{1,0:T(8,128)(2,1)} %bitcast.139, bf16[2,1024,2048]{2,1,0:T(8,128)(2,1)} %get-tuple-element.145.joined_ref), custom_call_target="tpu_custom_call" | custom-call | flops 100663296 | bytes 229376 | tf_op jit(solution)/shard_map/inner_weights/pallas_call | solution.py:647
  204.2 8.3 %all-to-all-done.3 = bf16[4,256,768]{2,1,0:T(8,128)(2,1)S(1)} async-done(((bf16[4,256,768]{2,1,0:T(8,128)(2,1)}), bf16[4,256,768]{2,1,0:T(8,128)(2,1)S(1)}, u32[]{:S(2)}, u32[]{:S(2)}) %all-to-all-start.3) | async-done | bytes 1572896 | tf_op jit(solution)/shard_map/all_to_all | solution.py:989
  213.7 14.4 %middle_backward.1 = (f32[1024,768]{1,0:T(8,128)}, bf16[1024,768]{1,0:T(8,128)(2,1)}, f32[8,8]{1,0:T(8,128)}, bf16[16,24,896]{2,1,0:T(8,128)(2,1)}, bf16[16,24,896]{2,1,0:T(8,128)(2,1)}) custom-call(s32[1]{0:T(128)} %bitcast.37.core_ref, bf16[1024,768]{1,0:T(8,128)(2,1)} %bitcast.142, f32[1,1024]{1,0:T(1,128)} %bitcast.167, s32[1024,2]{1,0:T(8,128)} %copy-done.4, ...), custom_call_target="tpu_custom_call" | custom-call | flops 62914560 | bytes 221184 | tf_op jit(solution)/shard_map/middle_backward/pallas_call | solution.py:883
  228.2 2.3 collective-permute-done.10
  232.3 34.4 %attend_backward.1 = (bf16[3,1024,768]{2,1,0:T(8,128)(2,1)}, bf16[16,24,2304]{2,1,0:T(8,128)(2,1)}, bf16[16,24,2304]{2,1,0:T(8,128)(2,1)}) custom-call(s32[1]{0:T(128)} %bitcast.37.core_ref, bf16[3,1024,768]{2,1,0:T(8,128)(2,1)} %get-tuple-element.137.query_ref.key_ref.value_ref, bf16[3,1024,768]{2,1,0:T(8,128)(2,1)} %get-tuple-element.137.query_ref.key_ref.value_ref, ...), custom_call_target="tpu_custom_call" | custom-call | flops 251658240 | bytes 172032 | tf_op jit(solution)/shard_map/attend_backward/pallas_call | solution.py:250
  267.5 3.9 %collective-permute-done.12 = bf16[16,24,2304]{2,1,0:T(8,128)(2,1)S(1)} collective-permute-done((bf16[16,24,2304]{2,1,0:T(8,128)(2,1)}, bf16[16,24,2304]{2,1,0:T(8,128)(2,1)S(1)}, u32[]{:S(2)}, u32[]{:S(2)}) %collective-permute-start.12) | collective-permute-done | bytes 1769504 | tf_op jit(solution)/shard_map/ppermute | solution.py:1051
  276.0 7.9 %all-to-all-start.4 = ((bf16[8,24,896]{2,1,0:T(8,128)(2,1)}), bf16[8,24,896]{2,1,0:T(8,128)(2,1)S(1)}, u32[]{:S(2)}, u32[]{:S(2)}) async-start(bf16[8,24,896]{2,1,0:T(8,128)(2,1)} %fusion.5), calls=%async_computation.4 | async-start | bytes 688128 | tf_op jit(solution)/shard_map/all_to_all | solution.py:989
  283.9 12.4 %collective-permute-done.13 = bf16[8,24,2304]{2,1,0:T(8,128)(2,1)} collective-permute-done((bf16[8,24,2304]{2,1,0:T(8,128)(2,1)}, bf16[8,24,2304]{2,1,0:T(8,128)(2,1)}, u32[]{:S(2)}, u32[]{:S(2)}) %collective-permute-start.13) | collective-permute-done | bytes 884768 | tf_op jit(solution)/shard_map/ppermute | solution.py:1056
  296.3 2.3 fusion.4
  298.6 7.9 %all-to-all-start.5 = ((bf16[8,24,2304]{2,1,0:T(8,128)(2,1)}), bf16[8,24,2304]{2,1,0:T(8,128)(2,1)S(1)}, u32[]{:S(2)}, u32[]{:S(2)}) async-start(bf16[8,24,2304]{2,1,0:T(8,128)(2,1)} %fusion.4), calls=%async_computation.5 | async-start | bytes 1769472 | tf_op jit(solution)/shard_map/all_to_all | solution.py:989
  306.5 2.3 dynamic-slice_bitcast_fusion.1
  312.0 9.5 %input_backward.1 = (f32[1024,768]{1,0:T(8,128)}, f32[1,768]{1,0:T(1,128)}) custom-call(bf16[3,1024,768]{2,1,0:T(8,128)(2,1)} %get-tuple-element.160.packed_ref, bf16[768,3200]{1,0:T(8,128)(2,1)} %bitcast.136, bf16[1024,768]{1,0:T(8,128)(2,1)} %hidden_ref.5, f32[1024,768]{1,0:T(8,128)} %get-tuple-element.161.grad_middle_ref, ...), custom_call_target="tpu_custom_call" | custom-call | flops 56623104 | bytes 196608 | tf_op jit(solution)/shard_map/input_backward/pallas_call | solution.py:957
  321.5 6.9 %all-to-all-done.5.in_ref = bf16[8,24,2304]{2,1,0:T(8,128)(2,1)S(1)} async-done(((bf16[8,24,2304]{2,1,0:T(8,128)(2,1)}), bf16[8,24,2304]{2,1,0:T(8,128)(2,1)S(1)}, u32[]{:S(2)}, u32[]{:S(2)}) %all-to-all-start.5) | async-done | bytes 884768 | tf_op jit(solution)/shard_map/all_to_all | solution.py:989
  329.4 3.0 own_sums.1
  332.4 3.6 all-to-all-start.6
  336.1 7.9 %mix_branches.1 = bf16[1024,768]{1,0:T(8,128)(2,1)} custom-call(s32[1024,2]{1,0:T(8,128)} %get-tuple-element.215.targets_ref, f32[1024,128]{1,0:T(8,128)} %get-tuple-element.134.table_ref, f32[1024,768]{1,0:T(8,128)} %get-tuple-element.135.middle_ref, bf16[1024,768]{1,0:T(8,128)(2,1)} %get-tuple-element.136.normed_ref, bf16[768,3200]{1,0:T(8,128)(2,1)} %bitcast.137, ...), custom_call_target="tpu_custom_call" | custom-call | flops 50331648 | bytes 147456 | tf_op jit(solution)/shard_map/mix_branches/pallas_call | solution.py:731
  344.9 10.9 %update.1 = (f32[1,1]{1,0:T(1,128)}, f32[24,2304]{1,0:T(8,128)}, f32[24,2304]{1,0:T(8,128)}, f32[24,2304]{1,0:T(8,128)}, bf16[24,2304]{1,0:T(8,128)(2,1)}, /*ind...) custom-call(s32[1]{0:T(128)} %bitcast.58.refs_0_, ...), custom_call_target="tpu_custom_call" | custom-call | flops 983040 | bytes 737280 | tf_op jit(solution)/shard_map/update/pallas_call | solution.py:1221
  (119 shorter events, 37.6 us)
Async XLA Ops:
  7.2 139.1 %all-gather.3.cloned.1.call-start = ((), (), s32[]{:S(2)}) async-start(), calls=%async_computation.11 | async-start | bytes 10616832 | tf_op jit(solution)/shard_map/all_gather | solution.py:1083
  13.3 8.5 %copy-start.8 = (s32[1024,2]{0,1:T(2,128)S(1)}, s32[1024,2]{0,1:T(2,128)}, u32[]{:S(2)}) copy-start(s32[1024,2]{0,1:T(2,128)} %param.32) | copy-start | bytes 24580
  13.4 8.5 %copy-start.13 = (s32[1,1024]{1,0:T(1,128)S(1)}, s32[1,1024]{1,0:T(1,128)}, u32[]{:S(2)}) copy-start(s32[1,1024]{1,0:T(1,128)} %param.33) | copy-start | bytes 12292
  14.8 16.3 %collective-permute-start = (bf16[24,3200]{1,0:T(8,128)(2,1)S(1)}, bf16[24,3200]{1,0:T(8,128)(2,1)S(1)}, u32[]{:S(2)}, u32[]{:S(2)}) collective-permute-start(bf16[24,3200]{1,0:T(8,128)(2,1)S(1)} %concatenate.7), channel_id=1, source_target_pairs={{0,8},{4,12},{8,16},{12,20},{16,24},{20,28},{24,0},{28,4},{1,9},{5... | collective-permute-start | bytes 460808 | tf_op jit(solution)/shard_map/ppermute | solution.py:1016
  17.9 13.2 %collective-permute-start.1 = (bf16[24,3200]{1,0:T(8,128)(2,1)S(1)}, bf16[24,3200]{1,0:T(8,128)(2,1)S(1)}, u32[]{:S(2)}, u32[]{:S(2)}) collective-permute-start(bf16[24,3200]{1,0:T(8,128)(2,1)S(1)} %concatenate.7), channel_id=1, source_target_pairs={{0,16},{4,20},{8,24},{12,28},{16,0},{20,4},{24,8},{28,12},{1,17},{... | collective-permute-start | bytes 460808 | tf_op jit(solution)/shard_map/ppermute | solution.py:1016
  20.5 10.7 %collective-permute-start.2 = (bf16[24,3200]{1,0:T(8,128)(2,1)S(1)}, bf16[24,3200]{1,0:T(8,128)(2,1)S(1)}, u32[]{:S(2)}, u32[]{:S(2)}) collective-permute-start(bf16[24,3200]{1,0:T(8,128)(2,1)S(1)} %concatenate.7), channel_id=1, source_target_pairs={{0,24},{4,28},{8,0},{12,4},{16,8},{20,12},{24,16},{28,20},{1,25},{... | collective-permute-start | bytes 460808 | tf_op jit(solution)/shard_map/ppermute | solution.py:1016
  31.3 24.9 %collective-permute-start.3 = (bf16[4,24,3200]{2,1,0:T(8,128)(2,1)S(1)}, bf16[4,24,3200]{2,1,0:T(8,128)(2,1)S(1)}, u32[]{:S(2)}, u32[]{:S(2)}) collective-permute-start(bf16[4,24,3200]{2,1,0:T(8,128)(2,1)S(1)} %bitcast_dynamic-update-slice_fusion.8), channel_id=1, source_target_pairs={{0,1},{1,0},{2,3},{3,2},{4,5},{5,4},{6,7},{7,6},{8,9},{9,8},{10,11... | collective-permute-start | bytes 1843208 | tf_op jit(solution)/shard_map/ppermute | solution.py:1032
  31.4 23.3 %collective-permute-start.4 = (bf16[4,24,3200]{2,1,0:T(8,128)(2,1)S(1)}, bf16[4,24,3200]{2,1,0:T(8,128)(2,1)S(1)}, u32[]{:S(2)}, u32[]{:S(2)}) collective-permute-start(bf16[4,24,3200]{2,1,0:T(8,128)(2,1)S(1)} %bitcast_dynamic-update-slice_fusion.8), channel_id=1, source_target_pairs={{0,4},{4,0},{8,12},{12,8},{16,20},{20,16},{24,28},{28,24},{1,5},{5... | collective-permute-start | bytes 1843208 | tf_op jit(solution)/shard_map/ppermute | solution.py:1025
  33.0 23.0 %collective-permute-start.6 = (bf16[4,24,3200]{2,1,0:T(8,128)(2,1)S(1)}, bf16[4,24,3200]{2,1,0:T(8,128)(2,1)S(1)}, u32[]{:S(2)}, u32[]{:S(2)}) collective-permute-start(bf16[4,24,3200]{2,1,0:T(8,128)(2,1)S(1)} %bitcast_dynamic-update-slice_fusion.8), channel_id=1, source_target_pairs={{0,2},{1,3},{2,0},{3,1},{4,6},{5,7},{6,4},{7,5},{8,10},{9,11},{10,... | collective-permute-start | bytes 1843208 | tf_op jit(solution)/shard_map/ppermute | solution.py:1031
  54.7 16.3 %collective-permute-start.5 = (bf16[4,24,3200]{2,1,0:T(8,128)(2,1)S(1)}, bf16[4,24,3200]{2,1,0:T(8,128)(2,1)S(1)}, u32[]{:S(2)}, u32[]{:S(2)}) collective-permute-start(bf16[4,24,3200]{2,1,0:T(8,128)(2,1)S(1)} %collective-permute-done.4), channel_id=1, source_target_pairs={{0,1},{1,0},{2,3},{3,2},{4,5},{5,4},{6,7},{7,6},{8,9},{9,8},{10,11... | collective-permute-start | bytes 1843208 | tf_op jit(solution)/shard_map/ppermute | solution.py:1032
  54.7 16.3 %collective-permute-start.8 = (bf16[4,24,3200]{2,1,0:T(8,128)(2,1)S(1)}, bf16[4,24,3200]{2,1,0:T(8,128)(2,1)S(1)}, u32[]{:S(2)}, u32[]{:S(2)}) collective-permute-start(bf16[4,24,3200]{2,1,0:T(8,128)(2,1)S(1)} %collective-permute-done.4), channel_id=1, source_target_pairs={{0,2},{1,3},{2,0},{3,1},{4,6},{5,7},{6,4},{7,5},{8,10},{9,11},{10,... | collective-permute-start | bytes 1843208 | tf_op jit(solution)/shard_map/ppermute | solution.py:1031
  56.0 15.2 %collective-permute-start.7 = (bf16[4,24,3200]{2,1,0:T(8,128)(2,1)S(1)}, bf16[4,24,3200]{2,1,0:T(8,128)(2,1)S(1)}, u32[]{:S(2)}, u32[]{:S(2)}) collective-permute-start(bf16[4,24,3200]{2,1,0:T(8,128)(2,1)S(1)} %collective-permute-done.6), channel_id=1, source_target_pairs={{0,1},{1,0},{2,3},{3,2},{4,5},{5,4},{6,7},{7,6},{8,9},{9,8},{10,11... | collective-permute-start | bytes 1843208 | tf_op jit(solution)/shard_map/ppermute | solution.py:1032
  70.9 2.0 collective-permute-start.9
  73.1 7.7 %copy-start.9 = (f32[1024,8]{0,1:T(8,128)S(1)}, f32[1024,8]{0,1:T(8,128)}, u32[]{:S(2)}) copy-start(f32[1024,8]{0,1:T(8,128)} %param.31) | copy-start | bytes 98308
  75.6 43.3 %all-to-all-start.1 = ((bf16[4,256,768]{2,1,0:T(8,128)(2,1)}), bf16[4,256,768]{2,1,0:T(8,128)(2,1)S(1)}, u32[]{:S(2)}, u32[]{:S(2)}) async-start(bf16[4,256,768]{2,1,0:T(8,128)(2,1)} %bitcast.16), calls=%async_computation.1 | async-start | bytes 3145728 | tf_op jit(solution)/shard_map/all_to_all | solution.py:989
  79.1 242.4 %reduce-scatter.5.cloned.1.call-start = ((), (), s32[]{:S(2)}) async-start(), calls=%async_computation.10 | async-start | bytes 3538944 | tf_op jit(solution)/shard_map/reduce_scatter | solution.py:1090
  118.8 27.6 %copy-start.3 = (bf16[4,256,768]{2,1,0:T(8,128)(2,1)}, bf16[4,256,768]{2,1,0:T(8,128)(2,1)S(1)}, u32[]{:S(2)}) copy-start(bf16[4,256,768]{2,1,0:T(8,128)(2,1)S(1)} %all-to-all-done.1) | copy-start | bytes 4718596
  174.4 14.4 %all-to-all-start.2 = ((f32[4,1,256]{2,1,0:T(1,128)}), f32[4,1,256]{2,1,0:T(1,128)S(1)}, u32[]{:S(2)}, u32[]{:S(2)}) async-start(f32[4,1,256]{2,1,0:T(1,128)} %bitcast.42), calls=%async_computation.2 | async-start | bytes 8192 | tf_op jit(solution)/shard_map/all_to_all | solution.py:989
  188.9 15.3 %copy-start.12 = (f32[4,1,256]{2,1,0:T(1,128)}, f32[4,1,256]{2,1,0:T(1,128)S(1)}, u32[]{:S(2)}) copy-start(f32[4,1,256]{2,1,0:T(1,128)S(1)} %all-to-all-done.2) | copy-start | bytes 12292
  188.9 23.6 %all-to-all-start.3 = ((bf16[4,256,768]{2,1,0:T(8,128)(2,1)}), bf16[4,256,768]{2,1,0:T(8,128)(2,1)S(1)}, u32[]{:S(2)}, u32[]{:S(2)}) async-start(bf16[4,256,768]{2,1,0:T(8,128)(2,1)} %bitcast.143), calls=%async_computation.3 | async-start | bytes 3145728 | tf_op jit(solution)/shard_map/all_to_all | solution.py:989
  192.5 136.0 %reduce-scatter.3.cloned.1.call-start = ((), (), s32[]{:S(2)}) async-start(), calls=%async_computation.9 | async-start | bytes 7077888 | tf_op jit(solution)/shard_map/reduce_scatter | solution.py:1090
  228.1 2.4 collective-permute-start.10
  231.8 34.9 %collective-permute-start.11 = (bf16[8,24,896]{2,1,0:T(8,128)(2,1)S(1)}, bf16[8,24,896]{2,1,0:T(8,128)(2,1)S(1)}, u32[]{:S(2)}, u32[]{:S(2)}) collective-permute-start(bf16[8,24,896]{2,1,0:T(8,128)(2,1)S(1)} %dynamic-slice_bitcast_fusion.5), channel_id=1, source_target_pairs={{0,2},{1,3},{2,0},{3,1},{4,6},{5,7},{6,4},{7,5},{8,10},{9,11},{10,... | collective-permute-start | bytes 1032200 | tf_op jit(solution)/shard_map/ppermute | solution.py:1056
  267.5 3.9 %collective-permute-start.12 = (bf16[16,24,2304]{2,1,0:T(8,128)(2,1)}, bf16[16,24,2304]{2,1,0:T(8,128)(2,1)S(1)}, u32[]{:S(2)}, u32[]{:S(2)}) collective-permute-start(bf16[16,24,2304]{2,1,0:T(8,128)(2,1)} %get-tuple-element.156), channel_id=1, source_target_pairs={{0,1},{1,0},{2,3},{3,2},{4,5},{5,4},{6,7},{7,6},{8,9},{9,8},{10,11... | collective-permute-start | bytes 5308424 | tf_op jit(solution)/shard_map/ppermute | solution.py:1051
  274.4 22.0 %collective-permute-start.13 = (bf16[8,24,2304]{2,1,0:T(8,128)(2,1)}, bf16[8,24,2304]{2,1,0:T(8,128)(2,1)}, u32[]{:S(2)}, u32[]{:S(2)}) collective-permute-start(bf16[8,24,2304]{2,1,0:T(8,128)(2,1)} %dynamic-slice_bitcast_fusion), channel_id=1, source_target_pairs={{0,2},{1,3},{2,0},{3,1},{4,6},{5,7},{6,4},{7,5},{8,10},{9,11},{10,... | collective-permute-start | bytes 2654216 | tf_op jit(solution)/shard_map/ppermute | solution.py:1056
  276.0 22.6 %all-to-all-start.4 = ((bf16[8,24,896]{2,1,0:T(8,128)(2,1)}), bf16[8,24,896]{2,1,0:T(8,128)(2,1)S(1)}, u32[]{:S(2)}, u32[]{:S(2)}) async-start(bf16[8,24,896]{2,1,0:T(8,128)(2,1)} %fusion.5), calls=%async_computation.4 | async-start | bytes 688128 | tf_op jit(solution)/shard_map/all_to_all | solution.py:989
  298.6 10.2 %copy-start.6 = (bf16[8,24,896]{2,1,0:T(8,128)(2,1)}, bf16[8,24,896]{2,1,0:T(8,128)(2,1)S(1)}, u32[]{:S(2)}) copy-start(bf16[8,24,896]{2,1,0:T(8,128)(2,1)S(1)} %all-to-all-done.4.shares_ref) | copy-start | bytes 1032196
  298.6 29.8 %all-to-all-start.5 = ((bf16[8,24,2304]{2,1,0:T(8,128)(2,1)}), bf16[8,24,2304]{2,1,0:T(8,128)(2,1)S(1)}, u32[]{:S(2)}, u32[]{:S(2)}) async-start(bf16[8,24,2304]{2,1,0:T(8,128)(2,1)} %fusion.4), calls=%async_computation.5 | async-start | bytes 1769472 | tf_op jit(solution)/shard_map/all_to_all | solution.py:989
  308.8 27.2 %collective-permute-start.14 = (bf16[256,768]{1,0:T(8,128)(2,1)}, bf16[256,768]{1,0:T(8,128)(2,1)}, u32[]{:S(2)}, u32[]{:S(2)}) collective-permute-start(bf16[256,768]{1,0:T(8,128)(2,1)} %get-tuple-element.219), channel_id=1, source_target_pairs={{0,1},{1,2},{2,3},{3,0},{4,5},{5,6},{6,7},{7,4},{8,9},{9,10},{10,1... | collective-permute-start | bytes 1179656 | tf_op jit(solution)/shard_map/ppermute | solution.py:998
  308.8 27.2 %collective-permute-start.15 = (bf16[256,768]{1,0:T(8,128)(2,1)S(1)}, bf16[256,768]{1,0:T(8,128)(2,1)}, u32[]{:S(2)}, u32[]{:S(2)}) collective-permute-start(bf16[256,768]{1,0:T(8,128)(2,1)S(1)} %get-tuple-element.218), channel_id=1, source_target_pairs={{0,2},{1,3},{2,0},{3,1},{4,6},{5,7},{6,4},{7,5},{8,10},{9,11},{10,... | collective-permute-start | bytes 1179656 | tf_op jit(solution)/shard_map/ppermute | solution.py:998
  310.6 25.4 %collective-permute-start.16 = (bf16[256,768]{1,0:T(8,128)(2,1)S(1)}, bf16[256,768]{1,0:T(8,128)(2,1)}, u32[]{:S(2)}, u32[]{:S(2)}) collective-permute-start(bf16[256,768]{1,0:T(8,128)(2,1)S(1)} %get-tuple-element.217), channel_id=1, source_target_pairs={{0,3},{1,0},{2,1},{3,2},{4,7},{5,4},{6,5},{7,6},{8,11},{9,8},{10,9... | collective-permute-start | bytes 1179656 | tf_op jit(solution)/shard_map/ppermute | solution.py:998
  332.4 11.8 %all-to-all-start.6 = ((f32[32,1,1024]{2,1,0:T(1,128)}), f32[32,1,1024]{2,1,0:T(1,128)S(1)}, u32[]{:S(2)}, u32[]{:S(2)}) async-start(f32[32,1,1024]{2,1,0:T(1,128)} %get-tuple-element.170), calls=%async_computation.8 | async-start | bytes 262144 | tf_op jit(solution)/shard_map/all_to_all | solution.py:989
  (8 other events, 30.8 us)
Sparse Core Ops, SparseCore 0:
  31.3 105.3 all-gather.2
  174.6 41.3 reduce-scatter.4
  218.3 68.1 reduce-scatter.2
